TPU v7x, 32 devices: a whole 2x2x4 slice. The times are simulated.
32 devices in a mesh: dp: 8 (over z, x), noise: 4 (over y, core).
Axes of the slice: x: 2, y: 2, z: 4, core: 2. Of those that a mesh axis runs over, the one named last changes fastest.
Arguments:
- clean_tokens: bfloat16 [32, 64, 1152], P(('dp', 'noise')), may hold values from -6 to 6
- noise_tokens: bfloat16 [4, 32, 64, 1152], P('noise', 'dp'), may hold values from -6 to 6
- time_index: int32 [4, 32], P('noise', 'dp'), may hold values from 0 to 999
- class_label: int32 [32], P(('dp', 'noise')), may hold values from 0 to 999
- velocity_cotangent: bfloat16 [4, 32, 64, 1152], P('noise', 'dp'), may hold values from -6 to 6
- encoder_modulate: bfloat16 [1152, 6912], P('dp', 'noise'), may hold values from -0.1875 to 0.1875
- encoder_attend: bfloat16 [1152, 3456], P('dp', 'noise'), may hold values from -0.1875 to 0.1875
- encoder_merge: bfloat16 [1152, 1152], P('dp', 'noise'), may hold values from -0.375 to 0.375
- encoder_gate: bfloat16 [1152, 3072], P('dp', 'noise'), may hold values from -0.1875 to 0.1875
- encoder_lift: bfloat16 [1152, 3072], P('dp', 'noise'), may hold values from -0.1875 to 0.1875
- encoder_lower: bfloat16 [3072, 1152], P('dp', 'noise'), may hold values from -0.109375 to 0.109375
- class_table: bfloat16 [1152, 1000], P('dp', 'noise'), may hold values from -6 to 6
- encoder_gains: float32 [2, 72], replicated, may hold values from 0.25 to 1.75
- decoder_modulate: bfloat16 [1152, 6912], P('dp', 'noise'), may hold values from -0.1875 to 0.1875
- decoder_attend: bfloat16 [1152, 3456], P('dp', 'noise'), may hold values from -0.1875 to 0.1875
- decoder_merge: bfloat16 [1152, 1152], P('dp', 'noise'), may hold values from -0.375 to 0.375
- decoder_gate: bfloat16 [1152, 3072], P('dp', 'noise'), may hold values from -0.1875 to 0.1875
- decoder_lift: bfloat16 [1152, 3072], P('dp', 'noise'), may hold values from -0.1875 to 0.1875
- decoder_lower: bfloat16 [3072, 1152], P('dp', 'noise'), may hold values from -0.109375 to 0.109375
- time_weight: bfloat16 [1152, 1152], P('dp', 'noise'), may hold values from -0.1875 to 0.1875
- decoder_gains: float32 [2, 72], replicated, may hold values from 0.25 to 1.75
Outputs:
- velocity: bfloat16 [4, 32, 64, 1152], P('noise', 'dp')
- latent_tokens: bfloat16 [32, 64, 1152], P(('dp', 'noise'))
- clean_grad: float32 [32, 64, 1152], P(('dp', 'noise'))
- grad_encoder_modulate: float32 [1152, 6912], P('dp', 'noise')
- grad_encoder_attend: float32 [1152, 3456], P('dp', 'noise')
- grad_encoder_merge: float32 [1152, 1152], P('dp', 'noise')
- grad_encoder_gate: float32 [1152, 3072], P('dp', 'noise')
- grad_encoder_lift: float32 [1152, 3072], P('dp', 'noise')
- grad_encoder_lower: float32 [3072, 1152], P('dp', 'noise')
- grad_class_table: float32 [1152, 1000], P('dp', 'noise')
- grad_encoder_gains: float32 [2, 72], replicated
- grad_decoder_modulate: float32 [1152, 6912], P('dp', 'noise')
- grad_decoder_attend: float32 [1152, 3456], P('dp', 'noise')
- grad_decoder_merge: float32 [1152, 1152], P('dp', 'noise')
- grad_decoder_gate: float32 [1152, 3072], P('dp', 'noise')
- grad_decoder_lift: float32 [1152, 3072], P('dp', 'noise')
- grad_decoder_lower: float32 [3072, 1152], P('dp', 'noise')
- grad_time_weight: float32 [1152, 1152], P('dp', 'noise')
- grad_decoder_gains: float32 [2, 72], replicated
All inputs are finite; a program needn't handle non-finite values.
Results may differ from a plain program's by a relative error of at most 0.035.
Values may be sent and summed in bfloat16 or wider, within the bound.
No kernel may reach another device: no remote copies, remote signals or barrier semaphores. Data moves between devices by JAX's collectives and lax.ppermute only.
A program may use at most 512 MiB of HBM per device.

v0:
```python
import math

import jax
import jax.numpy as jnp
from jax import lax
from jax.sharding import PartitionSpec as P

HEADS = 16
HEAD = 72
NT = 1000
GRID = 8


EPS = 1e-06


def layer_norm(value):
    center = value - jnp.mean(value, -1, keepdims=True)
    return center * lax.rsqrt(jnp.mean(center * center, -1, keepdims=True) + EPS)


def rms_norm(value, scale_gain):
    return value * lax.rsqrt(jnp.mean(value * value, -1, keepdims=True) + EPS) * scale_gain


def angle_tables(length):
    places = jnp.arange(length)
    quarter = HEAD // 4
    freqs = jnp.exp(-math.log(10000.0) * jnp.arange(quarter).astype(jnp.float32) / quarter)
    row_angle = (places // GRID).astype(jnp.float32)[:, None] * freqs[None, :]
    col_angle = (places % GRID).astype(jnp.float32)[:, None] * freqs[None, :]
    return (row_angle, col_angle)


def turn_half(value, angle):
    quarter = angle.shape[-1]
    cosine = jnp.cos(angle)[:, None, :]
    sine = jnp.sin(angle)[:, None, :]
    first = value[..., :quarter]
    second = value[..., quarter:]
    return jnp.concatenate([first * cosine - second * sine, second * cosine + first * sine], -1)


def rotate(value):
    row_angle, col_angle = angle_tables(value.shape[1])
    half = value.shape[-1] // 2
    return jnp.concatenate(
        [turn_half(value[..., :half], row_angle), turn_half(value[..., half:], col_angle)], -1
    )


def head_norms(project, gains):
    count, length, triple = project.shape
    width = triple // 3
    shape = (count, length, HEADS, width // HEADS)
    queries = rotate(rms_norm(project[..., :width].reshape(shape), gains[0]))
    keys_head = rotate(rms_norm(project[..., width : 2 * width].reshape(shape), gains[1]))
    values = project[..., 2 * width :].reshape(shape)
    return (queries, keys_head, values)


def sinusoid(times, width):
    half = width // 2
    freqs = jnp.exp(-math.log(10000.0) * jnp.arange(half).astype(jnp.float32) / half)
    angle = (times * 1000.0)[..., None] * freqs
    return jnp.concatenate([jnp.cos(angle), jnp.sin(angle)], -1)


def pre_mix(hidden, modulate):
    width = hidden.shape[-1]
    return layer_norm(hidden) * (1.0 + modulate[..., width : 2 * width]) + modulate[..., :width]


def mid_mix(hidden, merged, modulate):
    width = hidden.shape[-1]
    middle = hidden + modulate[..., 2 * width : 3 * width] * merged
    normed = (
        layer_norm(middle) * (1.0 + modulate[..., 4 * width : 5 * width])
        + modulate[..., 3 * width : 4 * width]
    )
    return (middle, normed)


def out_mix(middle, lowered, modulate):
    width = middle.shape[-1]
    return middle + modulate[..., 5 * width : 6 * width] * lowered


def activate(gate_act, lift_act):
    return jax.nn.silu(gate_act) * lift_act


def flat_rows(value):
    return value.reshape(-1, value.shape[-1])


def weight_grad(left, right):
    return jnp.dot(flat_rows(left).T, flat_rows(right), preferred_element_type=jnp.float32)


def block_forward(hidden, cond, weights, gains):
    w_mod, w_att, w_merge, w_gate, w_lift, w_lower = weights
    count, length, width = hidden.shape
    head_scale = HEAD ** (-0.5)
    silu_cond = jax.nn.silu(cond).astype(jnp.bfloat16)
    modulate = jnp.einsum("nsd,df->nsf", silu_cond, w_mod, preferred_element_type=jnp.float32)
    normed_one = pre_mix(hidden, modulate).astype(jnp.bfloat16)
    project = jnp.einsum("nsd,df->nsf", normed_one, w_att, preferred_element_type=jnp.float32)
    queries, keys_head, values = head_norms(project, gains)
    query_low = queries.astype(jnp.bfloat16)
    key_low = keys_head.astype(jnp.bfloat16)
    value_low = values.astype(jnp.bfloat16)
    scores = (
        jnp.einsum("nqhe,nkhe->nhqk", query_low, key_low, preferred_element_type=jnp.float32)
        * head_scale
    )
    top_score = jnp.max(scores, -1, keepdims=True)
    log_total = top_score + jnp.log(jnp.sum(jnp.exp(scores - top_score), -1, keepdims=True))
    prob_low = jnp.exp(scores - log_total).astype(jnp.bfloat16)
    mixed_low = (
        jnp.einsum("nhqk,nkhe->nqhe", prob_low, value_low, preferred_element_type=jnp.float32)
        .astype(jnp.bfloat16)
        .reshape(count, length, width)
    )
    merged = jnp.einsum("nsd,df->nsf", mixed_low, w_merge, preferred_element_type=jnp.float32)
    middle, normed = mid_mix(hidden, merged, modulate)
    normed_two = normed.astype(jnp.bfloat16)
    gate_act = jnp.einsum("nsd,df->nsf", normed_two, w_gate, preferred_element_type=jnp.float32)
    lift_act = jnp.einsum("nsd,df->nsf", normed_two, w_lift, preferred_element_type=jnp.float32)
    hidden_low = activate(gate_act, lift_act).astype(jnp.bfloat16)
    lowered = jnp.einsum("nsf,fd->nsd", hidden_low, w_lower, preferred_element_type=jnp.float32)
    output = out_mix(middle, lowered, modulate)
    kept = (
        silu_cond,
        modulate,
        normed_one,
        project,
        query_low,
        key_low,
        value_low,
        log_total,
        mixed_low,
        merged,
        middle,
        normed_two,
        gate_act,
        lift_act,
        hidden_low,
        lowered,
    )
    return (output, kept)


def block_backward(hidden, cond, weights, gains, kept, grad_out):
    w_mod, w_att, w_merge, w_gate, w_lift, w_lower = weights
    (
        silu_cond,
        modulate,
        normed_one,
        project,
        query_low,
        key_low,
        value_low,
        log_total,
        mixed_low,
        merged,
        middle,
        normed_two,
        gate_act,
        lift_act,
        hidden_low,
        lowered,
    ) = kept
    count, length, width = hidden.shape
    head_scale = HEAD ** (-0.5)
    _, out_pull = jax.vjp(out_mix, middle, lowered, modulate)
    grad_middle, grad_lowered, grad_mod_a = out_pull(grad_out)
    lowered_low = grad_lowered.astype(jnp.bfloat16)
    grad_w_lower = weight_grad(hidden_low, lowered_low)
    grad_hidden_act = jnp.einsum(
        "nsd,fd->nsf", lowered_low, w_lower, preferred_element_type=jnp.float32
    )
    _, act_pull = jax.vjp(activate, gate_act, lift_act)
    grad_gate_act, grad_lift_act = act_pull(grad_hidden_act)
    gate_low = grad_gate_act.astype(jnp.bfloat16)
    lift_low = grad_lift_act.astype(jnp.bfloat16)
    grad_w_gate = weight_grad(normed_two, gate_low)
    grad_w_lift = weight_grad(normed_two, lift_low)
    grad_normed = jnp.einsum(
        "nsf,df->nsd", gate_low, w_gate, preferred_element_type=jnp.float32
    ) + jnp.einsum("nsf,df->nsd", lift_low, w_lift, preferred_element_type=jnp.float32)
    _, mid_pull = jax.vjp(mid_mix, hidden, merged, modulate)
    grad_hidden, grad_merged, grad_mod_b = mid_pull((grad_middle, grad_normed))
    merged_low = grad_merged.astype(jnp.bfloat16)
    grad_w_merge = weight_grad(mixed_low, merged_low)
    grad_mixed = jnp.einsum("nsf,df->nsd", merged_low, w_merge, preferred_element_type=jnp.float32)
    mixed_grad_low = grad_mixed.astype(jnp.bfloat16).reshape(count, length, HEADS, width // HEADS)
    scores = (
        jnp.einsum("nqhe,nkhe->nhqk", query_low, key_low, preferred_element_type=jnp.float32)
        * head_scale
    )
    attn_prob = jnp.exp(scores - log_total)
    prob_low = attn_prob.astype(jnp.bfloat16)
    grad_values = jnp.einsum(
        "nhqk,nqhe->nkhe", prob_low, mixed_grad_low, preferred_element_type=jnp.float32
    )
    grad_prob = jnp.einsum(
        "nqhe,nkhe->nhqk", mixed_grad_low, value_low, preferred_element_type=jnp.float32
    )
    grad_scores = (
        attn_prob * (grad_prob - jnp.sum(grad_prob * attn_prob, -1, keepdims=True))
    ).astype(jnp.bfloat16)
    grad_queries = (
        jnp.einsum("nhqk,nkhe->nqhe", grad_scores, key_low, preferred_element_type=jnp.float32)
        * head_scale
    )
    grad_keys = (
        jnp.einsum("nhqk,nqhe->nkhe", grad_scores, query_low, preferred_element_type=jnp.float32)
        * head_scale
    )
    _, head_pull = jax.vjp(head_norms, project, gains)
    grad_project, grad_gains = head_pull((grad_queries, grad_keys, grad_values))
    project_low = grad_project.astype(jnp.bfloat16)
    grad_w_att = weight_grad(normed_one, project_low)
    grad_normed_one = jnp.einsum(
        "nsf,df->nsd", project_low, w_att, preferred_element_type=jnp.float32
    )
    _, pre_pull = jax.vjp(pre_mix, hidden, modulate)
    grad_hidden_b, grad_mod_c = pre_pull(grad_normed_one)
    mod_low = (grad_mod_a + grad_mod_b + grad_mod_c).astype(jnp.bfloat16)
    grad_w_mod = weight_grad(silu_cond, mod_low)
    grad_silu = jnp.einsum("nsf,df->nsd", mod_low, w_mod, preferred_element_type=jnp.float32)
    _, silu_pull = jax.vjp(jax.nn.silu, cond)
    grad_cond = silu_pull(grad_silu)[0]
    weight_grads = (grad_w_mod, grad_w_att, grad_w_merge, grad_w_gate, grad_w_lift, grad_w_lower)
    return (grad_hidden + grad_hidden_b, grad_cond, weight_grads, grad_gains)


def fetch_block(first, second, third, fourth, fifth, sixth, seventh):
    part = (
        lax.all_gather(first, "noise", axis=1, tiled=True),
        lax.all_gather(second, "noise", axis=1, tiled=True),
        lax.all_gather(third, "noise", axis=1, tiled=True),
        lax.all_gather(fourth, "noise", axis=1, tiled=True),
        lax.all_gather(fifth, "noise", axis=1, tiled=True),
        lax.all_gather(sixth, "noise", axis=1, tiled=True),
        lax.all_gather(seventh, "noise", axis=1, tiled=True),
    )
    return (
        lax.all_gather(part[0], "dp", axis=0, tiled=True),
        lax.all_gather(part[1], "dp", axis=0, tiled=True),
        lax.all_gather(part[2], "dp", axis=0, tiled=True),
        lax.all_gather(part[3], "dp", axis=0, tiled=True),
        lax.all_gather(part[4], "dp", axis=0, tiled=True),
        lax.all_gather(part[5], "dp", axis=0, tiled=True),
        lax.all_gather(part[6], "dp", axis=0, tiled=True),
    )


def fetch_again(first, second, third, fourth, fifth, sixth, seventh):
    part = (
        lax.all_gather(first, "noise", axis=1, tiled=True),
        lax.all_gather(second, "noise", axis=1, tiled=True),
        lax.all_gather(third, "noise", axis=1, tiled=True),
        lax.all_gather(fourth, "noise", axis=1, tiled=True),
        lax.all_gather(fifth, "noise", axis=1, tiled=True),
        lax.all_gather(sixth, "noise", axis=1, tiled=True),
        lax.all_gather(seventh, "noise", axis=1, tiled=True),
    )
    return (
        lax.all_gather(part[0], "dp", axis=0, tiled=True),
        lax.all_gather(part[1], "dp", axis=0, tiled=True),
        lax.all_gather(part[2], "dp", axis=0, tiled=True),
        lax.all_gather(part[3], "dp", axis=0, tiled=True),
        lax.all_gather(part[4], "dp", axis=0, tiled=True),
        lax.all_gather(part[5], "dp", axis=0, tiled=True),
        lax.all_gather(part[6], "dp", axis=0, tiled=True),
    )


def reduce_block(first, second, third, fourth, fifth, sixth, seventh):
    part = (
        lax.psum_scatter(first, "dp", scatter_dimension=0, tiled=True),
        lax.psum_scatter(second, "dp", scatter_dimension=0, tiled=True),
        lax.psum_scatter(third, "dp", scatter_dimension=0, tiled=True),
        lax.psum_scatter(fourth, "dp", scatter_dimension=0, tiled=True),
        lax.psum_scatter(fifth, "dp", scatter_dimension=0, tiled=True),
        lax.psum_scatter(sixth, "dp", scatter_dimension=0, tiled=True),
        lax.psum_scatter(seventh, "dp", scatter_dimension=0, tiled=True),
    )
    return (
        lax.psum_scatter(
            part[0].astype(jnp.bfloat16), "noise", scatter_dimension=1, tiled=True
        ).astype(jnp.float32),
        lax.psum_scatter(
            part[1].astype(jnp.bfloat16), "noise", scatter_dimension=1, tiled=True
        ).astype(jnp.float32),
        lax.psum_scatter(
            part[2].astype(jnp.bfloat16), "noise", scatter_dimension=1, tiled=True
        ).astype(jnp.float32),
        lax.psum_scatter(
            part[3].astype(jnp.bfloat16), "noise", scatter_dimension=1, tiled=True
        ).astype(jnp.float32),
        lax.psum_scatter(
            part[4].astype(jnp.bfloat16), "noise", scatter_dimension=1, tiled=True
        ).astype(jnp.float32),
        lax.psum_scatter(
            part[5].astype(jnp.bfloat16), "noise", scatter_dimension=1, tiled=True
        ).astype(jnp.float32),
        lax.psum_scatter(
            part[6].astype(jnp.bfloat16), "noise", scatter_dimension=1, tiled=True
        ).astype(jnp.float32),
    )


def reduce_single(matrix):
    part = lax.psum_scatter(matrix, "dp", scatter_dimension=0, tiled=True)
    return lax.psum_scatter(
        part.astype(jnp.bfloat16), "noise", scatter_dimension=1, tiled=True
    ).astype(jnp.float32)


def class_lookup(class_label, table):
    onehot = (class_label[:, None] == jnp.arange(table.shape[1])[None, :]).astype(jnp.bfloat16)
    cond = jnp.einsum("nc,dc->nd", onehot, table, preferred_element_type=jnp.float32)
    return (onehot, cond[:, None, :])


def per_device(
    clean_tokens,
    noise_tokens,
    time_index,
    class_label,
    velocity_cotangent,
    encoder_modulate,
    encoder_attend,
    encoder_merge,
    encoder_gate,
    encoder_lift,
    encoder_lower,
    class_table,
    encoder_gains,
    decoder_modulate,
    decoder_attend,
    decoder_merge,
    decoder_gate,
    decoder_lift,
    decoder_lower,
    time_weight,
    decoder_gains,
):
    clean_own = clean_tokens.astype(jnp.float32)
    encoder_full = fetch_block(
        encoder_modulate,
        encoder_attend,
        encoder_merge,
        encoder_gate,
        encoder_lift,
        encoder_lower,
        class_table,
    )
    onehot, class_cond = class_lookup(class_label, encoder_full[6])
    latent, _ = block_forward(clean_own, class_cond, encoder_full[:6], encoder_gains)
    latent_low = latent.astype(jnp.bfloat16)
    group_latent, group_clean = (
        lax.all_gather(latent_low, "noise", axis=0, tiled=True),
        lax.all_gather(clean_tokens, "noise", axis=0, tiled=True),
    )
    decoder_full = fetch_block(
        decoder_modulate,
        decoder_attend,
        decoder_merge,
        decoder_gate,
        decoder_lift,
        decoder_lower,
        time_weight,
    )
    times = (time_index[0].astype(jnp.float32) + 0.5) / NT
    sines = sinusoid(times, group_latent.shape[-1]).astype(jnp.bfloat16)
    temb = jnp.dot(sines, decoder_full[6], preferred_element_type=jnp.float32)
    cond = group_latent.astype(jnp.float32) + temb[:, None, :]
    ratio = times[:, None, None]
    noisy = (1.0 - ratio) * group_clean.astype(jnp.float32) + ratio * noise_tokens[0].astype(
        jnp.float32
    )
    output, kept = block_forward(noisy, cond, decoder_full[:6], decoder_gains)
    velocity = output.astype(jnp.bfloat16)[None]
    grad_noisy, grad_cond, decoder_grads, decoder_gain_grad = block_backward(
        noisy,
        cond,
        decoder_full[:6],
        decoder_gains,
        kept,
        velocity_cotangent[0].astype(jnp.float32),
    )
    temb_low = jnp.sum(grad_cond, 1).astype(jnp.bfloat16)
    grad_time = jnp.dot(sines.T, temb_low, preferred_element_type=jnp.float32)
    decoder_list = (
        decoder_grads[0],
        decoder_grads[1],
        decoder_grads[2],
        decoder_grads[3],
        decoder_grads[4],
        decoder_grads[5],
        grad_time,
    )
    decoder_out = [reduce_single(matrix) for matrix in decoder_list]
    grad_latent, grad_clean_part = (
        lax.psum_scatter(
            grad_cond.astype(jnp.bfloat16), "noise", scatter_dimension=0, tiled=True
        ).astype(jnp.float32),
        lax.psum_scatter(
            ((1.0 - ratio) * grad_noisy).astype(jnp.bfloat16),
            "noise",
            scatter_dimension=0,
            tiled=True,
        ).astype(jnp.float32),
    )
    encoder_again = fetch_again(
        encoder_modulate,
        encoder_attend,
        encoder_merge,
        encoder_gate,
        encoder_lift,
        encoder_lower,
        class_table,
    )
    onehot_again, class_again = class_lookup(class_label, encoder_again[6])
    _, kept_enc = block_forward(clean_own, class_again, encoder_again[:6], encoder_gains)
    grad_clean_enc, grad_class, encoder_grads, encoder_gain_grad = block_backward(
        clean_own, class_again, encoder_again[:6], encoder_gains, kept_enc, grad_latent
    )
    grad_table = jnp.dot(
        grad_class[:, 0, :].T, onehot_again.astype(jnp.float32), precision=lax.Precision.HIGHEST
    )
    encoder_out = reduce_block(
        encoder_grads[0],
        encoder_grads[1],
        encoder_grads[2],
        encoder_grads[3],
        encoder_grads[4],
        encoder_grads[5],
        grad_table,
    )
    gain_total = lax.psum((encoder_gain_grad, decoder_gain_grad), ("dp", "noise"))
    clean_grad = grad_clean_enc + grad_clean_part
    return (
        velocity,
        latent_low,
        clean_grad,
        encoder_out[0],
        encoder_out[1],
        encoder_out[2],
        encoder_out[3],
        encoder_out[4],
        encoder_out[5],
        encoder_out[6],
        gain_total[0],
        decoder_out[0],
        decoder_out[1],
        decoder_out[2],
        decoder_out[3],
        decoder_out[4],
        decoder_out[5],
        decoder_out[6],
        gain_total[1],
    )


def solution(mesh):
    return jax.shard_map(
        per_device,
        mesh=mesh,
        in_specs=(
            P(("dp", "noise"), None, None),
            P("noise", "dp", None, None),
            P("noise", "dp"),
            P(("dp", "noise")),
            P("noise", "dp", None, None),
            P("dp", "noise"),
            P("dp", "noise"),
            P("dp", "noise"),
            P("dp", "noise"),
            P("dp", "noise"),
            P("dp", "noise"),
            P("dp", "noise"),
            P(),
            P("dp", "noise"),
            P("dp", "noise"),
            P("dp", "noise"),
            P("dp", "noise"),
            P("dp", "noise"),
            P("dp", "noise"),
            P("dp", "noise"),
            P(),
        ),
        out_specs=(
            P("noise", "dp", None, None),
            P(("dp", "noise"), None, None),
            P(("dp", "noise"), None, None),
            P("dp", "noise"),
            P("dp", "noise"),
            P("dp", "noise"),
            P("dp", "noise"),
            P("dp", "noise"),
            P("dp", "noise"),
            P("dp", "noise"),
            P(),
            P("dp", "noise"),
            P("dp", "noise"),
            P("dp", "noise"),
            P("dp", "noise"),
            P("dp", "noise"),
            P("dp", "noise"),
            P("dp", "noise"),
            P(),
        ),
        check_vma=False,
    )
```

profile of v0, /device:TPU:0, one launch (start us, length us, event | category | flops | bytes accessed | tf_op | source)
XLA Modules:
  0.0 5629.7 jit_solution(563265990291202003)
XLA Ops:
  177.8 215.6 %all-gather.27.cloned.1.call-done = bf16[1152,6912]{1,0:T(8,128)(2,1)} async-done(((bf16[144,6912]{1,0:T(8,128)(2,1)}), bf16[1152,6912]{1,0:T(8,128)(2,1)}) %all-gather.27.cloned.1.call-update) | async-done | bytes 15925264 | tf_op jit(solution)/shard_map/all_gather | solution.py:250
  401.3 112.6 %all-gather.29.cloned.1.call-done = bf16[1152,3456]{1,0:T(8,128)(2,1)} async-done(((bf16[144,3456]{1,0:T(8,128)(2,1)}), bf16[1152,3456]{1,0:T(8,128)(2,1)}) %all-gather.29.cloned.1.call-update) | async-done | bytes 7962640 | tf_op jit(solution)/shard_map/all_gather | solution.py:251
  526.5 43.3 all-gather.31.cloned.1.call-done
  573.4 106.0 %all-gather.33.cloned.1.call-done = bf16[1152,3072]{1,0:T(8,128)(2,1)} async-done(((bf16[144,3072]{1,0:T(8,128)(2,1)}), bf16[1152,3072]{1,0:T(8,128)(2,1)}) %all-gather.33.cloned.1.call-update) | async-done | bytes 7077904 | tf_op jit(solution)/shard_map/all_gather | solution.py:253
  683.9 104.8 %all-gather.35.cloned.1.call-done = bf16[1152,3072]{1,0:T(8,128)(2,1)} async-done(((bf16[144,3072]{1,0:T(8,128)(2,1)}), bf16[1152,3072]{1,0:T(8,128)(2,1)}) %all-gather.35.cloned.1.call-update) | async-done | bytes 7077904 | tf_op jit(solution)/shard_map/all_gather | solution.py:254
  794.1 104.2 %all-gather.37.cloned.1.call-done = bf16[3072,1152]{0,1:T(8,128)(2,1)} async-done(((bf16[384,1152]{0,1:T(8,128)(2,1)}), bf16[3072,1152]{0,1:T(8,128)(2,1)}) %all-gather.37.cloned.1.call-update) | async-done | bytes 7077904 | tf_op jit(solution)/shard_map/all_gather | solution.py:255
  911.8 204.1 %all-gather.41.cloned.1.call-done = bf16[1152,6912]{1,0:T(8,128)(2,1)} async-done(((bf16[144,6912]{1,0:T(8,128)(2,1)}), bf16[1152,6912]{1,0:T(8,128)(2,1)}) %all-gather.41.cloned.1.call-update) | async-done | bytes 15925264 | tf_op jit(solution)/shard_map/all_gather | solution.py:250
  1127.8 108.5 %all-gather.43.cloned.1.call-done = bf16[1152,3456]{1,0:T(8,128)(2,1)} async-done(((bf16[144,3456]{1,0:T(8,128)(2,1)}), bf16[1152,3456]{1,0:T(8,128)(2,1)}) %all-gather.43.cloned.1.call-update) | async-done | bytes 7962640 | tf_op jit(solution)/shard_map/all_gather | solution.py:251
  1301.0 100.8 %all-gather.49.cloned.1.call-done = bf16[1152,3072]{1,0:T(8,128)(2,1)} async-done(((bf16[144,3072]{1,0:T(8,128)(2,1)}), bf16[1152,3072]{1,0:T(8,128)(2,1)}) %all-gather.49.cloned.1.call-update) | async-done | bytes 7077904 | tf_op jit(solution)/shard_map/all_gather | solution.py:254
  1408.8 102.0 %all-gather.51.cloned.1.call-done = bf16[3072,1152]{1,0:T(8,128)(2,1)} async-done(((bf16[384,1152]{1,0:T(8,128)(2,1)}), bf16[3072,1152]{1,0:T(8,128)(2,1)}) %all-gather.51.cloned.1.call-update) | async-done | bytes 7077904 | tf_op jit(solution)/shard_map/all_gather | solution.py:255
  1518.3 101.6 %all-gather.47.cloned.1.call-done = bf16[1152,3072]{1,0:T(8,128)(2,1)} async-done(((bf16[144,3072]{1,0:T(8,128)(2,1)}), bf16[1152,3072]{1,0:T(8,128)(2,1)}) %all-gather.47.cloned.1.call-update) | async-done | bytes 7077904 | tf_op jit(solution)/shard_map/all_gather | solution.py:253
  1709.7 27.3 fusion.154
  1931.3 83.1 %reduce-scatter.75.cloned.1.call-done = f32[144,1152]{1,0:T(8,128)} async-done(((f32[1152,1152]{1,0:T(8,128)}), f32[144,1152]{1,0:T(8,128)}) %reduce-scatter.75.cloned.1.call-update) | async-done | bytes 663568 | tf_op jit(solution)/shard_map/reduce_scatter | solution.py:317
  2016.7 105.7 %reduce-scatter.87.cloned.1.call-done = f32[144,1152]{1,0:T(8,128)} async-done(((f32[1152,1152]{1,0:T(8,128)}), f32[144,1152]{1,0:T(8,128)}) %reduce-scatter.87.cloned.1.call-update) | async-done | bytes 663568 | tf_op jit(solution)/shard_map/reduce_scatter | solution.py:317
  2124.6 105.3 %reduce-scatter.57.cloned.1.call-done = f32[144,1152]{1,0:T(8,128)} async-done(((f32[1152,1152]{1,0:T(8,128)}), f32[144,1152]{1,0:T(8,128)}) %reduce-scatter.57.cloned.1.call-update) | async-done | bytes 663568 | tf_op jit(solution)/shard_map/reduce_scatter | solution.py:285
  2232.2 230.8 %reduce-scatter.85.cloned.1.call-done = f32[384,1152]{1,0:T(8,128)} async-done(((f32[3072,1152]{1,0:T(8,128)}), f32[384,1152]{1,0:T(8,128)}) %reduce-scatter.85.cloned.1.call-update) | async-done | bytes 1769488 | tf_op jit(solution)/shard_map/reduce_scatter | solution.py:317
  2466.0 229.3 %reduce-scatter.77.cloned.1.call-done = f32[144,3072]{1,0:T(8,128)} async-done(((f32[1152,3072]{1,0:T(8,128)}), f32[144,3072]{1,0:T(8,128)}) %reduce-scatter.77.cloned.1.call-update) | async-done | bytes 1769488 | tf_op jit(solution)/shard_map/reduce_scatter | solution.py:317
  2697.8 229.8 %reduce-scatter.81.cloned.1.call-done = f32[144,3072]{1,0:T(8,128)} async-done(((f32[1152,3072]{1,0:T(8,128)}), f32[144,3072]{1,0:T(8,128)}) %reduce-scatter.81.cloned.1.call-update) | async-done | bytes 1769488 | tf_op jit(solution)/shard_map/reduce_scatter | solution.py:317
  2930.2 229.7 %reduce-scatter.67.cloned.1.call-done = f32[384,1152]{1,0:T(8,128)} async-done(((f32[3072,1152]{1,0:T(8,128)}), f32[384,1152]{1,0:T(8,128)}) %reduce-scatter.67.cloned.1.call-update) | async-done | bytes 1769488 | tf_op jit(solution)/shard_map/reduce_scatter | solution.py:288
  3162.9 229.3 %reduce-scatter.63.cloned.1.call-done = f32[144,3072]{1,0:T(8,128)} async-done(((f32[1152,3072]{1,0:T(8,128)}), f32[144,3072]{1,0:T(8,128)}) %reduce-scatter.63.cloned.1.call-update) | async-done | bytes 1769488 | tf_op jit(solution)/shard_map/reduce_scatter | solution.py:287
  3394.9 229.6 %reduce-scatter.59.cloned.1.call-done = f32[144,3072]{1,0:T(8,128)} async-done(((f32[1152,3072]{1,0:T(8,128)}), f32[144,3072]{1,0:T(8,128)}) %reduce-scatter.59.cloned.1.call-update) | async-done | bytes 1769488 | tf_op jit(solution)/shard_map/reduce_scatter | solution.py:286
  3627.2 270.3 %reduce-scatter.73.cloned.1.call-done = f32[144,3456]{1,0:T(8,128)} async-done(((f32[1152,3456]{1,0:T(8,128)}), f32[144,3456]{1,0:T(8,128)}) %reduce-scatter.73.cloned.1.call-update) | async-done | bytes 1990672 | tf_op jit(solution)/shard_map/reduce_scatter | solution.py:317
  3900.9 269.3 %reduce-scatter.55.cloned.1.call-done = f32[144,3456]{1,0:T(8,128)} async-done(((f32[1152,3456]{1,0:T(8,128)}), f32[144,3456]{1,0:T(8,128)}) %reduce-scatter.55.cloned.1.call-update) | async-done | bytes 1990672 | tf_op jit(solution)/shard_map/reduce_scatter | solution.py:284
  4173.6 512.5 %reduce-scatter.71.cloned.1.call-done = f32[144,6912]{1,0:T(8,128)} async-done(((f32[1152,6912]{1,0:T(8,128)}), f32[144,6912]{1,0:T(8,128)}) %reduce-scatter.71.cloned.1.call-update) | async-done | bytes 3981328 | tf_op jit(solution)/shard_map/reduce_scatter | solution.py:317
  4691.4 510.5 %reduce-scatter.53.cloned.1.call-done = f32[144,6912]{1,0:T(8,128)} async-done(((f32[1152,6912]{1,0:T(8,128)}), f32[144,6912]{1,0:T(8,128)}) %reduce-scatter.53.cloned.1.call-update) | async-done | bytes 3981328 | tf_op jit(solution)/shard_map/reduce_scatter | solution.py:283
  5209.2 39.4 all-reduce.47
  5418.4 25.1 reduce-scatter.65.cloned.1.call-done
  5445.2 25.3 reduce-scatter.61.cloned.1.call-done
  5472.3 30.3 reduce-scatter.99.cloned.1.call-done
  5504.6 30.0 reduce-scatter.91.cloned.1.call-done
  5536.6 41.0 reduce-scatter.97.cloned.1.call-done
  5580.1 40.4 reduce-scatter.89.cloned.1.call-done
  (753 shorter events, 813.7 us)
Async XLA Ops:
  76.1 712.6 %all-gather.35.cloned.1.call-start = ((), (), s32[]{:S(2)}) async-start(), calls=%async_computation.34 | async-start | bytes 7962624 | tf_op jit(solution)/shard_map/all_gather | solution.py:254
  85.9 812.3 %all-gather.37.cloned.1.call-start = ((), (), s32[]{:S(2)}) async-start(), calls=%async_computation.35 | async-start | bytes 7962624 | tf_op jit(solution)/shard_map/all_gather | solution.py:255
  95.7 1020.2 %all-gather.41.cloned.1.call-start = ((), (), s32[]{:S(2)}) async-start(), calls=%async_computation.37 | async-start | bytes 17915904 | tf_op jit(solution)/shard_map/all_gather | solution.py:250
  101.3 1135.0 %all-gather.43.cloned.1.call-start = ((), (), s32[]{:S(2)}) async-start(), calls=%async_computation.38 | async-start | bytes 8957952 | tf_op jit(solution)/shard_map/all_gather | solution.py:251
  113.6 1178.7 %all-gather.45.cloned.1.call-start = ((), (), s32[]{:S(2)}) async-start(), calls=%async_computation.39 | async-start | bytes 2985984 | tf_op jit(solution)/shard_map/all_gather | solution.py:252
  121.9 1279.9 %all-gather.49.cloned.1.call-start = ((), (), s32[]{:S(2)}) async-start(), calls=%async_computation.41 | async-start | bytes 7962624 | tf_op jit(solution)/shard_map/all_gather | solution.py:254
  131.7 1379.1 %all-gather.51.cloned.1.call-start = ((), (), s32[]{:S(2)}) async-start(), calls=%async_computation.42 | async-start | bytes 7962624 | tf_op jit(solution)/shard_map/all_gather | solution.py:255
  142.7 1477.2 %all-gather.47.cloned.1.call-start = ((), (), s32[]{:S(2)}) async-start(), calls=%async_computation.40 | async-start | bytes 7962624 | tf_op jit(solution)/shard_map/all_gather | solution.py:253
  152.6 1604.9 %reduce-scatter.49.cloned.1.call-start = ((), (), s32[]{:S(2)}) async-start(), calls=%async_computation.43 | async-start | bytes 737280 | tf_op jit(solution)/shard_map/reduce_scatter | solution.py:409
  1836.2 859.0 %reduce-scatter.77.cloned.1.call-start = ((), (), s32[]{:S(2)}) async-start(), calls=%async_computation.57 | async-start | bytes 15925248 | tf_op jit(solution)/shard_map/reduce_scatter | solution.py:317
  1845.0 1082.6 %reduce-scatter.81.cloned.1.call-start = ((), (), s32[]{:S(2)}) async-start(), calls=%async_computation.59 | async-start | bytes 15925248 | tf_op jit(solution)/shard_map/reduce_scatter | solution.py:317
  1853.5 1306.4 %reduce-scatter.67.cloned.1.call-start = ((), (), s32[]{:S(2)}) async-start(), calls=%async_computation.52 | async-start | bytes 15925248 | tf_op jit(solution)/shard_map/reduce_scatter | solution.py:288
  1861.5 1530.7 %reduce-scatter.63.cloned.1.call-start = ((), (), s32[]{:S(2)}) async-start(), calls=%async_computation.50 | async-start | bytes 15925248 | tf_op jit(solution)/shard_map/reduce_scatter | solution.py:287
  1869.6 1755.0 %reduce-scatter.59.cloned.1.call-start = ((), (), s32[]{:S(2)}) async-start(), calls=%async_computation.48 | async-start | bytes 15925248 | tf_op jit(solution)/shard_map/reduce_scatter | solution.py:286
  1877.7 2019.7 %reduce-scatter.73.cloned.1.call-start = ((), (), s32[]{:S(2)}) async-start(), calls=%async_computation.55 | async-start | bytes 17915904 | tf_op jit(solution)/shard_map/reduce_scatter | solution.py:317
  1888.9 2281.3 %reduce-scatter.55.cloned.1.call-start = ((), (), s32[]{:S(2)}) async-start(), calls=%async_computation.46 | async-start | bytes 17915904 | tf_op jit(solution)/shard_map/reduce_scatter | solution.py:284
  1898.0 2788.1 %reduce-scatter.71.cloned.1.call-start = ((), (), s32[]{:S(2)}) async-start(), calls=%async_computation.54 | async-start | bytes 35831808 | tf_op jit(solution)/shard_map/reduce_scatter | solution.py:317
  1917.7 3284.2 %reduce-scatter.53.cloned.1.call-start = ((), (), s32[]{:S(2)}) async-start(), calls=%async_computation.45 | async-start | bytes 35831808 | tf_op jit(solution)/shard_map/reduce_scatter | solution.py:283
  1929.3 3319.3 %all-reduce.50.cloned.1.call-start = ((), (), s32[]{:S(2)}) async-start(), calls=%async_computation.74 | async-start | bytes 589824
  1931.2 3329.8 %reduce-scatter.101.cloned.1.call-start = ((), (), s32[]{:S(2)}) async-start(), calls=%async_computation.71 | async-start | bytes 737280
  2016.6 3269.2 %reduce-scatter.105.cloned.1.call-start = ((), (), s32[]{:S(2)}) async-start(), calls=%async_computation.73 | async-start | bytes 737280
  2124.6 3185.8 %reduce-scatter.93.cloned.1.call-start = ((), (), s32[]{:S(2)}) async-start(), calls=%async_computation.67 | async-start | bytes 737280
  2232.1 3104.7 %reduce-scatter.103.cloned.1.call-start = ((), (), s32[]{:S(2)}) async-start(), calls=%async_computation.72 | async-start | bytes 1105920
  2465.9 2897.5 %reduce-scatter.79.cloned.1.call-start = ((), (), s32[]{:S(2)}) async-start(), calls=%async_computation.58 | async-start | bytes 1105920 | tf_op jit(solution)/shard_map/reduce_scatter | solution.py:318
  2697.7 2692.1 %reduce-scatter.83.cloned.1.call-start = ((), (), s32[]{:S(2)}) async-start(), calls=%async_computation.60 | async-start | bytes 1105920 | tf_op jit(solution)/shard_map/reduce_scatter | solution.py:318
  2930.2 2486.1 %reduce-scatter.95.cloned.1.call-start = ((), (), s32[]{:S(2)}) async-start(), calls=%async_computation.68 | async-start | bytes 1105920
  3162.8 2280.7 %reduce-scatter.65.cloned.1.call-start = ((), (), s32[]{:S(2)}) async-start(), calls=%async_computation.51 | async-start | bytes 1105920 | tf_op jit(solution)/shard_map/reduce_scatter | solution.py:304
  3394.7 2075.9 %reduce-scatter.61.cloned.1.call-start = ((), (), s32[]{:S(2)}) async-start(), calls=%async_computation.49 | async-start | bytes 1105920 | tf_op jit(solution)/shard_map/reduce_scatter | solution.py:301
  3627.1 1875.5 %reduce-scatter.99.cloned.1.call-start = ((), (), s32[]{:S(2)}) async-start(), calls=%async_computation.70 | async-start | bytes 2211840
  3900.8 1633.7 %reduce-scatter.91.cloned.1.call-start = ((), (), s32[]{:S(2)}) async-start(), calls=%async_computation.66 | async-start | bytes 2211840
  4173.5 1404.1 %reduce-scatter.97.cloned.1.call-start = ((), (), s32[]{:S(2)}) async-start(), calls=%async_computation.69 | async-start | bytes 4423680
  4691.4 929.1 %reduce-scatter.89.cloned.1.call-start = ((), (), s32[]{:S(2)}) async-start(), calls=%async_computation.65 | async-start | bytes 4423680
  (201 other events, 14986.7 us)
Sparse Core Ops, SparseCore 0:
  66.6 52.7 all-gather.24
  122.0 53.5 all-gather.38
  177.6 215.7 all-gather.26
  396.1 117.7 all-gather.28
  516.6 53.1 all-gather.30
  572.1 107.3 all-gather.32
  681.7 106.9 all-gather.34
  790.6 107.6 all-gather.36
  900.5 215.3 all-gather.40
  1118.5 117.7 all-gather.42
  1239.0 53.1 all-gather.44
  1294.3 107.3 all-gather.48
  1403.8 106.9 all-gather.50
  1512.8 106.9 all-gather.46
  1811.7 95.2 reduce-scatter.68
  1910.4 103.8 reduce-scatter.74
  2018.4 103.9 reduce-scatter.86
  2125.9 103.9 reduce-scatter.56
  2234.0 228.9 reduce-scatter.84
  2466.9 228.2 reduce-scatter.76
  2699.3 228.2 reduce-scatter.80
  2931.6 228.2 reduce-scatter.66
  3163.8 228.2 reduce-scatter.62
  3396.2 228.2 reduce-scatter.58
  3629.0 268.4 reduce-scatter.72
  3901.7 268.4 reduce-scatter.54
  4174.6 511.4 reduce-scatter.70
  4690.4 511.4 reduce-scatter.52
  5204.8 31.4 all-reduce.49
  5505.2 29.3 reduce-scatter.90
  5537.1 40.4 reduce-scatter.96
  5580.0 40.4 reduce-scatter.88
  (14 shorter events, 332.9 us)
where the time goes:
time: 5640 us; the launch traced here: 5630 us
  waiting for transfers between devices  4940 us (88%)
  matrix products  263 us (5%)
  blocking collectives  168 us (3%)
  local copies, waits for them, and re-layouts  129 us (2%)
  other arithmetic  113 us (2%)
    reduce_scatter x7, waiting for transfers between devices, reduce_single(): part = lax.psum_scatter(matrix, 'dp', scatter_dimension=0, tiled=True)  1660 us
    reduce_scatter x1, waiting for transfers between devices, reduce_block(): lax.psum_scatter(first, 'dp', scatter_dimension=0, tiled=True)  510 us
    all_gather x2, waiting for transfers between devices, fetch_block(): lax.all_gather(part[0], 'dp', axis=0, tiled=True)  420 us
    reduce_scatter x1, waiting for transfers between devices, reduce_block(): lax.psum_scatter(second, 'dp', scatter_dimension=0, tiled=True)  269 us
    unnamed x56, waiting for transfers between devices  250 us
    reduce_scatter x1, waiting for transfers between devices, reduce_block(): lax.psum_scatter(sixth, 'dp', scatter_dimension=0, tiled=True)  230 us
    reduce_scatter x1, waiting for transfers between devices, reduce_block(): lax.psum_scatter(fourth, 'dp', scatter_dimension=0, tiled=True)  230 us
    reduce_scatter x1, waiting for transfers between devices, reduce_block(): lax.psum_scatter(fifth, 'dp', scatter_dimension=0, tiled=True)  229 us
  transfers between devices with their start and end apart: 46, of which 41 were waited for; matrix products, arithmetic and copies ran while one was open for 6% of the time, Pallas kernels for 0%

commit v1 on v0

v1 whole, which is shorter than its diff:
```python
import functools
import math

import jax
import jax.numpy as jnp
import numpy as np
from jax import lax
from jax.experimental import pallas as pl
from jax.experimental.pallas import tpu as pltpu
from jax.sharding import PartitionSpec as P

HEADS = 16
HEAD = 72
NT = 1000
GRID = 8


EPS = 1e-06


def angle_tables(length):
    places = jnp.arange(length)
    quarter = HEAD // 4
    freqs = jnp.exp(-math.log(10000.0) * jnp.arange(quarter).astype(jnp.float32) / quarter)
    row_angle = (places // GRID).astype(jnp.float32)[:, None] * freqs[None, :]
    col_angle = (places % GRID).astype(jnp.float32)[:, None] * freqs[None, :]
    return (row_angle, col_angle)


def sinusoid(times, width):
    half = width // 2
    freqs = jnp.exp(-math.log(10000.0) * jnp.arange(half).astype(jnp.float32) / half)
    angle = (times * 1000.0)[..., None] * freqs
    return jnp.concatenate([jnp.cos(angle), jnp.sin(angle)], -1)


BF = jnp.bfloat16
F32 = jnp.float32


def dot(left, right):
    return jnp.dot(left, right, preferred_element_type=F32)


def dot_nt(left, right):
    return lax.dot_general(left, right, (((1,), (1,)), ((), ())), preferred_element_type=F32)


def dot_tn(left, right):
    return lax.dot_general(left, right, (((0,), (0,)), ((), ())), preferred_element_type=F32)


def dot_tt(left, right):
    return lax.dot_general(left, right, (((0,), (1,)), ((), ())), preferred_element_type=F32)


def pick(array, index, axis=0):
    return lax.dynamic_index_in_dim(array, index, axis, keepdims=False)


class Noise:
    def __init__(self, count):
        self.count = count
        self.me = lax.axis_index("noise")
        self.quick = count == 4

    def swap(self, array, mask):
        return lax.ppermute(array, "noise", [(n, n ^ mask) for n in range(self.count)])

    def order(self, near):
        odd = self.me % 2 == 1
        far = self.me // 2 == 1
        near = [
            jnp.where(odd, near[1], near[0]),
            jnp.where(odd, near[0], near[1]),
            jnp.where(odd, near[3], near[2]),
            jnp.where(odd, near[2], near[3]),
        ]
        return [
            jnp.where(far, near[2], near[0]),
            jnp.where(far, near[3], near[1]),
            jnp.where(far, near[0], near[2]),
            jnp.where(far, near[1], near[3]),
        ]

    def gather(self, array):
        if not self.quick:
            whole = lax.all_gather(array, "noise", axis=0, tiled=False)
            return [whole[n] for n in range(self.count)]
        across = self.swap(array, 2)
        beside = self.swap(array, 1)
        corner = self.swap(across, 1)
        return self.order([array, beside, across, corner])

    def near(self, array):
        across = self.swap(array, 2)
        beside = self.swap(array, 1)
        return [array, beside, across, self.swap(across, 1)]

    def near_sum(self, keep, send):
        half = keep.astype(F32) + self.swap(send, 1).astype(F32)
        return half[0] + self.swap(half[1].astype(BF), 2).astype(F32)

    def scatter_sum(self, blocks, wire=BF):
        if not self.quick:
            return lax.psum_scatter(
                blocks.astype(wire), "noise", scatter_dimension=0, tiled=False
            ).astype(F32)
        core = self.me % 2
        far = self.me // 2
        pairs = blocks.reshape((2, 2) + blocks.shape[1:])
        keep = pick(pairs, core, 1).astype(F32)
        send = pick(pairs, 1 - core, 1).astype(wire)
        half = keep + self.swap(send, 1).astype(F32)
        return pick(half, far) + self.swap(pick(half, 1 - far).astype(wire), 2).astype(F32)

    def total(self, array):
        if not self.quick:
            return lax.psum(array, "noise")
        array = array + self.swap(array, 1)
        return array + self.swap(array, 2)

    def exchange(self, blocks):
        if not self.quick:
            whole = lax.all_to_all(blocks, "noise", 0, 0)
            return [whole[n] for n in range(self.count)]
        near = [pick(blocks, self.me)]
        for mask in (1, 2, 3):
            near.append(self.swap(pick(blocks, self.me ^ mask), mask))
        return self.order(near)


class Groups:
    def __init__(self, count):
        self.count = count
        self.quick = count == 8
        self.sides = 2
        self.line = count // 2
        self.place = lax.axis_index("dp")
        self.spot = self.place // self.sides
        self.side = self.place % self.sides
        self.across = [
            (z * 2 + x, z * 2 + 1 - x) for z in range(self.line) for x in range(2)
        ]

    def shift(self, array, spots, step):
        pairs = [(z * 2 + x, (z + step) * 2 + x) for z in spots for x in range(2)]
        return lax.ppermute(array, "dp", pairs)

    def swap(self, array, mask):
        return lax.ppermute(array, "dp", [(n, n ^ mask) for n in range(self.count)])

    def gather_whole(self, array):
        return lax.all_gather(array, "dp", axis=0, tiled=False)

    def sum_whole(self, blocks):
        return lax.psum_scatter(
            blocks.astype(BF), "dp", scatter_dimension=0, tiled=False
        ).astype(F32)

    def gather(self, array):
        if not self.quick:
            return self.gather_whole(array)
        last = self.line - 1
        lower, upper = [], []
        up = down = array
        for step in range(1, self.line):
            up = self.shift(up, range(step - 1, last), 1)
            down = self.shift(down, range(1, self.line - step + 1), -1)
            lower.append(up)
            upper.append(down)
        stack = jnp.stack(lower[::-1] + [array] + upper)
        own = lax.dynamic_slice_in_dim(stack, last - self.spot, self.line, 0)
        other = lax.ppermute(own, "dp", self.across)
        first = jnp.where(self.side == 0, own, other)
        second = jnp.where(self.side == 0, other, own)
        whole = jnp.stack([first, second], 1)
        return whole.reshape((self.count,) + array.shape)

    def scatter_sum(self, blocks, wire=BF):
        if not self.quick:
            return self.sum_whole(blocks)
        last = self.line - 1
        pairs = blocks.reshape((self.line, 2) + blocks.shape[1:])
        keep = pick(pairs, self.side, 1).astype(F32)
        send = pick(pairs, 1 - self.side, 1).astype(wire)
        half = keep + lax.ppermute(send, "dp", self.across).astype(F32)
        up = down = None
        for step in range(1, self.line):
            ahead = pick(half, jnp.minimum(self.spot + self.line - step, last))
            behind = pick(half, jnp.maximum(self.spot - self.line + step, 0))
            if up is not None:
                ahead = ahead + up
                behind = behind + down
            up = self.shift(ahead.astype(wire), range(0, step), 1).astype(F32)
            down = self.shift(
                behind.astype(wire), range(self.line - step, self.line), -1
            ).astype(F32)
        return pick(half, self.spot) + up + down

    def gather_small(self, array):
        if not self.quick:
            return self.gather_whole(array)
        array = array[None]
        for mask in (1, 2, 4):
            other = self.swap(array, mask)
            high = (self.place // mask) % 2 == 1
            array = jnp.where(
                high, jnp.concatenate([other, array]), jnp.concatenate([array, other])
            )
        return array

    def sum_small(self, blocks):
        if not self.quick:
            return lax.psum_scatter(blocks, "dp", scatter_dimension=0, tiled=False)
        for mask in (4, 2, 1):
            halves = blocks.reshape((2, -1) + blocks.shape[1:])
            high = (self.place // mask) % 2
            blocks = pick(halves, high) + self.swap(pick(halves, 1 - high), mask)
        return blocks[0]

    def total(self, array):
        if not self.quick:
            return lax.psum(array, "dp")
        for mask in (1, 2, 4):
            array = array + self.swap(array, mask)
        return array


def split_pieces(noise, weight, pieces):
    count = noise.count
    rows, width = weight.shape
    chunk = width // pieces
    slots = -(-pieces // count)
    parts = jnp.moveaxis(weight.reshape(rows, pieces, chunk), 1, 0)
    parts = jnp.concatenate(
        [parts, jnp.zeros((slots * count - pieces, rows, chunk), weight.dtype)]
    ).reshape(slots, count, rows, chunk)
    parts = jnp.roll(parts, pieces * noise.me, axis=1)
    return jnp.moveaxis(parts, 1, 0)


def take_pieces(noise, came, pieces):
    count = noise.count
    out = []
    for piece in range(pieces):
        chunk = count * piece + noise.me
        out.append(came[chunk // pieces, (chunk % pieces) // count])
    return jnp.stack(out, 1)


def return_pieces(noise, grad):
    count = noise.count
    pieces = grad.shape[1]
    slots = -(-pieces // count)
    rows = []
    for target in range(count):
        first = (noise.me - pieces * target) % count
        line = []
        for slot in range(slots):
            turn = jnp.minimum(first + slot * count, pieces - 1)
            line.append(pick(grad, (pieces * target + turn) // count, 1))
        rows.append(jnp.stack(line))
    return jnp.stack(rows)


def join_pieces(noise, came, pieces):
    count = noise.count
    out = []
    for turn in range(pieces):
        chunk = pieces * noise.me + turn
        out.append(came[chunk % count, turn // count])
    joined = jnp.stack(out, 1)
    return joined.reshape(joined.shape[0], -1)


def split_units(noise, groups, weight):
    count = noise.count
    rows, width = weight.shape
    low = groups.count // count
    parts = weight.reshape(rows, low, count, width // (low * count))
    return parts.transpose(2, 0, 1, 3).reshape(count, rows, width // count)


def take_units(noise, groups, came):
    count, rows, width = came.shape
    return jnp.moveaxis(came, 0, 1).reshape(rows, count * width)


def return_units(noise, grad):
    rows, width = grad.shape
    return jnp.moveaxis(grad.reshape(rows, noise.count, width // noise.count), 1, 0)


def join_units(noise, groups, came):
    count, rows, width = came.shape
    low = groups.count // count
    parts = came.reshape(count, rows, low, width // low)
    return parts.transpose(1, 2, 0, 3).reshape(rows, count * width)


def place_weights(noise, groups, w_att, w_gate, w_lift, w_lower, w_mod=None):
    rows = w_att.shape[0]
    att = split_pieces(noise, w_att, 3)
    chunk = att.shape[-1]
    parts = [att.reshape(noise.count, rows, chunk)]
    if w_mod is not None:
        mod = split_pieces(noise, w_mod, 6)
        parts += [mod[:, 0], mod[:, 1]]
    parts.append(split_units(noise, groups, w_gate))
    parts.append(split_units(noise, groups, w_lift))
    unit = parts[-1].shape[-1]
    parts.append(w_lower.reshape(noise.count, rows, unit))
    came = jnp.stack(noise.exchange(jnp.concatenate(parts, -1)))
    spot = 0
    out = [take_pieces(noise, came[:, None, :, :chunk], 3)]
    spot = chunk
    if w_mod is not None:
        mod = jnp.stack([came[:, :, chunk : 2 * chunk], came[:, :, 2 * chunk : 3 * chunk]], 1)
        out.append(take_pieces(noise, mod, 6))
        spot = 3 * chunk
    out.append(take_units(noise, groups, came[:, :, spot : spot + unit]))
    spot += unit
    out.append(take_units(noise, groups, came[:, :, spot : spot + unit]))
    spot += unit
    lower = came[:, :, spot:].reshape(noise.count, -1, w_lower.shape[1])
    lower = jnp.moveaxis(lower, 0, 1)
    out.append(lower.reshape(lower.shape[0], -1))
    return out


def flat(weight):
    return weight.reshape(weight.shape[0] * weight.shape[1], -1)


def norm_parts(value):
    mean = jnp.mean(value, -1, keepdims=True)
    center = value - mean
    inverse = lax.rsqrt(jnp.mean(center * center, -1, keepdims=True) + EPS)
    return center * inverse, inverse


def norm_back(grad, normed, inverse):
    first = jnp.mean(grad, -1, keepdims=True)
    second = jnp.mean(grad * normed, -1, keepdims=True)
    return inverse * (grad - first - normed * second)


def silu_slope(value):
    gate = jax.nn.sigmoid(value)
    return gate * (1.0 + value * (1.0 - gate))


VMEM_BYTES = 48 * 1024 * 1024
STEP = 256


def kernel_call(kernel, grid, ins, outs, scratch=(), scalars=1):
    return pl.pallas_call(
        kernel,
        out_shape=[shape for shape, _ in outs],
        grid_spec=pltpu.PrefetchScalarGridSpec(
            num_scalar_prefetch=scalars,
            grid=grid,
            in_specs=ins,
            out_specs=[spec for _, spec in outs],
            scratch_shapes=list(scratch),
        ),
        compiler_params=pltpu.CompilerParams(vmem_limit_bytes=VMEM_BYTES),
    )


def row_spec(width):
    return pl.BlockSpec((STEP, width), lambda n, *_: (n, 0))


def up_spec(width):
    return pl.BlockSpec((width, STEP), lambda n, *_: (0, n))


def full_spec(shape):
    return pl.BlockSpec(shape, lambda n, *_: (0,) * len(shape))


def shaped(shape, dtype):
    return jax.ShapeDtypeStruct(shape, dtype)


def joined(me_ref, near, parts):
    for n, ref in enumerate(near):
        parts[me_ref[0] ^ n] = ref[...]
    return jnp.concatenate([parts[n] for n in range(4)])


def near_scratch(near):
    return [pltpu.VMEM((4, near[0].shape[0], STEP), BF)]


def join_kernel(upward, me_ref, x0, x1, x2, x3, w_ref, full_ref, out_ref, parts):
    whole = joined(me_ref, (x0, x1, x2, x3), parts)
    full_ref[...] = whole
    if upward:
        out_ref[...] = dot_tn(w_ref[...], whole)
    else:
        out_ref[...] = dot_tn(whole, w_ref[...])


def join_dot(me, near, weight, upward=False):
    quarter, rows = near[0].shape
    width = weight.shape[1]
    if upward:
        out = (shaped((width, rows), F32), up_spec(width))
    else:
        out = (shaped((rows, width), F32), row_spec(width))
    return kernel_call(
        functools.partial(join_kernel, upward),
        (rows // STEP,),
        [up_spec(quarter)] * 4 + [full_spec(weight.shape)],
        [(shaped((4 * quarter, rows), BF), up_spec(4 * quarter)), out],
        near_scratch(near),
    )(me, *near, weight)


def units_kernel(me_ref, x0, x1, x2, x3, w_ref, full_ref, out_ref, hid_ref, parts):
    whole = joined(me_ref, (x0, x1, x2, x3), parts)
    full_ref[...] = whole
    acts = dot_tn(whole, w_ref[...])
    out_ref[...] = acts
    unit = hid_ref.shape[1]
    hid_ref[...] = (jax.nn.silu(acts[:, :unit]) * acts[:, unit:]).astype(BF)


def units_dot(me, near, weight):
    quarter, rows = near[0].shape
    width = weight.shape[1]
    return kernel_call(
        units_kernel,
        (rows // STEP,),
        [up_spec(quarter)] * 4 + [full_spec(weight.shape)],
        [
            (shaped((4 * quarter, rows), BF), up_spec(4 * quarter)),
            (shaped((rows, width), F32), row_spec(width)),
            (shaped((rows, width // 2), BF), row_spec(width // 2)),
        ],
        near_scratch(near),
    )(me, *near, weight)


def lower_kernel(me_ref, x0, x1, x2, x3, w_ref, full_ref, out_ref, parts):
    whole = joined(me_ref, (x0, x1, x2, x3), parts).T
    full_ref[...] = whole
    out_ref[...] = dot_nt(whole, w_ref[...])


def lower_back_dot(me, near, weight):
    quarter, rows = near[0].shape
    width = weight.shape[0]
    return kernel_call(
        lower_kernel,
        (rows // STEP,),
        [up_spec(quarter)] * 4 + [full_spec(weight.shape)],
        [
            (shaped((rows, 4 * quarter), BF), row_spec(4 * quarter)),
            (shaped((rows, width), F32), row_spec(width)),
        ],
        near_scratch(near),
    )(me, *near, weight)


def give(parts, keep_ref, send_ref):
    keep_ref[0] = parts[0]
    keep_ref[1] = parts[2]
    send_ref[0] = parts[1]
    send_ref[1] = parts[3]


def give_outs(rows, quarter):
    pair = pl.BlockSpec((2, quarter, STEP), lambda n, *_: (0, 0, n))
    return [(shaped((2, quarter, rows), BF), pair)] * 2


def spread_kernel(me_ref, y_ref, w_ref, keep_ref, send_ref, parts):
    quarter = keep_ref.shape[1]
    value = y_ref[...]
    for n in range(4):
        term = dot_nt(w_ref[n * quarter : (n + 1) * quarter], value)
        parts[me_ref[0] ^ n] = term.astype(BF)
    give(parts, keep_ref, send_ref)


def spread_dot(me, value, weight):
    rows, width = value.shape
    quarter = weight.shape[0] // 4
    return kernel_call(
        spread_kernel,
        (rows // STEP,),
        [row_spec(width), full_spec(weight.shape)],
        give_outs(rows, quarter),
        [pltpu.VMEM((4, quarter, STEP), BF)],
    )(me, value, weight)


def spread_up_kernel(me_ref, y_ref, w_ref, keep_ref, send_ref, parts):
    quarter = keep_ref.shape[1]
    value = y_ref[...]
    for n in range(4):
        term = dot(w_ref[n * quarter : (n + 1) * quarter], value)
        parts[me_ref[0] ^ n] = term.astype(BF)
    give(parts, keep_ref, send_ref)


def spread_up_dot(me, value, weight):
    width, rows = value.shape
    quarter = weight.shape[0] // 4
    return kernel_call(
        spread_up_kernel,
        (rows // STEP,),
        [up_spec(width), full_spec(weight.shape)],
        give_outs(rows, quarter),
        [pltpu.VMEM((4, quarter, STEP), BF)],
    )(me, value, weight)


def lowered_kernel(me_ref, y_ref, w_ref, keep_ref, send_ref, parts):
    quarter = keep_ref.shape[1]
    term = dot(y_ref[...], w_ref[...]).astype(BF).T
    for n in range(4):
        parts[me_ref[0] ^ n] = term[n * quarter : (n + 1) * quarter]
    give(parts, keep_ref, send_ref)


def lowered_dot(me, value, weight):
    rows, width = value.shape
    quarter = weight.shape[1] // 4
    return kernel_call(
        lowered_kernel,
        (rows // STEP,),
        [row_spec(width), full_spec(weight.shape)],
        give_outs(rows, quarter),
        [pltpu.VMEM((4, quarter, STEP), BF)],
    )(me, value, weight)


def acts_back_kernel(me_ref, g_ref, a_ref, w_ref, acts_ref, keep_ref, send_ref, parts):
    quarter = keep_ref.shape[1]
    unit = g_ref.shape[1]
    grad = g_ref[...]
    gate_act, lift_act = a_ref[:, :unit], a_ref[:, unit:]
    gate = jax.nn.sigmoid(gate_act)
    slope = gate * (1.0 + gate_act * (1.0 - gate))
    acts_ref[:, :unit] = (grad * lift_act * slope).astype(BF)
    acts_ref[:, unit:] = (grad * (gate_act * gate)).astype(BF)
    value = acts_ref[...]
    for n in range(4):
        term = dot_nt(w_ref[n * quarter : (n + 1) * quarter], value)
        parts[me_ref[0] ^ n] = term.astype(BF)
    give(parts, keep_ref, send_ref)


def acts_back(me, grad, acts, weight):
    rows, unit = grad.shape
    quarter = weight.shape[0] // 4
    return kernel_call(
        acts_back_kernel,
        (rows // STEP,),
        [row_spec(unit), row_spec(2 * unit), full_spec(weight.shape)],
        [(shaped((rows, 2 * unit), BF), row_spec(2 * unit))] + give_outs(rows, quarter),
        [pltpu.VMEM((4, quarter, STEP), BF)],
    )(me, grad, acts, weight)


def grad_kernel(x_ref, y_ref, out_ref):
    out_ref[...] = dot(x_ref[...], y_ref[...]).astype(BF)


def grad_turned_kernel(x_ref, y_ref, out_ref):
    out_ref[...] = dot_nt(x_ref[...], y_ref[...]).astype(BF)


def grad_low_kernel(x_ref, y_ref, out_ref):
    out_ref[...] = dot_tn(x_ref[...], y_ref[...]).astype(BF)


def grad_dot(left, right, kernel=grad_kernel):
    step = 384
    low = kernel is grad_low_kernel
    width, rows = left.shape[::-1] if low else left.shape
    wide = right.shape[0] if kernel is grad_turned_kernel else right.shape[1]
    if low:
        spec = pl.BlockSpec((rows, step), lambda n: (0, n))
    else:
        spec = pl.BlockSpec((step, rows), lambda n: (n, 0))
    return pl.pallas_call(
        kernel,
        out_shape=shaped((width, wide), BF),
        grid=(width // step,),
        in_specs=[spec, pl.BlockSpec(right.shape, lambda n: (0, 0))],
        out_specs=pl.BlockSpec((step, wide), lambda n: (n, 0)),
        compiler_params=pltpu.CompilerParams(vmem_limit_bytes=VMEM_BYTES),
    )(left, right)


def mod_kernel(x_ref, w_ref, out_ref):
    out_ref[...] = dot(x_ref[...], w_ref[...]).T


def mod_dot(value, weight):
    rows, width = value.shape
    wide = weight.shape[1]
    return kernel_call(
        mod_kernel,
        (rows // STEP,),
        [row_spec(width), full_spec(weight.shape)],
        [(shaped((wide, rows), F32), up_spec(wide))],
        scalars=0,
    )(value, weight)[0]


def mod_back_kernel(*refs):
    parts, (w_ref, cat_ref, out_ref) = refs[:6], refs[6:]
    grad = jnp.concatenate([ref[...] for ref in parts]).T
    cat_ref[...] = grad
    out_ref[...] = dot_nt(grad, w_ref[...])


def mod_back(parts, weight):
    quarter, rows = parts[0].shape
    return kernel_call(
        mod_back_kernel,
        (rows // STEP,),
        [up_spec(quarter)] * 6 + [full_spec(weight.shape)],
        [
            (shaped((rows, 6 * quarter), BF), row_spec(6 * quarter)),
            (shaped((rows, weight.shape[0]), F32), row_spec(weight.shape[0])),
        ],
        scalars=0,
    )(*parts, weight)


def kind_width(kind, quarter):
    if kind[0] == "pieces":
        return -(-kind[1] // 4) * quarter
    if kind[0] == "units":
        return kind[1] // 4
    return quarter


def pack_parts(me, kinds, low, quarter):
    out = []
    spot = 0
    for item, kind in enumerate(kinds):
        for far in range(4):
            to = me ^ far
            if kind[0] == "pieces":
                count = kind[1]
                for slot in range(-(-count // 4)):
                    turn = (to - count * me) % 4 + 4 * slot
                    if turn < count:
                        out.append(
                            (item, far, None, turn * quarter, spot + slot * quarter, quarter)
                        )
            elif kind[0] == "units":
                each = kind[1] // (4 * low)
                for n in range(low):
                    at = n * 4 * each + to * each
                    out.append((item, far, None, at, spot + n * each, each))
            else:
                out.append((item, far, (to * kind[1], kind[1]), 0, spot, quarter))
        spot += kind_width(kind, quarter)
    return out


def unpack_parts(me, kinds, low, quarter):
    out = []
    spot = 0
    for item, kind in enumerate(kinds):
        for far in range(4):
            come = me ^ far
            if kind[0] == "pieces":
                count = kind[1]
                for slot in range(-(-count // 4)):
                    turn = (me - count * come) % 4 + 4 * slot
                    if turn < count:
                        piece = (count * come + turn) // 4
                        out.append(
                            (item, far, None, piece * quarter, spot + slot * quarter, quarter)
                        )
            elif kind[0] == "units":
                each = kind[1] // (4 * low)
                for n in range(low):
                    at = (come * low + n) * each
                    out.append((item, far, None, at, spot + n * each, each))
            else:
                out.append((item, far, (0, kind[1]), come * quarter, spot, quarter))
        spot += kind_width(kind, quarter)
    return out


def pack_kernel(plan, me_ref, *refs):
    items, out_ref = refs[:-1], refs[-1]
    out_ref[...] = jnp.zeros_like(out_ref)
    for me in range(4):

        @pl.when(me_ref[0] == me)
        def _():
            for item, far, lines, at, spot, size in plan(me):
                first, count = lines or (0, out_ref.shape[1])
                out_ref[far, :count, spot : spot + size] = items[item][
                    first : first + count, at : at + size
                ].astype(BF)


def unpack_kernel(plan, me_ref, *refs):
    packets, outs = refs[:4], refs[4:]
    for me in range(4):

        @pl.when(me_ref[0] == me)
        def _():
            for item, far, lines, at, spot, size in plan(me):
                first, count = lines or (0, packets[0].shape[0])
                outs[item][first : first + count, at : at + size] = packets[far][
                    :count, spot : spot + size
                ].astype(outs[item].dtype)


def whole_call(kernel, outs, me, args):
    return kernel_call(
        kernel,
        (1,),
        [full_spec(arg.shape) for arg in args],
        [(out, full_spec(out.shape)) for out in outs],
    )(me, *args)


def trade(noise, me, arrays, kinds, low, back, shapes, dtype):
    quarter = kind_quarter(kinds, arrays, back)
    width = sum(kind_width(kind, quarter) for kind in kinds)
    lines = max(a.shape[0] for a, kind in zip(arrays, kinds) if kind[0] != "lower")
    there, here = (unpack_parts, pack_parts) if back else (pack_parts, unpack_parts)
    packed = whole_call(
        functools.partial(
            pack_kernel, functools.partial(there, kinds=kinds, low=low, quarter=quarter)
        ),
        [shaped((4, lines, width), BF)],
        me,
        arrays,
    )[0]
    near = [packed[0]] + [noise.swap(packed[n], n) for n in (1, 2, 3)]
    return whole_call(
        functools.partial(
            unpack_kernel, functools.partial(here, kinds=kinds, low=low, quarter=quarter)
        ),
        [shaped(shape, dtype) for shape in shapes],
        me,
        near,
    )


def kind_quarter(kinds, arrays, back):
    for array, kind in zip(arrays, kinds):
        if kind[0] == "pieces":
            return array.shape[1] // kind[1]
        if kind[0] == "lower":
            return array.shape[1] // 4 if back else array.shape[1]


def attend_tables(length, repeat, gains):
    heads = HEADS // 4
    row_angle, col_angle = angle_tables(length)
    angle = jnp.concatenate([row_angle, row_angle, col_angle, col_angle], -1)
    angle = jnp.tile(angle, (repeat, heads))
    spread = jnp.tile(gains, (1, heads))
    return jnp.cos(angle), jnp.sin(angle), spread


def attend_matrices():
    width = HEADS // 4 * HEAD
    quarter = HEAD // 4
    index = np.arange(width)
    same = (index[:, None] // HEAD == index[None, :] // HEAD).astype(np.float32)
    second = (index % (2 * quarter)) >= quarter
    source = np.where(second, index - quarter, index + quarter)
    turn = np.zeros((width, width), np.float32)
    turn[source, index] = np.where(second, 1.0, -1.0)
    low = jnp.asarray(same, BF), jnp.asarray(turn, BF), jnp.asarray(turn.T, BF)
    return low


def halves_dot(value, matrix):
    high = value.astype(BF)
    rest = (value - high.astype(F32)).astype(BF)
    return dot(high, matrix) + dot(rest, matrix)


def head_masks(width):
    lane = lax.broadcasted_iota(jnp.int32, (1, width), 1)
    return [
        jnp.logical_and(lane >= n * HEAD, lane < (n + 1) * HEAD).astype(F32)
        for n in range(width // HEAD)
    ]


def ready_heads(value, gain, cosine, sine, same, turn):
    inverse = lax.rsqrt(halves_dot(value * value, same) * (1.0 / HEAD) + EPS)
    normed = value * inverse
    scaled = normed * gain
    turned = scaled * cosine + halves_dot(scaled, turn) * sine
    return turned.astype(BF), normed, inverse


def stack_heads(value, masks):
    value = value.astype(F32)
    return jnp.concatenate([value * mask for mask in masks]).astype(BF)


def fold_heads(value, masks, length):
    out = value[:length] * masks[0]
    for n in range(1, len(masks)):
        out = out + value[n * length : (n + 1) * length] * masks[n]
    return out


def prob_of(stacked, keys_low):
    scores = dot_nt(stacked, keys_low) * HEAD ** (-0.5)
    grown = jnp.exp(scores - jnp.max(scores, -1, keepdims=True))
    return grown / jnp.sum(grown, -1, keepdims=True)


def attend_kernel(
    length,
    upward,
    p_ref,
    cos_ref,
    sin_ref,
    gain_ref,
    same_ref,
    turn_ref,
    out_ref,
    mixed_ref,
):
    width = mixed_ref.shape[1]
    q_ref, k_ref, v_ref = [p_ref[:, n * width : (n + 1) * width] for n in range(3)]
    masks = head_masks(width)
    same, turn = same_ref[...], turn_ref[...]
    cosine, sine = cos_ref[...], sin_ref[...]
    query, _, _ = ready_heads(q_ref, gain_ref[0:1], cosine, sine, same, turn)
    key, _, _ = ready_heads(k_ref, gain_ref[1:2], cosine, sine, same, turn)
    value = v_ref.astype(BF)
    for image in range(mixed_ref.shape[0] // length):
        part = slice(image * length, (image + 1) * length)
        prob = prob_of(stack_heads(query[part], masks), key[part])
        mixed = dot(prob.astype(BF), value[part])
        mixed_ref[part] = fold_heads(mixed, masks, length)
    if upward:
        out_ref[...] = mixed_ref[...].T.astype(BF)
    else:
        out_ref[...] = mixed_ref[...].astype(BF)


def attend_back_kernel(
    length,
    upward,
    p_ref,
    cos_ref,
    sin_ref,
    gain_ref,
    same_ref,
    turn_ref,
    back_ref,
    grad_ref,
    dp_ref,
    dg_ref,
    gq_ref,
    gk_ref,
    gv_ref,
):
    width = gq_ref.shape[1]
    q_ref, k_ref, v_ref = [p_ref[:, n * width : (n + 1) * width] for n in range(3)]
    masks = head_masks(width)
    same, turn, back = same_ref[...], turn_ref[...], back_ref[...]
    cosine, sine = cos_ref[...], sin_ref[...]
    query, q_norm, q_inv = ready_heads(q_ref, gain_ref[0:1], cosine, sine, same, turn)
    key, k_norm, k_inv = ready_heads(k_ref, gain_ref[1:2], cosine, sine, same, turn)
    value = v_ref.astype(BF)
    grad = grad_ref[...].T if upward else grad_ref[...]
    for image in range(q_ref.shape[0] // length):
        part = slice(image * length, (image + 1) * length)
        stacked = stack_heads(query[part], masks)
        prob = prob_of(stacked, key[part])
        grads = stack_heads(grad[part], masks)
        gv_ref[part] = dot_tn(prob.astype(BF), grads)
        g_prob = dot_nt(grads, value[part])
        g_score = prob * (g_prob - jnp.sum(g_prob * prob, -1, keepdims=True))
        g_score = g_score.astype(BF)
        gq_ref[part] = fold_heads(dot(g_score, key[part]), masks, length)
        gk_ref[part] = dot_tn(g_score, stacked)

    @pl.when(pl.program_id(0) == 0)
    def _():
        dg_ref[...] = jnp.zeros_like(dg_ref)

    for n, (g_ref, normed, inverse) in enumerate(
        ((gq_ref, q_norm, q_inv), (gk_ref, k_norm, k_inv))
    ):
        turned = g_ref[...] * HEAD ** (-0.5)
        scaled = turned * cosine + halves_dot(turned * sine, back)
        dg_ref[n : n + 1] += jnp.sum(scaled * normed, 0, keepdims=True)
        weighed = scaled * gain_ref[n : n + 1]
        mean = halves_dot(weighed * normed, same) * (1.0 / HEAD)
        out = inverse * (weighed - normed * mean)
        dp_ref[:, n * width : (n + 1) * width] = out.astype(BF)
    dp_ref[:, 2 * width :] = gv_ref[...].astype(BF)


def attend_blocks(rows, length, width):
    step = STEP

    def row(size):
        return pl.BlockSpec((step, size), lambda n: (n, 0))

    def whole(*shape):
        return pl.BlockSpec(shape, lambda n: (0, 0))

    return step, row, whole


def attend_forward(project, gains, length, upward=False):
    rows, width = project.shape[0], project.shape[1] // 3
    step, row, whole = attend_blocks(rows, length, width)
    cosine, sine, spread = attend_tables(length, step // length, gains)
    same, turn, _ = attend_matrices()
    return pl.pallas_call(
        functools.partial(attend_kernel, length, upward),
        out_shape=shaped((width, rows) if upward else (rows, width), BF),
        grid=(rows // step,),
        in_specs=[row(3 * width), whole(step, width), whole(step, width), whole(2, width)]
        + [whole(width, width)] * 2,
        out_specs=up_spec(width) if upward else row(width),
        scratch_shapes=[pltpu.VMEM((step, width), F32)],
        compiler_params=pltpu.CompilerParams(vmem_limit_bytes=VMEM_BYTES),
    )(project, cosine, sine, spread, same, turn)


def attend_backward(grad_low, gains, project, length, upward=False):
    rows, width = project.shape[0], project.shape[1] // 3
    step, row, whole = attend_blocks(rows, length, width)
    cosine, sine, spread = attend_tables(length, step // length, gains)
    same, turn, back = attend_matrices()
    grad, gain_grad = pl.pallas_call(
        functools.partial(attend_back_kernel, length, upward),
        out_shape=(shaped((rows, 3 * width), BF), shaped((2, width), F32)),
        grid=(rows // step,),
        in_specs=[row(3 * width), whole(step, width), whole(step, width), whole(2, width)]
        + [whole(width, width)] * 3
        + [up_spec(width) if upward else row(width)],
        out_specs=(row(3 * width), whole(2, width)),
        scratch_shapes=[pltpu.VMEM((step, width), F32)] * 3,
        compiler_params=pltpu.CompilerParams(vmem_limit_bytes=VMEM_BYTES),
    )(project, cosine, sine, spread, same, turn, back, grad_low)
    return grad, jnp.sum(gain_grad.reshape(2, width // HEAD, HEAD), 1)


def per_device(
    groups_count,
    noise_count,
    clean_tokens,
    noise_tokens,
    time_index,
    class_label,
    velocity_cotangent,
    encoder_modulate,
    encoder_attend,
    encoder_merge,
    encoder_gate,
    encoder_lift,
    encoder_lower,
    class_table,
    encoder_gains,
    decoder_modulate,
    decoder_attend,
    decoder_merge,
    decoder_gate,
    decoder_lift,
    decoder_lower,
    time_weight,
    decoder_gains,
):
    noise = Noise(noise_count)
    groups = Groups(groups_count)
    own_images, length, width = clean_tokens.shape
    images = own_images * noise_count
    levels = noise_count
    quarter = width // noise_count
    own_rows = own_images * length
    rows = images * length
    place = noise.me * quarter

    def columns(value):
        return lax.dynamic_slice_in_dim(value, place, quarter, value.ndim - 1)

    def column_blocks(value):
        return jnp.moveaxis(value.reshape(value.shape[0], noise_count, quarter), 1, 0)

    def token_blocks(value):
        return value.reshape(noise_count, own_rows, width)

    me = noise.me.reshape(1)
    unit = encoder_gate.shape[1]
    chunk_rows = encoder_attend.shape[0]
    lower_rows = encoder_lower.shape[0] // noise_count
    low_units = groups_count // noise_count
    e_kinds = (("pieces", 3), ("units", unit), ("units", unit), ("lower", lower_rows))
    d_kinds = e_kinds + (("pieces", 6),)
    shapes = ((chunk_rows, 3 * quarter), (chunk_rows, unit), (chunk_rows, unit))
    shapes += ((lower_rows, width), (chunk_rows, 6 * quarter))
    if groups.quick:
        e_att_s, e_gate_s, e_lift_s, e_lower_s = trade(
            noise,
            me,
            (encoder_attend, encoder_gate, encoder_lift, encoder_lower),
            e_kinds,
            low_units,
            False,
            shapes[:4],
            BF,
        )
    else:
        e_att_s, e_gate_s, e_lift_s, e_lower_s = place_weights(
            noise, groups, encoder_attend, encoder_gate, encoder_lift, encoder_lower
        )
    (
        e_att_s,
        e_gate_s,
        e_lift_s,
        e_lower_s,
        clean_tokens,
        noise_tokens,
        velocity_cotangent,
        time_index,
        class_label,
        decoder_attend,
        decoder_gate,
    ) = lax.optimization_barrier(
        (
            e_att_s,
            e_gate_s,
            e_lift_s,
            e_lower_s,
            clean_tokens,
            noise_tokens,
            velocity_cotangent,
            time_index,
            class_label,
            decoder_attend,
            decoder_gate,
        )
    )
    e_first = groups.gather(
        jnp.concatenate([e_att_s.reshape(chunk_rows, -1), encoder_merge], -1)
    )
    e_att = flat(e_first[:, :, : 3 * quarter])
    e_merge = flat(e_first[:, :, 3 * quarter :])
    e_second = groups.gather(jnp.concatenate([e_gate_s, e_lift_s], -1))
    e_gate = flat(e_second[:, :, :unit])
    e_lift = flat(e_second[:, :, unit:])
    e_lower = flat(groups.gather(e_lower_s))
    if groups.quick:
        d_att_s, d_gate_s, d_lift_s, d_lower_s, d_mod_s = trade(
            noise,
            me,
            (decoder_attend, decoder_gate, decoder_lift, decoder_lower, decoder_modulate),
            d_kinds,
            low_units,
            False,
            shapes,
            BF,
        )
    else:
        d_att_s, d_mod_s, d_gate_s, d_lift_s, d_lower_s = place_weights(
            noise,
            groups,
            decoder_attend,
            decoder_gate,
            decoder_lift,
            decoder_lower,
            decoder_modulate,
        )
    d_first_s = jnp.concatenate(
        [
            d_mod_s.reshape(chunk_rows, -1),
            d_att_s.reshape(chunk_rows, -1),
            decoder_merge,
            time_weight,
        ],
        -1,
    )

    def pad_lower(part):
        ends = ((0, 0),) * (part.ndim - 1) + ((0, 2 * unit - width),)
        return jnp.pad(part, ends)

    d_second_s = jnp.concatenate(
        [jnp.concatenate([d_gate_s, d_lift_s], -1), pad_lower(d_lower_s)]
    )
    d_first_s, _ = lax.optimization_barrier((d_first_s, e_second))
    d_whole = flat(groups.gather_whole(d_first_s))
    d_second_s, d_whole = lax.optimization_barrier((d_second_s, d_whole))
    d_pair = groups.gather_whole(d_second_s)
    d_mod, d_att, d_merge, d_time = [
        d_whole[:, first * quarter : last * quarter]
        for first, last in ((0, 6), (6, 9), (9, 10), (10, 11))
    ]
    d_units = flat(d_pair[:, :chunk_rows])
    d_lower = flat(d_pair[:, chunk_rows:, :width])

    facts = jnp.concatenate([class_label, time_index[0]])
    facts = jnp.stack(noise.gather(facts))
    times = (facts[:, own_images:].astype(F32) + 0.5) / NT
    labels = groups.gather_small(facts[:, :own_images].reshape(-1)).reshape(-1)

    here = class_table.shape[1]
    onehot = (
        labels[:, None] == (jnp.arange(here) + noise.me * here)[None, :]
    ).astype(BF)
    class_cond = noise.total(dot_nt(onehot, class_table))
    class_low = jax.nn.silu(class_cond).astype(BF)
    class_mod = dot(class_low, encoder_modulate)
    class_mod = groups.sum_small(
        class_mod.reshape(groups_count, images, class_mod.shape[1])
    )
    class_mod = jnp.concatenate(noise.gather(class_mod), -1)

    clean_group = jnp.concatenate(noise.gather(clean_tokens.reshape(own_rows, width)))
    clean_all = clean_group.astype(F32)
    own_times = (time_index[0].astype(F32) + 0.5) / NT
    own_ratio = jnp.repeat(own_times, length)[:, None]
    own_noise = noise_tokens[0].reshape(rows, width)
    own_cot = velocity_cotangent[0].reshape(rows, width)
    own_noisy = (1.0 - own_ratio) * clean_all + own_ratio * own_noise.astype(F32)
    own_mean = jnp.mean(own_noisy, -1)
    own_center = own_noisy - own_mean[:, None]
    own_inverse = lax.rsqrt(jnp.mean(own_center * own_center, -1) + EPS)
    stats = jnp.stack(noise.gather(jnp.stack([own_mean, own_inverse])))
    mean_one = stats[:, 0].reshape(1, -1)
    inverse_one = stats[:, 1].reshape(1, -1)
    came = noise.exchange(
        jnp.stack(
            [
                own_noise.T.reshape(noise_count, quarter, rows),
                own_cot.T.reshape(noise_count, quarter, rows),
            ],
            1,
        )
    )
    noise_cols = jnp.concatenate([part[0] for part in came], -1)
    cot_cols = jnp.concatenate([part[1] for part in came], -1).astype(F32)

    e_piece = [
        jnp.repeat(part, length, axis=0) for part in jnp.split(class_mod, 6, axis=-1)
    ]
    e_norm_one, e_inverse_one = norm_parts(clean_all)
    e_one = (e_norm_one * (1.0 + e_piece[1]) + e_piece[0]).astype(BF)
    e_heads = dot(e_one, e_att)
    e_mixed = attend_forward(e_heads, encoder_gains, length)
    e_mixed_all = jnp.concatenate(noise.gather(e_mixed), -1)
    e_merged = jnp.concatenate(
        noise.gather(dot(e_mixed_all, e_merge).astype(BF)), -1
    ).astype(F32)
    e_middle = clean_all + e_piece[2] * e_merged
    e_norm_two, e_inverse_two = norm_parts(e_middle)
    e_two = (e_norm_two * (1.0 + e_piece[4]) + e_piece[3]).astype(BF)
    e_gate_act = dot(e_two, e_gate)
    e_lift_act = dot(e_two, e_lift)
    e_hidden = (jax.nn.silu(e_gate_act) * e_lift_act).astype(BF)
    e_lowered = noise.scatter_sum(token_blocks(dot(e_hidden, e_lower)))

    def own_part(value):
        return lax.dynamic_slice_in_dim(value, noise.me * own_rows, own_rows, 0)

    latent_own = own_part(e_middle) + own_part(e_piece[5]) * e_lowered
    latent_low = latent_own.astype(BF)
    latent_all = jnp.concatenate(noise.gather(latent_low)).astype(F32)

    sines = sinusoid(times, width).astype(BF).reshape(levels * images, width)
    temb = jnp.concatenate(noise.gather(dot(sines, d_time)), -1)
    cond = (
        latent_all.reshape(1, images, length, width)
        + temb.reshape(levels, images, 1, width)
    ).reshape(levels * rows, width)
    cond_low = jax.nn.silu(cond).astype(BF)
    mod = mod_dot(cond_low, d_mod)
    shift_one, scale_one, gate_one, shift_two, scale_two, gate_two = [
        mod[n * quarter : (n + 1) * quarter] for n in range(6)
    ]
    ratio = jnp.repeat(times.reshape(-1), length)[None]
    clean_up = lax.dynamic_slice_in_dim(clean_group.T, place, quarter, 0).astype(F32)
    noisy = (1.0 - ratio) * jnp.tile(clean_up, (1, levels)) + ratio * noise_cols.astype(F32)
    norm_one = (noisy - mean_one) * inverse_one
    one = (norm_one * (1.0 + scale_one) + shift_one).astype(BF)
    one_all, heads = join_dot(me, noise.near(one), d_att)
    mixed = attend_forward(heads, decoder_gains, length, True)
    mixed_all, merged = join_dot(me, noise.near(mixed), d_merge, True)
    middle = noisy + gate_one * merged
    part_mean = jnp.mean(middle, 0)
    part_center = middle - part_mean[None]
    part_square = jnp.sum(part_center * part_center, 0)
    parts = noise.near(jnp.stack([part_mean, part_square]))
    mean_two = sum(part[0] for part in parts) / noise_count
    square = sum(part[1] + quarter * (part[0] - mean_two) ** 2 for part in parts)
    inverse_two = lax.rsqrt(square / width + EPS)[None]
    norm_two = (middle - mean_two[None]) * inverse_two
    two = (norm_two * (1.0 + scale_two) + shift_two).astype(BF)
    two_all, acts, hidden = units_dot(me, noise.near(two), d_units)
    lowered = noise.near_sum(*lowered_dot(me, hidden, d_lower))
    output = (middle + gate_two * lowered).astype(BF)
    velocity = jnp.concatenate(
        noise.exchange(jnp.moveaxis(output.reshape(quarter, levels, rows), 1, 0))
    )
    velocity = velocity.T.reshape(1, images, length, width)

    def norm_back_cols(grad, normed, inverse):
        sums = noise.total(jnp.stack([jnp.sum(grad, 0), jnp.sum(grad * normed, 0)]))
        sums = sums[:, None] / width
        return inverse * (grad - sums[0] - normed * sums[1])

    low_cols = (cot_cols * gate_two).astype(BF)
    low_all, g_hidden = lower_back_dot(me, noise.near(low_cols), d_lower)
    g_gate_two = cot_cols * lowered
    g_acts, *given = acts_back(me, g_hidden, acts, d_units)
    g_two = noise.near_sum(*given)
    gw_lower = grad_dot(hidden, low_all, grad_low_kernel)
    gw_units = grad_dot(two_all, g_acts)
    g_middle = cot_cols + norm_back_cols(g_two * (1.0 + scale_two), norm_two, inverse_two)
    g_merged_low = (g_middle * gate_one).astype(BF)
    g_mixed = noise.near_sum(*spread_up_dot(me, g_merged_low, d_merge))
    gw_merge = grad_dot(mixed_all, g_merged_low, grad_turned_kernel)
    g_heads, d_gain_grad = attend_backward(
        g_mixed.astype(BF), decoder_gains, heads, length, True
    )
    g_one = noise.near_sum(*spread_dot(me, g_heads, d_att))
    gw_att = grad_dot(one_all, g_heads)
    g_noisy = g_middle + norm_back_cols(g_one * (1.0 + scale_one), norm_one, inverse_one)
    g_parts = (
        g_one,
        g_one * norm_one,
        g_middle * merged,
        g_two,
        g_two * norm_two,
        g_gate_two,
    )
    g_mod, g_cond_low = mod_back([part.astype(BF) for part in g_parts], d_mod)
    gw_mod = grad_dot(cond_low, g_mod, grad_low_kernel)
    g_cond = g_cond_low * silu_slope(cond)
    g_temb = noise.scatter_sum(
        column_blocks(jnp.sum(g_cond.reshape(levels * images, length, width), 1)), F32
    ).astype(BF)
    gw_time = dot_tn(sines, g_temb)
    g_latent = noise.scatter_sum(token_blocks(jnp.sum(g_cond.reshape(levels, rows, width), 0)))
    g_clean_cols = jnp.sum(
        ((1.0 - ratio) * g_noisy).reshape(quarter, levels, rows), 1
    ).astype(BF).T
    g_clean = jnp.concatenate(
        noise.exchange(g_clean_cols.reshape(noise_count, own_rows, quarter)), -1
    ).astype(F32)

    piece = [own_part(part) for part in e_piece]
    norm_two_own = own_part(e_norm_two)
    norm_one_own = own_part(e_norm_one)
    e_low_all = jnp.concatenate(noise.gather((g_latent * piece[5]).astype(BF)))
    e_g_gate_two = g_latent * e_lowered
    ew_lower = dot_tn(e_hidden, e_low_all)
    e_g_hidden = dot_nt(e_low_all, e_lower)
    e_g_gate_low = (e_g_hidden * e_lift_act * silu_slope(e_gate_act)).astype(BF)
    e_g_lift_low = (e_g_hidden * jax.nn.silu(e_gate_act)).astype(BF)
    ew_gate = dot_tn(e_two, e_g_gate_low)
    ew_lift = dot_tn(e_two, e_g_lift_low)
    e_g_two = noise.scatter_sum(
        token_blocks(dot_nt(e_g_gate_low, e_gate) + dot_nt(e_g_lift_low, e_lift))
    )
    e_g_middle = g_latent + norm_back(
        e_g_two * (1.0 + piece[4]), norm_two_own, own_part(e_inverse_two)
    )
    e_merged_low = jnp.concatenate(noise.gather((e_g_middle * piece[2]).astype(BF)))
    e_merged_cols = columns(e_merged_low)
    ew_merge = dot_tn(e_mixed_all, e_merged_cols)
    e_g_mixed = noise.scatter_sum(column_blocks(dot_nt(e_merged_cols, e_merge)))
    e_g_heads, e_gain_grad = attend_backward(
        e_g_mixed.astype(BF), encoder_gains, e_heads, length
    )
    ew_att = dot_tn(e_one, e_g_heads)
    e_g_one = noise.scatter_sum(token_blocks(dot_nt(e_g_heads, e_att)))
    e_g_clean = e_g_middle + norm_back(
        e_g_one * (1.0 + piece[1]), norm_one_own, own_part(e_inverse_one)
    )
    clean_grad = (e_g_clean + g_clean).reshape(own_images, length, width)
    e_g_mod = jnp.concatenate(
        [
            e_g_one,
            e_g_one * norm_one_own,
            e_g_middle * own_part(e_merged),
            e_g_two,
            e_g_two * norm_two_own,
            e_g_gate_two,
        ],
        -1,
    )
    e_g_mod = jnp.sum(e_g_mod.reshape(own_images, length, -1), 1).astype(BF)
    every_mod = noise.exchange(
        jnp.moveaxis(e_g_mod.reshape(own_images, noise_count, -1), 1, 0)
    )
    every_mod = groups.gather_small(jnp.concatenate(every_mod))
    every_mod = every_mod.reshape(-1, every_mod.shape[-1])
    grad_e_mod = dot_tn(class_low, every_mod)
    g_class = noise.total(dot_nt(every_mod, encoder_modulate)) * silu_slope(class_cond)
    grad_table = lax.dot_general(
        g_class,
        onehot.astype(F32),
        (((0,), (0,)), ((), ())),
        precision=lax.Precision.HIGHEST,
        preferred_element_type=F32,
    )

    def by_group(grad):
        low = grad.astype(BF)
        return low.reshape((groups_count, -1) + low.shape[1:])

    def finish_pieces(mine, pieces):
        mine = mine.astype(BF).reshape(mine.shape[0], pieces, quarter)
        came = jnp.stack(noise.exchange(return_pieces(noise, mine)))
        return join_pieces(noise, came, pieces).astype(F32)

    def finish_units(mine):
        came = jnp.stack(noise.exchange(return_units(noise, mine.astype(BF))))
        return join_units(noise, groups, came).astype(F32)

    def finish_lower(mine):
        mine = mine.astype(BF).reshape(-1, width)
        came = jnp.stack(noise.exchange(column_blocks(mine)))
        return came.reshape(-1, quarter).astype(F32)

    def finish(arrays, picked, e_or_d):
        kinds = tuple(e_or_d[n] for n in picked)
        full = (
            (chunk_rows, encoder_attend.shape[1]),
            (chunk_rows, unit),
            (chunk_rows, unit),
            encoder_lower.shape,
            (chunk_rows, encoder_modulate.shape[1]),
        )
        if groups.quick:
            return trade(
                noise,
                me,
                arrays,
                kinds,
                low_units,
                True,
                [full[n] for n in picked],
                F32,
            )
        ends = {"units": finish_units, "lower": finish_lower}
        return [
            finish_pieces(array, kind[1]) if kind[0] == "pieces" else ends[kind[0]](array)
            for array, kind in zip(arrays, kinds)
        ]

    d_second = groups.sum_whole(
        jnp.concatenate([by_group(gw_units), pad_lower(by_group(gw_lower))], 1)
    )
    grad_d_gate, grad_d_lift, grad_d_lower = finish(
        (
            d_second[:chunk_rows, :unit],
            d_second[:chunk_rows, unit:],
            d_second[chunk_rows:, :width],
        ),
        (1, 2, 3),
        d_kinds,
    )
    d_first = groups.sum_whole(
        jnp.concatenate([by_group(part) for part in [gw_mod, gw_att, gw_merge, gw_time]], -1)
    )
    grad_d_att, grad_d_mod = finish(
        (d_first[:, 6 * quarter : 9 * quarter], d_first[:, : 6 * quarter]), (0, 4), d_kinds
    )
    grad_d_merge = d_first[:, 9 * quarter : 10 * quarter]
    grad_time = d_first[:, 10 * quarter :]
    e_low_sum = groups.scatter_sum(by_group(ew_lower))
    e_second = groups.scatter_sum(
        jnp.concatenate([by_group(ew_gate), by_group(ew_lift)], -1)
    )
    e_first = groups.scatter_sum(
        jnp.concatenate([by_group(part) for part in [ew_att, ew_merge]], -1)
    )
    grad_e_att, grad_e_gate, grad_e_lift, grad_e_lower = finish(
        (e_first[:, : 3 * quarter], e_second[:, :unit], e_second[:, unit:], e_low_sum),
        (0, 1, 2, 3),
        e_kinds,
    )
    grad_e_merge = e_first[:, 3 * quarter :]
    gain_total = groups.total(noise.total(jnp.stack([e_gain_grad, d_gain_grad])))
    return (
        velocity,
        latent_low.reshape(own_images, length, width),
        clean_grad,
        grad_e_mod,
        grad_e_att,
        grad_e_merge,
        grad_e_gate,
        grad_e_lift,
        grad_e_lower,
        grad_table,
        gain_total[0],
        grad_d_mod,
        grad_d_att,
        grad_d_merge,
        grad_d_gate,
        grad_d_lift,
        grad_d_lower,
        grad_time,
        gain_total[1],
    )


def solution(mesh):
    return jax.shard_map(
        functools.partial(per_device, mesh.shape["dp"], mesh.shape["noise"]),
        mesh=mesh,
        in_specs=(
            P(("dp", "noise"), None, None),
            P("noise", "dp", None, None),
            P("noise", "dp"),
            P(("dp", "noise")),
            P("noise", "dp", None, None),
            P("dp", "noise"),
            P("dp", "noise"),
            P("dp", "noise"),
            P("dp", "noise"),
            P("dp", "noise"),
            P("dp", "noise"),
            P("dp", "noise"),
            P(),
            P("dp", "noise"),
            P("dp", "noise"),
            P("dp", "noise"),
            P("dp", "noise"),
            P("dp", "noise"),
            P("dp", "noise"),
            P("dp", "noise"),
            P(),
        ),
        out_specs=(
            P("noise", "dp", None, None),
            P(("dp", "noise"), None, None),
            P(("dp", "noise"), None, None),
            P("dp", "noise"),
            P("dp", "noise"),
            P("dp", "noise"),
            P("dp", "noise"),
            P("dp", "noise"),
            P("dp", "noise"),
            P("dp", "noise"),
            P(),
            P("dp", "noise"),
            P("dp", "noise"),
            P("dp", "noise"),
            P("dp", "noise"),
            P("dp", "noise"),
            P("dp", "noise"),
            P("dp", "noise"),
            P(),
        ),
        check_vma=False,
    )
```

time: 5640 us -> 1030 us (0.18)
  waiting for transfers between devices: 4940 us -> 366 us
  matrix products: 263 us -> 23.1 us
  starting transfers between devices: 2.88 us -> 175 us
  blocking collectives: 168 us -> 0 us
  Pallas kernels: 0 us -> 151 us
    reduce_scatter x20 -> x2, waiting for transfers between devices: 3350 us -> 0.01 us  [sum_whole(): lax.psum_scatter(blocks.astype(BF), 'dp', scatter_dimension=0, tiled=False)]
    all_gather x16 -> x2, waiting for transfers between devices: 1330 us -> 25.3 us  [gather_whole(): return lax.all_gather(array, 'dp', axis=0, tiled=False)]
    ppermute x0 -> x156, waiting for transfers between devices: none -> 340 us  [the longest x102 166 us: swap(): lax.ppermute(array, 'noise', [(n, n ^ mask) for n in range(self.count)])]
    unnamed x56 -> x4, waiting for transfers between devices: 250 us -> 0.07 us
    dot_general x50 -> x22, matrix products: 263 us -> 23.1 us  [the longest x7 8.02 us: dot_nt(): lax.dot_general(left, right, (((1,), (1,)), ((), ())), preferred_element_...]
    ppermute x0 -> x156, starting transfers between devices: none -> 174 us  [the longest x36 88.5 us: shift(): return lax.ppermute(array, 'dp', pairs)]
    pallas_call x0 -> x29, Pallas kernels: none -> 151 us  [the longest x2 34.8 us: attend_backward(): pl.pallas_call(functools.partial(attend_back_kernel, length, upward), out...]
    all_gather x14 -> x0, blocking collectives: 128 us -> none  [the longest x2 22.7 us: fetch_block(): lax.all_gather(second, 'noise', axis=1, tiled=True)]
  transfers between devices with their start and end apart: 46 -> 160, of which waited for: 41 -> 62; matrix products, arithmetic and copies ran while one was open for 6% -> 26% of each run, Pallas kernels for 0% -> 15%
where the time goes in v1:
time: 1030 us; the launch traced here: 1010 us
  waiting for transfers between devices  366 us (36%)
  starting transfers between devices  175 us (17%)
  local copies, waits for them, and re-layouts  161 us (16%)
  Pallas kernels  151 us (15%)
  other arithmetic  118 us (11%)
  matrix products  23.1 us (2%)
  between operations  18.3 us (2%)
    ppermute x102, waiting for transfers between devices, swap(): lax.ppermute(array, 'noise', [(n, n ^ mask) for n in range(self.count)])  166 us
    ppermute x36, starting transfers between devices, shift(): return lax.ppermute(array, 'dp', pairs)  88.5 us
    ppermute x12, waiting for transfers between devices, swap(): return lax.ppermute(array, 'dp', [(n, n ^ mask) for n in range(self.count)])  78.4 us
    unnamed x445, local copies, waits for them, and re-layouts  62.6 us
    ppermute x102, starting transfers between devices, swap(): lax.ppermute(array, 'noise', [(n, n ^ mask) for n in range(self.count)])  55.9 us
    ppermute x3, waiting for transfers between devices, gather(): other = lax.ppermute(own, 'dp', self.across)  45.2 us
    ppermute x36, waiting for transfers between devices, shift(): return lax.ppermute(array, 'dp', pairs)  44.1 us
    pallas_call x2, Pallas kernels, attend_backward(): pl.pallas_call(functools.partial(attend_back_kernel, length, upward), out...  34.8 us
  transfers between devices with their start and end apart: 160, of which 62 were waited for; matrix products, arithmetic and copies ran while one was open for 26% of the time, Pallas kernels for 15%

profile of v1, /device:TPU:0, one launch (start us, length us, event | category | flops | bytes accessed | tf_op | source)
XLA Modules:
  0.0 1012.5 jit_solution(995936337310342570)
XLA Ops:
  23.8 6.0 collective-permute-done.2.refs_3_
  107.2 8.8 collective-permute-start.23
  121.0 7.8 collective-permute-done.40
  136.7 11.0 %collective-permute-done.41 = bf16[144,1536]{1,0:T(8,128)(2,1)S(1)} collective-permute-done((bf16[144,1536]{1,0:T(8,128)(2,1)}, bf16[144,1536]{1,0:T(8,128)(2,1)S(1)}, u32[]{:S(2)}, u32[]{:S(2)}) %collective-permute-start.41) | collective-permute-done | bytes 442400 | tf_op jit(solution)/shard_map/ppermute | solution.py:148
  167.2 6.5 collective-permute-done.57.refs_3_
  207.4 35.2 %collective-permute-done.29 = bf16[4,144,1152]{2,1,0:T(8,128)(2,1)S(1)} collective-permute-done((bf16[4,144,1152]{2,1,0:T(8,128)(2,1)S(1)}, bf16[4,144,1152]{2,1,0:T(8,128)(2,1)S(1)}, u32[]{:S(2)}, u32[]{:S(2)}) %collective-permute-start.29) | collective-permute-done | bytes 1327136 | tf_op jit(solution)/shard_map/ppermute | solution.py:174
  266.8 10.0 collective-permute-done.49
  298.6 25.3 %all-gather.5.cloned.1.call-done = bf16[1152,3168]{1,0:T(8,128)(2,1)} async-done(((bf16[144,3168]{1,0:T(8,128)(2,1)}), bf16[1152,3168]{1,0:T(8,128)(2,1)}) %all-gather.5.cloned.1.call-update) | async-done | bytes 7299088 | tf_op jit(solution)/shard_map/all_gather | solution.py:154
  353.6 9.6 shard_map.443
  367.7 15.0 %collective-permute-done.65.x2 = bf16[288,1024]{1,0:T(8,128)(2,1)} collective-permute-done((bf16[288,1024]{1,0:T(8,128)(2,1)}, bf16[288,1024]{1,0:T(8,128)(2,1)}, u32[]{:S(2)}, u32[]{:S(2)}) %collective-permute-start.65) | collective-permute-done | bytes 589856 | tf_op jit(solution)/shard_map/ppermute | solution.py:68
  385.6 7.3 shard_map.444
  395.0 14.9 %shard_map.445.x0 = bf16[288,1024]{1,0:T(8,128)(2,1)S(1)} custom-call(f32[1024,864]{1,0:T(8,128)S(1)} %copy-done.2, f32[256,288]{1,0:T(8,128)S(1)} %copy.201.cos_ref, f32[256,288]{1,0:T(8,128)S(1)} %copy-done.4, f32[2,288]{1,0:T(2,128)S(1)} %tile.23.gain_ref, bf16[288,288]{1,0:T(8,128)(2,1)S(1)} %copy-done.20, bf16[288,288]{1,0:T(8,128)(2,1)S(1)} %copy-done.22), custom_call_target="tpu_custom_call" | custom-call | tf_op jit(solution)/shard_map/pallas_call | solution.py:932
  411.1 14.7 %collective-permute-done.68.x2 = bf16[288,1024]{1,0:T(8,128)(2,1)S(1)} collective-permute-done((bf16[288,1024]{1,0:T(8,128)(2,1)S(1)}, bf16[288,1024]{1,0:T(8,128)(2,1)S(1)}, u32[]{:S(2)}, u32[]{:S(2)}) %collective-permute-start.68) | collective-permute-done | bytes 589856 | tf_op jit(solution)/shard_map/ppermute | solution.py:68
  440.6 14.8 %collective-permute-done.74.x2 = bf16[288,1024]{1,0:T(8,128)(2,1)} collective-permute-done((bf16[288,1024]{1,0:T(8,128)(2,1)}, bf16[288,1024]{1,0:T(8,128)(2,1)}, u32[]{:S(2)}, u32[]{:S(2)}) %collective-permute-start.74) | collective-permute-done | bytes 589856 | tf_op jit(solution)/shard_map/ppermute | solution.py:68
  461.9 9.2 shard_map.447
  486.7 9.5 shard_map.450
  518.4 6.6 collective-permute-done.77
  525.0 12.0 %collective-permute-done.85 = bf16[288,1024]{1,0:T(8,128)(2,1)} collective-permute-done((bf16[288,1024]{1,0:T(8,128)(2,1)}, bf16[288,1024]{1,0:T(8,128)(2,1)}, u32[]{:S(2)}, u32[]{:S(2)}) %collective-permute-start.85) | collective-permute-done | bytes 589856 | tf_op jit(solution)/shard_map/ppermute | solution.py:68
  559.4 14.2 %collective-permute-done.89 = bf16[288,1024]{1,0:T(8,128)(2,1)S(1)} collective-permute-done((bf16[288,1024]{1,0:T(8,128)(2,1)S(1)}, bf16[288,1024]{1,0:T(8,128)(2,1)S(1)}, u32[]{:S(2)}, u32[]{:S(2)}) %collective-permute-start.89) | collective-permute-done | bytes 589856 | tf_op jit(solution)/shard_map/ppermute | solution.py:68
  573.8 28.2 %shard_map.452 = (bf16[1024,864]{1,0:T(8,128)(2,1)S(1)}, f32[2,288]{1,0:T(2,128)S(1)}) custom-call(f32[1024,864]{1,0:T(8,128)} %get-tuple-element.97.p_ref, f32[256,288]{1,0:T(8,128)S(1)} %copy.201.cos_ref, f32[256,288]{1,0:T(8,128)S(1)} %copy-done.5, f32[2,288]{1,0:T(2,128)S(1)} %tile.23.gain_ref, bf16[288,288]{1,0:T(8,128)(2,1)S(1)} %copy-done.20, ...), custom_call_target="tpu_custom_call" | custom-call | tf_op jit(solution)/shard_map/pallas_call | solution.py:949
  602.0 6.7 shard_map.453
  648.5 9.3 shard_map.454
  679.5 6.4 shard_map.458
  710.9 12.7 %concatenate.208 = bf16[8,144,3168]{2,1,0:T(8,128)(2,1)} concatenate(bf16[8,144,1728]{2,1,0:T(8,128)(2,1)} %bitcast.655, bf16[8,144,864]{2,1,0:T(8,128)(2,1)S(1)} %bitcast.636, bf16[8,144,288]{2,1,0:T(8,128)(2,1)} %bitcast.638, bf16[8,144,288]{2,1,0:T(8,128)(2,1)} %bitcast.689), dimensions={2} | concatenate | bytes 14598144 | tf_op jit(solution)/shard_map/concatenate | solution.py:1380
  754.8 6.2 collective-permute-done.131
  766.6 6.8 collective-permute-start.132
  773.5 6.6 shard_map.455
  788.3 33.1 %collective-permute-done.145 = f32[2,2,72]{2,1,0:T(2,128)S(1)} collective-permute-done((f32[2,2,72]{2,1,0:T(2,128)S(1)}, f32[2,2,72]{2,1,0:T(2,128)S(1)}, u32[]{:S(2)}, u32[]{:S(2)}) %collective-permute-start.145) | collective-permute-done | bytes 1184 | tf_op jit(solution)/shard_map/ppermute | solution.py:151
  828.7 5.8 collective-permute-start.147
  854.5 29.0 %collective-permute-done.114 = bf16[1,4,1728]{2,1,0:T(4,128)(2,1)S(1)} collective-permute-done((bf16[1,4,1728]{2,1,0:T(4,128)(2,1)S(1)}, bf16[1,4,1728]{2,1,0:T(4,128)(2,1)S(1)}, u32[]{:S(2)}, u32[]{:S(2)}) %collective-permute-start.114) | collective-permute-done | bytes 13856 | tf_op jit(solution)/shard_map/ppermute | solution.py:151
  941.6 12.3 %collective-permute-start.120 = (bf16[144,1152]{1,0:T(8,128)(2,1)S(1)}, bf16[144,1152]{1,0:T(8,128)(2,1)S(1)}, u32[]{:S(2)}, u32[]{:S(2)}) collective-permute-start(bf16[144,1152]{1,0:T(8,128)(2,1)S(1)} %get-tuple-element.282), channel_id=1, source_target_pairs={{0,8},{4,12},{8,16},{12,20},{16,24},{20,28},{1,9},{5,13},{9,17},{1... | collective-permute-start | bytes 995336 | tf_op jit(solution)/shard_map/ppermute | solution.py:148
  955.3 5.9 collective-permute-done.130
  (1063 shorter events, 587.0 us)
Async XLA Ops:
  7.2 316.6 %all-gather.5.cloned.1.call-start = ((), (), s32[]{:S(2)}) async-start(), calls=%async_computation.4 | async-start | bytes 8294400 | tf_op jit(solution)/shard_map/all_gather | solution.py:154
  31.7 57.7 %collective-permute-start.6 = (bf16[64,1152]{1,0:T(8,128)(2,1)}, bf16[64,1152]{1,0:T(8,128)(2,1)}, u32[]{:S(2)}, u32[]{:S(2)}) collective-permute-start(bf16[64,1152]{1,0:T(8,128)(2,1)} %bitcast.718), channel_id=1, source_target_pairs={{0,2},{1,3},{2,0},{3,1},{4,6},{5,7},{6,4},{7,5},{8,10},{9,11},{10,... | collective-permute-start | bytes 442376 | tf_op jit(solution)/shard_map/ppermute | solution.py:68
  33.2 72.6 %collective-permute-start.8 = (bf16[64,1152]{1,0:T(8,128)(2,1)}, bf16[64,1152]{1,0:T(8,128)(2,1)}, u32[]{:S(2)}, u32[]{:S(2)}) collective-permute-start(bf16[64,1152]{1,0:T(8,128)(2,1)} %bitcast.719), channel_id=1, source_target_pairs={{0,1},{1,0},{2,3},{3,2},{4,5},{5,4},{6,7},{7,6},{8,9},{9,8},{10,11... | collective-permute-start | bytes 442376 | tf_op jit(solution)/shard_map/ppermute | solution.py:68
  39.3 52.7 %collective-permute-start.10 = (bf16[2,288,256]{2,1,0:T(8,128)(2,1)}, bf16[2,288,256]{2,1,0:T(8,128)(2,1)}, u32[]{:S(2)}, u32[]{:S(2)}) collective-permute-start(bf16[2,288,256]{2,1,0:T(8,128)(2,1)} %get-tuple-element.314), channel_id=1, source_target_pairs={{0,2},{1,3},{2,0},{3,1},{4,6},{5,7},{6,4},{7,5},{8,10},{9,11},{10,... | collective-permute-start | bytes 884744 | tf_op jit(solution)/shard_map/ppermute | solution.py:68
  92.0 24.0 %collective-permute-start.39 = (bf16[144,1536]{1,0:T(8,128)(2,1)}, bf16[144,1536]{1,0:T(8,128)(2,1)}, u32[]{:S(2)}, u32[]{:S(2)}) collective-permute-start(bf16[144,1536]{1,0:T(8,128)(2,1)} %copy-done.147), channel_id=1, source_target_pairs={{8,0},{12,4},{16,8},{20,12},{24,16},{28,20},{9,1},{13,5},{17,9},{2... | collective-permute-start | bytes 1327112 | tf_op jit(solution)/shard_map/ppermute | solution.py:148
  93.3 58.5 %collective-permute-start.43 = (bf16[96,1152]{1,0:T(8,128)(2,1)S(1)}, bf16[96,1152]{1,0:T(8,128)(2,1)}, u32[]{:S(2)}, u32[]{:S(2)}) collective-permute-start(bf16[96,1152]{1,0:T(8,128)(2,1)S(1)} %get-tuple-element.87), channel_id=1, source_target_pairs={{0,8},{4,12},{8,16},{12,20},{16,24},{20,28},{1,9},{5,13},{9,17},{1... | collective-permute-start | bytes 663560 | tf_op jit(solution)/shard_map/ppermute | solution.py:148
  105.9 46.0 %collective-permute-start.46 = (bf16[96,1152]{1,0:T(8,128)(2,1)S(1)}, bf16[96,1152]{1,0:T(8,128)(2,1)}, u32[]{:S(2)}, u32[]{:S(2)}) collective-permute-start(bf16[96,1152]{1,0:T(8,128)(2,1)S(1)} %get-tuple-element.87), channel_id=1, source_target_pairs={{8,0},{12,4},{16,8},{20,12},{24,16},{28,20},{9,1},{13,5},{17,9},{2... | collective-permute-start | bytes 663560 | tf_op jit(solution)/shard_map/ppermute | solution.py:148
  107.2 46.3 %collective-permute-start.23 = (bf16[144,1152]{1,0:T(8,128)(2,1)}, bf16[144,1152]{1,0:T(8,128)(2,1)}, u32[]{:S(2)}, u32[]{:S(2)}) collective-permute-start(bf16[144,1152]{1,0:T(8,128)(2,1)} %pad_maximum_fusion.7), channel_id=1, source_target_pairs={{0,8},{4,12},{8,16},{12,20},{16,24},{20,28},{1,9},{5,13},{9,17},{1... | collective-permute-start | bytes 995336 | tf_op jit(solution)/shard_map/ppermute | solution.py:148
  128.8 24.9 %collective-permute-start.26 = (bf16[144,1152]{1,0:T(8,128)(2,1)}, bf16[144,1152]{1,0:T(8,128)(2,1)}, u32[]{:S(2)}, u32[]{:S(2)}) collective-permute-start(bf16[144,1152]{1,0:T(8,128)(2,1)} %pad_maximum_fusion.7), channel_id=1, source_target_pairs={{8,0},{12,4},{16,8},{20,12},{24,16},{28,20},{9,1},{13,5},{17,9},{2... | collective-permute-start | bytes 995336 | tf_op jit(solution)/shard_map/ppermute | solution.py:148
  149.9 37.8 %collective-permute-start.42 = (bf16[4,144,1536]{2,1,0:T(8,128)(2,1)}, bf16[4,144,1536]{2,1,0:T(8,128)(2,1)}, u32[]{:S(2)}, u32[]{:S(2)}) collective-permute-start(bf16[4,144,1536]{2,1,0:T(8,128)(2,1)} %constant_dynamic-slice_fusion.15), channel_id=1, source_target_pairs={{0,4},{4,0},{8,12},{12,8},{16,20},{20,16},{24,28},{28,24},{1,5},{5... | collective-permute-start | bytes 5308424 | tf_op jit(solution)/shard_map/ppermute | solution.py:174
  156.2 27.8 %collective-permute-start.24 = (bf16[144,1152]{1,0:T(8,128)(2,1)}, bf16[144,1152]{1,0:T(8,128)(2,1)}, u32[]{:S(2)}, u32[]{:S(2)}) collective-permute-start(bf16[144,1152]{1,0:T(8,128)(2,1)} %collective-permute-done.23), channel_id=1, source_target_pairs={{8,16},{12,20},{16,24},{20,28},{9,17},{13,21},{17,25},{21,29},{10,... | collective-permute-start | bytes 995336 | tf_op jit(solution)/shard_map/ppermute | solution.py:148
  157.8 27.7 %collective-permute-start.27 = (bf16[144,1152]{1,0:T(8,128)(2,1)}, bf16[144,1152]{1,0:T(8,128)(2,1)}, u32[]{:S(2)}, u32[]{:S(2)}) collective-permute-start(bf16[144,1152]{1,0:T(8,128)(2,1)} %collective-permute-done.26), channel_id=1, source_target_pairs={{8,0},{12,4},{16,8},{20,12},{9,1},{13,5},{17,9},{21,13},{10,2},{14... | collective-permute-start | bytes 995336 | tf_op jit(solution)/shard_map/ppermute | solution.py:148
  192.3 264.0 %all-gather.7.cloned.1.call-start = ((), (), s32[]{:S(2)}) async-start(), calls=%async_computation.5 | async-start | bytes 6635520 | tf_op jit(solution)/shard_map/all_gather | solution.py:154
  201.2 41.3 %collective-permute-start.29 = (bf16[4,144,1152]{2,1,0:T(8,128)(2,1)S(1)}, bf16[4,144,1152]{2,1,0:T(8,128)(2,1)S(1)}, u32[]{:S(2)}, u32[]{:S(2)}) collective-permute-start(bf16[4,144,1152]{2,1,0:T(8,128)(2,1)S(1)} %constant_dynamic-slice_fusion.16), channel_id=1, source_target_pairs={{0,4},{4,0},{8,12},{12,8},{16,20},{20,16},{24,28},{28,24},{1,5},{5... | collective-permute-start | bytes 3981320 | tf_op jit(solution)/shard_map/ppermute | solution.py:174
  206.4 70.4 %collective-permute-start.49 = (bf16[4,96,1152]{2,1,0:T(8,128)(2,1)}, bf16[4,96,1152]{2,1,0:T(8,128)(2,1)}, u32[]{:S(2)}, u32[]{:S(2)}) collective-permute-start(bf16[4,96,1152]{2,1,0:T(8,128)(2,1)} %constant_dynamic-slice_fusion.14), channel_id=1, source_target_pairs={{0,4},{4,0},{8,12},{12,8},{16,20},{20,16},{24,28},{28,24},{1,5},{5... | collective-permute-start | bytes 2654216 | tf_op jit(solution)/shard_map/ppermute | solution.py:174
  297.6 30.4 %collective-permute-start.50 = (bf16[2,64,1152]{2,1,0:T(8,128)(2,1)}, bf16[2,64,1152]{2,1,0:T(8,128)(2,1)}, u32[]{:S(2)}, u32[]{:S(2)}) collective-permute-start(bf16[2,64,1152]{2,1,0:T(8,128)(2,1)} %fusion.62), channel_id=1, source_target_pairs={{0,1},{1,0},{2,3},{3,2},{4,5},{5,4},{6,7},{7,6},{8,9},{9,8},{10,11... | collective-permute-start | bytes 884744 | tf_op jit(solution)/shard_map/ppermute | solution.py:68
  323.8 645.1 %reduce-scatter.5.cloned.1.call-start = ((), (), s32[]{:S(2)}) async-start(), calls=%async_computation.3 | async-start | bytes 6635520 | tf_op jit(solution)/shard_map/reduce_scatter | solution.py:157
  476.2 30.9 %collective-permute-start.76 = (bf16[2,288,1024]{2,1,0:T(8,128)(2,1)}, bf16[2,288,1024]{2,1,0:T(8,128)(2,1)S(1)}, u32[]{:S(2)}, u32[]{:S(2)}) collective-permute-start(bf16[2,288,1024]{2,1,0:T(8,128)(2,1)} %get-tuple-element.102), channel_id=1, source_target_pairs={{0,1},{1,0},{2,3},{3,2},{4,5},{5,4},{6,7},{7,6},{8,9},{9,8},{10,11... | collective-permute-start | bytes 3538952 | tf_op jit(solution)/shard_map/ppermute | solution.py:68
  513.9 23.0 %collective-permute-start.85 = (bf16[288,1024]{1,0:T(8,128)(2,1)}, bf16[288,1024]{1,0:T(8,128)(2,1)}, u32[]{:S(2)}, u32[]{:S(2)}) collective-permute-start(bf16[288,1024]{1,0:T(8,128)(2,1)} %fusion.47), channel_id=1, source_target_pairs={{0,2},{1,3},{2,0},{3,1},{4,6},{5,7},{6,4},{7,5},{8,10},{9,11},{10,... | collective-permute-start | bytes 1769480 | tf_op jit(solution)/shard_map/ppermute | solution.py:68
  518.3 453.5 %reduce-scatter.3.cloned.1.call-start = ((), (), s32[]{:S(2)}) async-start(), calls=%async_computation.2 | async-start | bytes 8294400 | tf_op jit(solution)/shard_map/reduce_scatter | solution.py:157
  669.5 25.0 %collective-permute-start.148 = (f32[2,16,288]{2,0,1:T(2,128)}, f32[2,16,288]{2,0,1:T(2,128)}, u32[]{:S(2)}, u32[]{:S(2)}) collective-permute-start(f32[2,16,288]{2,0,1:T(2,128)} %bitcast.632), channel_id=1, source_target_pairs={{0,1},{1,0},{2,3},{3,2},{4,5},{5,4},{6,7},{7,6},{8,9},{9,8},{10,11... | collective-permute-start | bytes 110600 | tf_op jit(solution)/shard_map/ppermute | solution.py:68
  733.4 27.7 %collective-permute-start.131 = (bf16[4,96,1152]{2,1,0:T(8,128)(2,1)}, bf16[4,96,1152]{2,1,0:T(8,128)(2,1)}, u32[]{:S(2)}, u32[]{:S(2)}) collective-permute-start(bf16[4,96,1152]{2,1,0:T(8,128)(2,1)} %dynamic-slice_bitcast_fusion), channel_id=1, source_target_pairs={{0,4},{4,0},{8,12},{12,8},{16,20},{20,16},{24,28},{28,24},{1,5},{5... | collective-permute-start | bytes 2654216 | tf_op jit(solution)/shard_map/ppermute | solution.py:187
  748.4 149.7 %collective-permute-start.124 = (bf16[4,144,1536]{2,1,0:T(8,128)(2,1)}, bf16[4,144,1536]{2,1,0:T(8,128)(2,1)}, u32[]{:S(2)}, u32[]{:S(2)}) collective-permute-start(bf16[4,144,1536]{2,1,0:T(8,128)(2,1)} %fusion.10), channel_id=1, source_target_pairs={{0,4},{4,0},{8,12},{12,8},{16,20},{20,16},{24,28},{28,24},{1,5},{5... | collective-permute-start | bytes 5308424 | tf_op jit(solution)/shard_map/ppermute | solution.py:187
  783.8 38.3 %collective-permute-start.104 = (bf16[2,64,1152]{2,1,0:T(8,128)(2,1)S(1)}, bf16[2,64,1152]{2,1,0:T(8,128)(2,1)S(1)}, u32[]{:S(2)}, u32[]{:S(2)}) collective-permute-start(bf16[2,64,1152]{2,1,0:T(8,128)(2,1)S(1)} %fusion.65), channel_id=1, source_target_pairs={{0,1},{1,0},{2,3},{3,2},{4,5},{5,4},{6,7},{7,6},{8,9},{9,8},{10,11... | collective-permute-start | bytes 884744 | tf_op jit(solution)/shard_map/ppermute | solution.py:68
  786.4 34.9 %collective-permute-start.145 = (f32[2,2,72]{2,1,0:T(2,128)S(1)}, f32[2,2,72]{2,1,0:T(2,128)S(1)}, u32[]{:S(2)}, u32[]{:S(2)}) collective-permute-start(f32[2,2,72]{2,1,0:T(2,128)S(1)} %fusion.191), channel_id=1, source_target_pairs={{0,4},{4,0},{8,12},{12,8},{16,20},{20,16},{24,28},{28,24},{1,5},{5... | collective-permute-start | bytes 3464 | tf_op jit(solution)/shard_map/ppermute | solution.py:151
  849.2 35.9 %collective-permute-start.135 = (bf16[96,1152]{1,0:T(8,128)(2,1)S(1)}, bf16[96,1152]{1,0:T(8,128)(2,1)S(1)}, u32[]{:S(2)}, u32[]{:S(2)}) collective-permute-start(bf16[96,1152]{1,0:T(8,128)(2,1)S(1)} %copy-done.165), channel_id=1, source_target_pairs={{24,16},{28,20},{25,17},{29,21},{26,18},{30,22},{27,19},{31,23}} | collective-permute-start | bytes 663560 | tf_op jit(solution)/shard_map/ppermute | solution.py:148
  849.9 35.2 %collective-permute-start.133 = (bf16[96,1152]{1,0:T(8,128)(2,1)S(1)}, bf16[96,1152]{1,0:T(8,128)(2,1)S(1)}, u32[]{:S(2)}, u32[]{:S(2)}) collective-permute-start(bf16[96,1152]{1,0:T(8,128)(2,1)S(1)} %copy-done.166), channel_id=1, source_target_pairs={{0,8},{4,12},{8,16},{12,20},{1,9},{5,13},{9,17},{13,21},{2,10},{6,... | collective-permute-start | bytes 663560 | tf_op jit(solution)/shard_map/ppermute | solution.py:148
  851.7 55.6 %collective-permute-start.117 = (bf16[4,144,1152]{2,1,0:T(8,128)(2,1)}, bf16[4,144,1152]{2,1,0:T(8,128)(2,1)}, u32[]{:S(2)}, u32[]{:S(2)}) collective-permute-start(bf16[4,144,1152]{2,1,0:T(8,128)(2,1)} %fusion.15), channel_id=1, source_target_pairs={{0,4},{4,0},{8,12},{12,8},{16,20},{20,16},{24,28},{28,24},{1,5},{5... | collective-permute-start | bytes 3981320 | tf_op jit(solution)/shard_map/ppermute | solution.py:187
  852.3 31.2 %collective-permute-start.114 = (bf16[1,4,1728]{2,1,0:T(4,128)(2,1)S(1)}, bf16[1,4,1728]{2,1,0:T(4,128)(2,1)S(1)}, u32[]{:S(2)}, u32[]{:S(2)}) collective-permute-start(bf16[1,4,1728]{2,1,0:T(4,128)(2,1)S(1)} %maximum_bitcast_fusion.1), channel_id=1, source_target_pairs={{0,4},{4,0},{8,12},{12,8},{16,20},{20,16},{24,28},{28,24},{1,5},{5... | collective-permute-start | bytes 41480 | tf_op jit(solution)/shard_map/ppermute | solution.py:151
  897.2 78.5 %collective-permute-start.142 = (f32[32,144]{1,0:T(8,128)S(1)}, f32[32,144]{1,0:T(8,128)S(1)}, u32[]{:S(2)}, u32[]{:S(2)}) collective-permute-start(f32[32,144]{1,0:T(8,128)S(1)} %add.853), channel_id=1, source_target_pairs={{0,2},{1,3},{2,0},{3,1},{4,6},{5,7},{6,4},{7,5},{8,10},{9,11},{10,... | collective-permute-start | bytes 55304 | tf_op jit(solution)/shard_map/ppermute | solution.py:68
  905.1 22.1 %collective-permute-start.128 = (bf16[144,1536]{1,0:T(8,128)(2,1)S(1)}, bf16[144,1536]{1,0:T(8,128)(2,1)S(1)}, u32[]{:S(2)}, u32[]{:S(2)}) collective-permute-start(bf16[144,1536]{1,0:T(8,128)(2,1)S(1)} %get-tuple-element.274), channel_id=1, source_target_pairs={{24,16},{28,20},{25,17},{29,21},{26,18},{30,22},{27,19},{31,23}} | collective-permute-start | bytes 1327112 | tf_op jit(solution)/shard_map/ppermute | solution.py:148
  933.1 22.1 %collective-permute-start.127 = (bf16[144,1536]{1,0:T(8,128)(2,1)S(1)}, bf16[144,1536]{1,0:T(8,128)(2,1)S(1)}, u32[]{:S(2)}, u32[]{:S(2)}) collective-permute-start(bf16[144,1536]{1,0:T(8,128)(2,1)S(1)} %get-tuple-element.271), channel_id=1, source_target_pairs={{0,8},{4,12},{8,16},{12,20},{16,24},{20,28},{1,9},{5,13},{9,17},{1... | collective-permute-start | bytes 1327112 | tf_op jit(solution)/shard_map/ppermute | solution.py:148
  (336 other events, 3520.9 us)
Sparse Core Ops, SparseCore 0:
  192.4 131.3 all-gather.4
  326.0 93.6 all-gather.6
  518.4 110.5 reduce-scatter.4
  723.7 150.4 reduce-scatter.2

commit v2 on v1

--- a/solution.py
+++ b/solution.py
@@ -19,11 +19,11 @@
 
 
 def angle_tables(length):
-    places = jnp.arange(length)
+    places = np.arange(length)
     quarter = HEAD // 4
-    freqs = jnp.exp(-math.log(10000.0) * jnp.arange(quarter).astype(jnp.float32) / quarter)
-    row_angle = (places // GRID).astype(jnp.float32)[:, None] * freqs[None, :]
-    col_angle = (places % GRID).astype(jnp.float32)[:, None] * freqs[None, :]
+    freqs = np.exp(-math.log(10000.0) * np.arange(quarter) / quarter)
+    row_angle = (places // GRID)[:, None] * freqs[None, :]
+    col_angle = (places % GRID)[:, None] * freqs[None, :]
     return (row_angle, col_angle)
 
 
@@ -147,6 +147,14 @@
         pairs = [(z * 2 + x, (z + step) * 2 + x) for z in spots for x in range(2)]
         return lax.ppermute(array, "dp", pairs)
 
+    def turn(self, array, step):
+        pairs = [
+            (z * 2 + x, (z + step) % self.line * 2 + x)
+            for z in range(self.line)
+            for x in range(2)
+        ]
+        return lax.ppermute(array, "dp", pairs)
+
     def swap(self, array, mask):
         return lax.ppermute(array, "dp", [(n, n ^ mask) for n in range(self.count)])
 
@@ -160,43 +168,23 @@
 
     def gather(self, array):
         if not self.quick:
-            return self.gather_whole(array)
-        last = self.line - 1
-        lower, upper = [], []
-        up = down = array
-        for step in range(1, self.line):
-            up = self.shift(up, range(step - 1, last), 1)
-            down = self.shift(down, range(1, self.line - step + 1), -1)
-            lower.append(up)
-            upper.append(down)
-        stack = jnp.stack(lower[::-1] + [array] + upper)
-        own = lax.dynamic_slice_in_dim(stack, last - self.spot, self.line, 0)
-        other = lax.ppermute(own, "dp", self.across)
-        first = jnp.where(self.side == 0, own, other)
-        second = jnp.where(self.side == 0, other, own)
-        whole = jnp.stack([first, second], 1)
-        return whole.reshape((self.count,) + array.shape)
+            return self.gather_whole(array), array
+        near = [array] + [self.turn(array, step) for step in (1, 2, 3)]
+        far = [lax.ppermute(part, "dp", self.across) for part in near]
+        return place_blocks(self.place.reshape(1), near + far), near[3]
 
     def scatter_sum(self, blocks, wire=BF):
         if not self.quick:
             return self.sum_whole(blocks)
-        last = self.line - 1
         pairs = blocks.reshape((self.line, 2) + blocks.shape[1:])
         keep = pick(pairs, self.side, 1).astype(F32)
         send = pick(pairs, 1 - self.side, 1).astype(wire)
         half = keep + lax.ppermute(send, "dp", self.across).astype(F32)
-        up = down = None
-        for step in range(1, self.line):
-            ahead = pick(half, jnp.minimum(self.spot + self.line - step, last))
-            behind = pick(half, jnp.maximum(self.spot - self.line + step, 0))
-            if up is not None:
-                ahead = ahead + up
-                behind = behind + down
-            up = self.shift(ahead.astype(wire), range(0, step), 1).astype(F32)
-            down = self.shift(
-                behind.astype(wire), range(self.line - step, self.line), -1
-            ).astype(F32)
-        return pick(half, self.spot) + up + down
+        total = pick(half, self.spot)
+        for step in (1, 3, 2):
+            part = pick(half, (self.spot + step) % self.line).astype(wire)
+            total = total + self.turn(part, step).astype(F32)
+        return total
 
     def gather_small(self, array):
         if not self.quick:
@@ -209,6 +197,16 @@
                 high, jnp.concatenate([other, array]), jnp.concatenate([array, other])
             )
         return array
+
+    def gather_direct(self, array):
+        if not self.quick:
+            return self.gather_whole(array)
+        came = [array]
+        for step in range(1, self.count):
+            pairs = [(n, (n + step) % self.count) for n in range(self.count)]
+            came.append(lax.ppermute(array, "dp", pairs))
+        turned = jnp.stack((came + came)[::-1])
+        return lax.dynamic_slice_in_dim(turned, self.count - 1 - self.place, self.count, 0)
 
     def sum_small(self, blocks):
         if not self.quick:
@@ -396,6 +394,33 @@
     return [pltpu.VMEM((4, near[0].shape[0], STEP), BF)]
 
 
+def place_kernel(place_ref, *refs):
+    blocks, out_ref, sems = refs[:8], refs[8], refs[9]
+    spot, side = place_ref[0] // 2, place_ref[0] % 2
+    copies = []
+    for n, ref in enumerate(blocks):
+        line = (spot + 4 - n % 4) % 4
+        at = line * 2 + (side if n < 4 else 1 - side)
+        copies.append(pltpu.make_async_copy(ref, out_ref.at[at], sems.at[n]))
+    for copy in copies:
+        copy.start()
+    for copy in copies:
+        copy.wait()
+
+
+def place_blocks(place, blocks):
+    block = blocks[0]
+    return pl.pallas_call(
+        place_kernel,
+        out_shape=shaped((len(blocks),) + block.shape, block.dtype),
+        in_specs=[pl.BlockSpec(memory_space=pltpu.SMEM)]
+        + [pl.BlockSpec(memory_space=pl.ANY)] * len(blocks),
+        out_specs=pl.BlockSpec(memory_space=pl.ANY),
+        scratch_shapes=[pltpu.SemaphoreType.DMA((len(blocks),))],
+        compiler_params=pltpu.CompilerParams(vmem_limit_bytes=8 * 1024 * 1024),
+    )(place, *blocks)
+
+
 def join_kernel(upward, me_ref, x0, x1, x2, x3, w_ref, full_ref, out_ref, parts):
     whole = joined(me_ref, (x0, x1, x2, x3), parts)
     full_ref[...] = whole
@@ -767,10 +792,10 @@
 def attend_tables(length, repeat, gains):
     heads = HEADS // 4
     row_angle, col_angle = angle_tables(length)
-    angle = jnp.concatenate([row_angle, row_angle, col_angle, col_angle], -1)
-    angle = jnp.tile(angle, (repeat, heads))
+    angle = np.concatenate([row_angle, row_angle, col_angle, col_angle], -1)
+    angle = np.tile(angle, (repeat, heads))
     spread = jnp.tile(gains, (1, heads))
-    return jnp.cos(angle), jnp.sin(angle), spread
+    return jnp.asarray(np.cos(angle), F32), jnp.asarray(np.sin(angle), F32), spread
 
 
 def attend_matrices():
@@ -786,10 +811,8 @@
     return low
 
 
-def halves_dot(value, matrix):
-    high = value.astype(BF)
-    rest = (value - high.astype(F32)).astype(BF)
-    return dot(high, matrix) + dot(rest, matrix)
+def low_dot(value, matrix):
+    return dot(value.astype(BF), matrix)
 
 
 def head_masks(width):
@@ -801,10 +824,10 @@
 
 
 def ready_heads(value, gain, cosine, sine, same, turn):
-    inverse = lax.rsqrt(halves_dot(value * value, same) * (1.0 / HEAD) + EPS)
+    inverse = lax.rsqrt(low_dot(value * value, same) * (1.0 / HEAD) + EPS)
     normed = value * inverse
     scaled = normed * gain
-    turned = scaled * cosine + halves_dot(scaled, turn) * sine
+    turned = scaled * cosine + low_dot(scaled, turn) * sine
     return turned.astype(BF), normed, inverse
 
 
@@ -903,10 +926,10 @@
         ((gq_ref, q_norm, q_inv), (gk_ref, k_norm, k_inv))
     ):
         turned = g_ref[...] * HEAD ** (-0.5)
-        scaled = turned * cosine + halves_dot(turned * sine, back)
+        scaled = turned * cosine + low_dot(turned * sine, back)
         dg_ref[n : n + 1] += jnp.sum(scaled * normed, 0, keepdims=True)
         weighed = scaled * gain_ref[n : n + 1]
-        mean = halves_dot(weighed * normed, same) * (1.0 / HEAD)
+        mean = low_dot(weighed * normed, same) * (1.0 / HEAD)
         out = inverse * (weighed - normed * mean)
         dp_ref[:, n * width : (n + 1) * width] = out.astype(BF)
     dp_ref[:, 2 * width :] = gv_ref[...].astype(BF)
@@ -1004,6 +1027,11 @@
     def token_blocks(value):
         return value.reshape(noise_count, own_rows, width)
 
+    facts = jnp.concatenate([class_label, time_index[0]])
+    facts = jnp.stack(noise.gather(facts))
+    times = (facts[:, own_images:].astype(F32) + 0.5) / NT
+    labels = groups.gather_small(facts[:, :own_images].reshape(-1)).reshape(-1)
+
     me = noise.me.reshape(1)
     unit = encoder_gate.shape[1]
     chunk_rows = encoder_attend.shape[0]
@@ -1036,8 +1064,6 @@
         clean_tokens,
         noise_tokens,
         velocity_cotangent,
-        time_index,
-        class_label,
         decoder_attend,
         decoder_gate,
     ) = lax.optimization_barrier(
@@ -1049,21 +1075,36 @@
             clean_tokens,
             noise_tokens,
             velocity_cotangent,
-            time_index,
-            class_label,
             decoder_attend,
             decoder_gate,
         )
     )
-    e_first = groups.gather(
+    e_first, early = groups.gather(
         jnp.concatenate([e_att_s.reshape(chunk_rows, -1), encoder_merge], -1)
     )
+    labels, early = lax.optimization_barrier((labels, early))
+
+    here = class_table.shape[1]
+    onehot = (
+        labels[:, None] == (jnp.arange(here) + noise.me * here)[None, :]
+    ).astype(BF)
+    class_cond = noise.total(dot_nt(onehot, class_table))
+    class_low = jax.nn.silu(class_cond).astype(BF)
+    class_mod = dot(class_low, encoder_modulate)
+    class_mod = groups.sum_small(
+        class_mod.reshape(groups_count, images, class_mod.shape[1])
+    )
+    class_mod = jnp.concatenate(noise.gather(class_mod), -1)
+
     e_att = flat(e_first[:, :, : 3 * quarter])
     e_merge = flat(e_first[:, :, 3 * quarter :])
-    e_second = groups.gather(jnp.concatenate([e_gate_s, e_lift_s], -1))
-    e_gate = flat(e_second[:, :, :unit])
-    e_lift = flat(e_second[:, :, unit:])
-    e_lower = flat(groups.gather(e_lower_s))
+    e_second_s, _, _ = lax.optimization_barrier(
+        (jnp.concatenate([e_gate_s, e_lift_s], -1), early, class_low)
+    )
+    e_pair, later = groups.gather(e_second_s)
+    e_units = flat(e_pair)
+    e_lower_s, _, class_mod = lax.optimization_barrier((e_lower_s, later, class_mod))
+    e_lower = flat(groups.gather(e_lower_s)[0])
     if groups.quick:
         d_att_s, d_gate_s, d_lift_s, d_lower_s, d_mod_s = trade(
             noise,
@@ -1102,34 +1143,12 @@
     d_second_s = jnp.concatenate(
         [jnp.concatenate([d_gate_s, d_lift_s], -1), pad_lower(d_lower_s)]
     )
-    d_first_s, _ = lax.optimization_barrier((d_first_s, e_second))
+    d_first_s, _, _, _ = lax.optimization_barrier((d_first_s, e_first, e_units, e_lower))
     d_whole = flat(groups.gather_whole(d_first_s))
-    d_second_s, d_whole = lax.optimization_barrier((d_second_s, d_whole))
-    d_pair = groups.gather_whole(d_second_s)
     d_mod, d_att, d_merge, d_time = [
         d_whole[:, first * quarter : last * quarter]
         for first, last in ((0, 6), (6, 9), (9, 10), (10, 11))
     ]
-    d_units = flat(d_pair[:, :chunk_rows])
-    d_lower = flat(d_pair[:, chunk_rows:, :width])
-
-    facts = jnp.concatenate([class_label, time_index[0]])
-    facts = jnp.stack(noise.gather(facts))
-    times = (facts[:, own_images:].astype(F32) + 0.5) / NT
-    labels = groups.gather_small(facts[:, :own_images].reshape(-1)).reshape(-1)
-
-    here = class_table.shape[1]
-    onehot = (
-        labels[:, None] == (jnp.arange(here) + noise.me * here)[None, :]
-    ).astype(BF)
-    class_cond = noise.total(dot_nt(onehot, class_table))
-    class_low = jax.nn.silu(class_cond).astype(BF)
-    class_mod = dot(class_low, encoder_modulate)
-    class_mod = groups.sum_small(
-        class_mod.reshape(groups_count, images, class_mod.shape[1])
-    )
-    class_mod = jnp.concatenate(noise.gather(class_mod), -1)
-
     clean_group = jnp.concatenate(noise.gather(clean_tokens.reshape(own_rows, width)))
     clean_all = clean_group.astype(F32)
     own_times = (time_index[0].astype(F32) + 0.5) / NT
@@ -1162,6 +1181,10 @@
     e_one = (e_norm_one * (1.0 + e_piece[1]) + e_piece[0]).astype(BF)
     e_heads = dot(e_one, e_att)
     e_mixed = attend_forward(e_heads, encoder_gains, length)
+    e_mixed, d_second_s = lax.optimization_barrier((e_mixed, d_second_s))
+    d_pair = groups.gather_whole(d_second_s)
+    d_units = flat(d_pair[:, :chunk_rows])
+    d_lower = flat(d_pair[:, chunk_rows:, :width])
     e_mixed_all = jnp.concatenate(noise.gather(e_mixed), -1)
     e_merged = jnp.concatenate(
         noise.gather(dot(e_mixed_all, e_merge).astype(BF)), -1
@@ -1169,8 +1192,9 @@
     e_middle = clean_all + e_piece[2] * e_merged
     e_norm_two, e_inverse_two = norm_parts(e_middle)
     e_two = (e_norm_two * (1.0 + e_piece[4]) + e_piece[3]).astype(BF)
-    e_gate_act = dot(e_two, e_gate)
-    e_lift_act = dot(e_two, e_lift)
+    e_acts = dot(e_two, e_units)
+    e_gate_act = e_acts[:, :unit]
+    e_lift_act = e_acts[:, unit:]
     e_hidden = (jax.nn.silu(e_gate_act) * e_lift_act).astype(BF)
     e_lowered = noise.scatter_sum(token_blocks(dot(e_hidden, e_lower)))
 
@@ -1272,11 +1296,9 @@
     e_g_hidden = dot_nt(e_low_all, e_lower)
     e_g_gate_low = (e_g_hidden * e_lift_act * silu_slope(e_gate_act)).astype(BF)
     e_g_lift_low = (e_g_hidden * jax.nn.silu(e_gate_act)).astype(BF)
-    ew_gate = dot_tn(e_two, e_g_gate_low)
-    ew_lift = dot_tn(e_two, e_g_lift_low)
-    e_g_two = noise.scatter_sum(
-        token_blocks(dot_nt(e_g_gate_low, e_gate) + dot_nt(e_g_lift_low, e_lift))
-    )
+    e_g_acts = jnp.concatenate([e_g_gate_low, e_g_lift_low], -1)
+    ew_units = dot_tn(e_two, e_g_acts)
+    e_g_two = noise.scatter_sum(token_blocks(dot_nt(e_g_acts, e_units)))
     e_g_middle = g_latent + norm_back(
         e_g_two * (1.0 + piece[4]), norm_two_own, own_part(e_inverse_two)
     )
@@ -1308,8 +1330,13 @@
     every_mod = noise.exchange(
         jnp.moveaxis(e_g_mod.reshape(own_images, noise_count, -1), 1, 0)
     )
-    every_mod = groups.gather_small(jnp.concatenate(every_mod))
-    every_mod = every_mod.reshape(-1, every_mod.shape[-1])
+    every_mod = jnp.concatenate(every_mod)
+    gains = noise.total(jnp.stack([e_gain_grad, d_gain_grad]))
+    message = jnp.concatenate([every_mod.astype(F32).reshape(-1), gains.reshape(-1)])
+    message = groups.gather_direct(message)
+    every_mod, gain_total = message[:, : every_mod.size], message[:, every_mod.size :]
+    every_mod = every_mod.astype(BF).reshape(-1, encoder_modulate.shape[1])
+    gain_total = jnp.sum(gain_total, 0).reshape(gains.shape)
     grad_e_mod = dot_tn(class_low, every_mod)
     g_class = noise.total(dot_nt(every_mod, encoder_modulate)) * silu_slope(class_cond)
     grad_table = lax.dot_general(
@@ -1386,7 +1413,7 @@
     grad_time = d_first[:, 10 * quarter :]
     e_low_sum = groups.scatter_sum(by_group(ew_lower))
     e_second = groups.scatter_sum(
-        jnp.concatenate([by_group(ew_gate), by_group(ew_lift)], -1)
+        by_group(ew_units)
     )
     e_first = groups.scatter_sum(
         jnp.concatenate([by_group(part) for part in [ew_att, ew_merge]], -1)
@@ -1397,7 +1424,6 @@
         e_kinds,
     )
     grad_e_merge = e_first[:, 3 * quarter :]
-    gain_total = groups.total(noise.total(jnp.stack([e_gain_grad, d_gain_grad])))
     return (
         velocity,
         latent_low.reshape(own_images, length, width),

time: 1030 us -> 962 us (0.934)
  starting transfers between devices: 175 us -> 130 us
  other arithmetic: 118 us -> 99.2 us
  waiting for transfers between devices: 366 us -> 382 us
  local copies, waits for them, and re-layouts: 161 us -> 148 us
    ppermute x12 -> x6, waiting for transfers between devices: 78.4 us -> 31.1 us  [swap(): return lax.ppermute(array, 'dp', [(n, n ^ mask) for n in range(self.count)])]
    ppermute x39 -> x37, waiting for transfers between devices: 89.3 us -> 123 us  [the longest x18 114 us: turn(): return lax.ppermute(array, 'dp', pairs)]
    ppermute x39 -> x37, starting transfers between devices: 92.1 us -> 64.2 us  [the longest x18 44.6 us: turn(): return lax.ppermute(array, 'dp', pairs)]
    ppermute x102, waiting for transfers between devices: 166 us -> 191 us  [swap(): lax.ppermute(array, 'noise', [(n, n ^ mask) for n in range(self.count)])]
    ppermute x3, waiting for transfers between devices: 6.24 us -> 25.8 us  [scatter_sum(): half = keep + lax.ppermute(send, 'dp', self.across).astype(F32)]
    ppermute x12 -> x6, starting transfers between devices: 23.6 us -> 6.43 us  [swap(): return lax.ppermute(array, 'dp', [(n, n ^ mask) for n in range(self.count)])]
    all_gather x2, waiting for transfers between devices: 25.3 us -> 10.5 us  [gather_whole(): return lax.all_gather(array, 'dp', axis=0, tiled=False)]
    unnamed x445 -> x448, local copies, waits for them, and re-layouts: 62.6 us -> 50.6 us
  transfers between devices with their start and end apart: 160 -> 152, of which waited for: 62 -> 64; matrix products, arithmetic and copies ran while one was open for 26% -> 23% of each run, Pallas kernels for 15% -> 15%
where the time goes in v2:
time: 962 us; the launch traced here: 946 us
  waiting for transfers between devices  382 us (40%)
  local copies, waits for them, and re-layouts  148 us (15%)
  Pallas kernels  146 us (15%)
  starting transfers between devices  130 us (14%)
  other arithmetic  99.2 us (10%)
  matrix products  23.9 us (2%)
  between operations  18 us (2%)
    ppermute x102, waiting for transfers between devices, swap(): lax.ppermute(array, 'noise', [(n, n ^ mask) for n in range(self.count)])  191 us
    ppermute x18, waiting for transfers between devices, turn(): return lax.ppermute(array, 'dp', pairs)  114 us
    ppermute x102, starting transfers between devices, swap(): lax.ppermute(array, 'noise', [(n, n ^ mask) for n in range(self.count)])  56.3 us
    unnamed x448, local copies, waits for them, and re-layouts  50.6 us
    ppermute x18, starting transfers between devices, turn(): return lax.ppermute(array, 'dp', pairs)  44.6 us
    ppermute x6, waiting for transfers between devices, swap(): return lax.ppermute(array, 'dp', [(n, n ^ mask) for n in range(self.count)])  31.1 us
    pallas_call x2, Pallas kernels, attend_backward(): pl.pallas_call(functools.partial(attend_back_kernel, length, upward), out...  28.9 us
    ppermute x3, waiting for transfers between devices, scatter_sum(): half = keep + lax.ppermute(send, 'dp', self.across).astype(F32)  25.8 us
  transfers between devices with their start and end apart: 152, of which 64 were waited for; matrix products, arithmetic and copies ran while one was open for 23% of the time, Pallas kernels for 15%

profile of v2, /device:TPU:0, one launch (start us, length us, event | category | flops | bytes accessed | tf_op | source)
XLA Modules:
  0.0 945.9 jit_solution(13486938415983731483)
XLA Ops:
  36.5 7.9 collective-permute-done.13
  63.8 14.5 %collective-permute-done.19 = f32[4,4,1728]{2,1,0:T(4,128)} collective-permute-done((f32[4,4,1728]{2,1,0:T(4,128)S(1)}, f32[4,4,1728]{2,1,0:T(4,128)}, u32[]{:S(2)}, u32[]{:S(2)}) %collective-permute-start.19) | collective-permute-done | bytes 110624 | tf_op jit(solution)/shard_map/ppermute | solution.py:159
  91.5 8.1 collective-permute-done.32.refs_2_
  124.0 26.0 %collective-permute-done.41.refs_2_ = bf16[144,1536]{1,0:T(8,128)(2,1)S(1)} collective-permute-done((bf16[144,1536]{1,0:T(8,128)(2,1)S(1)}, bf16[144,1536]{1,0:T(8,128)(2,1)S(1)}, u32[]{:S(2)}, u32[]{:S(2)}) %collective-permute-start.41) | collective-permute-done | bytes 442400 | tf_op jit(solution)/shard_map/ppermute | solution.py:156
  152.9 8.0 collective-permute-done.47.refs_2_
  204.5 14.0 %collective-permute-done.6 = bf16[64,1152]{1,0:T(8,128)(2,1)S(1)} collective-permute-done((bf16[64,1152]{1,0:T(8,128)(2,1)S(1)}, bf16[64,1152]{1,0:T(8,128)(2,1)S(1)}, u32[]{:S(2)}, u32[]{:S(2)}) %collective-permute-start.6) | collective-permute-done | bytes 147488 | tf_op jit(solution)/shard_map/ppermute | solution.py:68
  247.4 6.6 collective-permute-done.37
  292.1 10.5 %all-gather.5.cloned.1.call-done = bf16[1152,3168]{1,0:T(8,128)(2,1)} async-done(((bf16[144,3168]{1,0:T(8,128)(2,1)}), bf16[1152,3168]{1,0:T(8,128)(2,1)}) %all-gather.5.cloned.1.call-update) | async-done | bytes 7299088 | tf_op jit(solution)/shard_map/all_gather | solution.py:162
  316.9 9.5 %shard_map.518 = f32[1728,1024]{1,0:T(8,128)} custom-call(bf16[1024,1152]{1,0:T(8,128)(2,1)S(1)} %fusion.5.x_ref, bf16[1152,1728]{1,0:T(8,128)(2,1)} %slice.371.w_ref.refs_6_), custom_call_target="tpu_custom_call" | custom-call | tf_op jit(solution)/shard_map/pallas_call | solution.py:635
  331.7 14.4 %collective-permute-done.65.x2 = bf16[288,1024]{1,0:T(8,128)(2,1)} collective-permute-done((bf16[288,1024]{1,0:T(8,128)(2,1)}, bf16[288,1024]{1,0:T(8,128)(2,1)}, u32[]{:S(2)}, u32[]{:S(2)}) %collective-permute-start.65) | collective-permute-done | bytes 589856 | tf_op jit(solution)/shard_map/ppermute | solution.py:68
  349.0 7.4 shard_map.519
  358.4 12.2 %shard_map.520.x0 = bf16[288,1024]{1,0:T(8,128)(2,1)S(1)} custom-call(f32[1024,864]{1,0:T(8,128)S(1)} %copy-done.2, f32[256,288]{1,0:T(8,128)S(1)} %copy-done.15, f32[256,288]{1,0:T(8,128)S(1)} %copy-done.17, f32[2,288]{1,0:T(2,128)S(1)} %tile.17.gain_ref, bf16[288,288]{1,0:T(8,128)(2,1)S(1)} %copy-done.27, bf16[288,288]{1,0:T(8,128)(2,1)S(1)} %copy-done.29), custom_call_target="tpu_custom_call" | custom-call | tf_op jit(solution)/shard_map/pallas_call | solution.py:955
  372.3 14.1 %collective-permute-done.68.x2 = bf16[288,1024]{1,0:T(8,128)(2,1)S(1)} collective-permute-done((bf16[288,1024]{1,0:T(8,128)(2,1)S(1)}, bf16[288,1024]{1,0:T(8,128)(2,1)S(1)}, u32[]{:S(2)}, u32[]{:S(2)}) %collective-permute-start.68) | collective-permute-done | bytes 589856 | tf_op jit(solution)/shard_map/ppermute | solution.py:68
  402.2 14.3 %collective-permute-done.74.x2 = bf16[288,1024]{1,0:T(8,128)(2,1)} collective-permute-done((bf16[288,1024]{1,0:T(8,128)(2,1)}, bf16[288,1024]{1,0:T(8,128)(2,1)}, u32[]{:S(2)}, u32[]{:S(2)}) %collective-permute-start.74) | collective-permute-done | bytes 589856 | tf_op jit(solution)/shard_map/ppermute | solution.py:68
  423.5 9.2 shard_map.522
  446.5 8.6 shard_map.525
  459.3 12.9 %collective-permute-done.77 = bf16[288,1024]{1,0:T(8,128)(2,1)S(1)} collective-permute-done((bf16[288,1024]{1,0:T(8,128)(2,1)S(1)}, bf16[288,1024]{1,0:T(8,128)(2,1)S(1)}, u32[]{:S(2)}, u32[]{:S(2)}) %collective-permute-start.77) | collective-permute-done | bytes 589856 | tf_op jit(solution)/shard_map/ppermute | solution.py:68
  472.2 12.0 %collective-permute-done.85 = bf16[288,1024]{1,0:T(8,128)(2,1)S(1)} collective-permute-done((bf16[288,1024]{1,0:T(8,128)(2,1)S(1)}, bf16[288,1024]{1,0:T(8,128)(2,1)S(1)}, u32[]{:S(2)}, u32[]{:S(2)}) %collective-permute-start.85) | collective-permute-done | bytes 589856 | tf_op jit(solution)/shard_map/ppermute | solution.py:68
  513.2 14.3 %collective-permute-done.89 = bf16[288,1024]{1,0:T(8,128)(2,1)S(1)} collective-permute-done((bf16[288,1024]{1,0:T(8,128)(2,1)S(1)}, bf16[288,1024]{1,0:T(8,128)(2,1)S(1)}, u32[]{:S(2)}, u32[]{:S(2)}) %collective-permute-start.89) | collective-permute-done | bytes 589856 | tf_op jit(solution)/shard_map/ppermute | solution.py:68
  527.8 23.6 %shard_map.527 = (bf16[1024,864]{1,0:T(8,128)(2,1)S(1)}, f32[2,288]{1,0:T(2,128)S(1)}) custom-call(f32[1024,864]{1,0:T(8,128)} %get-tuple-element.101.p_ref, f32[256,288]{1,0:T(8,128)S(1)} %copy-done.15, f32[256,288]{1,0:T(8,128)S(1)} %copy-done.18, f32[2,288]{1,0:T(2,128)S(1)} %tile.17.gain_ref, bf16[288,288]{1,0:T(8,128)(2,1)S(1)} %copy-done.27, ...), custom_call_target="tpu_custom_call" | custom-call | tf_op jit(solution)/shard_map/pallas_call | solution.py:972
  551.4 6.7 shard_map.528
  597.7 9.3 shard_map.529
  628.8 6.4 shard_map.533
  663.1 12.5 %concatenate.165 = bf16[8,144,3168]{2,1,0:T(8,128)(2,1)} concatenate(bf16[8,144,1728]{2,1,0:T(8,128)(2,1)} %bitcast.551, bf16[8,144,864]{2,1,0:T(8,128)(2,1)S(1)} %bitcast.526, bf16[8,144,288]{2,1,0:T(8,128)(2,1)} %bitcast.532, bf16[8,144,288]{2,1,0:T(8,128)(2,1)} %bitcast.570), dimensions={2} | concatenate | bytes 14598144 | tf_op jit(solution)/shard_map/concatenate | solution.py:1407
  703.1 9.1 collective-permute-done.131
  731.6 8.1 collective-permute-done.133
  739.8 23.4 %collective-permute-done.134 = bf16[96,1152]{1,0:T(8,128)(2,1)S(1)} collective-permute-done((bf16[96,1152]{1,0:T(8,128)(2,1)S(1)}, bf16[96,1152]{1,0:T(8,128)(2,1)S(1)}, u32[]{:S(2)}, u32[]{:S(2)}) %collective-permute-start.134) | collective-permute-done | bytes 221216 | tf_op jit(solution)/shard_map/ppermute | solution.py:156
  821.1 16.7 %collective-permute-done.123 = bf16[4,144,1152]{2,1,0:T(8,128)(2,1)} collective-permute-done((bf16[4,144,1152]{2,1,0:T(8,128)(2,1)}, bf16[4,144,1152]{2,1,0:T(8,128)(2,1)}, u32[]{:S(2)}, u32[]{:S(2)}) %collective-permute-start.123) | collective-permute-done | bytes 1327136 | tf_op jit(solution)/shard_map/ppermute | solution.py:182
  840.8 10.1 %collective-permute-start.125 = (bf16[144,1152]{1,0:T(8,128)(2,1)S(1)}, bf16[144,1152]{1,0:T(8,128)(2,1)S(1)}, u32[]{:S(2)}, u32[]{:S(2)}) collective-permute-start(bf16[144,1152]{1,0:T(8,128)(2,1)S(1)} %get-tuple-element.298), channel_id=1, source_target_pairs={{0,24},{4,28},{8,0},{12,4},{16,8},{20,12},{24,16},{28,20},{1,25},{... | collective-permute-start | bytes 995336 | tf_op jit(solution)/shard_map/ppermute | solution.py:156
  852.9 11.0 %collective-permute-start.126 = (bf16[144,1152]{1,0:T(8,128)(2,1)S(1)}, bf16[144,1152]{1,0:T(8,128)(2,1)S(1)}, u32[]{:S(2)}, u32[]{:S(2)}) collective-permute-start(bf16[144,1152]{1,0:T(8,128)(2,1)S(1)} %get-tuple-element.297), channel_id=1, source_target_pairs={{0,16},{4,20},{8,24},{12,28},{16,0},{20,4},{24,8},{28,12},{1,17},{... | collective-permute-start | bytes 995336 | tf_op jit(solution)/shard_map/ppermute | solution.py:156
  863.9 22.8 %collective-permute-done.130 = bf16[144,1536]{1,0:T(8,128)(2,1)S(1)} collective-permute-done((bf16[144,1536]{1,0:T(8,128)(2,1)S(1)}, bf16[144,1536]{1,0:T(8,128)(2,1)S(1)}, u32[]{:S(2)}, u32[]{:S(2)}) %collective-permute-start.130) | collective-permute-done | bytes 442400 | tf_op jit(solution)/shard_map/ppermute | solution.py:156
  886.9 13.8 %collective-permute-done.126 = bf16[144,1152]{1,0:T(8,128)(2,1)S(1)} collective-permute-done((bf16[144,1152]{1,0:T(8,128)(2,1)S(1)}, bf16[144,1152]{1,0:T(8,128)(2,1)S(1)}, u32[]{:S(2)}, u32[]{:S(2)}) %collective-permute-start.126) | collective-permute-done | bytes 331808 | tf_op jit(solution)/shard_map/ppermute | solution.py:156
  (1028 shorter events, 530.0 us)
Async XLA Ops:
  7.2 295.4 %all-gather.5.cloned.1.call-start = ((), (), s32[]{:S(2)}) async-start(), calls=%async_computation.4 | async-start | bytes 8294400 | tf_op jit(solution)/shard_map/all_gather | solution.py:162
  54.7 23.5 %collective-permute-start.19 = (f32[4,4,1728]{2,1,0:T(4,128)S(1)}, f32[4,4,1728]{2,1,0:T(4,128)}, u32[]{:S(2)}, u32[]{:S(2)}) collective-permute-start(f32[4,4,1728]{2,1,0:T(4,128)S(1)} %dynamic-slice_bitcast_fusion.2), channel_id=1, source_target_pairs={{0,16},{4,20},{8,24},{12,28},{16,0},{20,4},{24,8},{28,12},{1,17},{... | collective-permute-start | bytes 331784 | tf_op jit(solution)/shard_map/ppermute | solution.py:159
  57.6 29.0 %collective-permute-start.25 = (bf16[144,1152]{1,0:T(8,128)(2,1)S(1)}, bf16[144,1152]{1,0:T(8,128)(2,1)}, u32[]{:S(2)}, u32[]{:S(2)}) collective-permute-start(bf16[144,1152]{1,0:T(8,128)(2,1)S(1)} %pad_maximum_fusion.6.refs_0_), channel_id=1, source_target_pairs={{0,8},{4,12},{8,16},{12,20},{16,24},{20,28},{24,0},{28,4},{1,9},{5... | collective-permute-start | bytes 995336 | tf_op jit(solution)/shard_map/ppermute | solution.py:156
  58.8 28.3 %collective-permute-start.26 = (bf16[144,1152]{1,0:T(8,128)(2,1)S(1)}, bf16[144,1152]{1,0:T(8,128)(2,1)}, u32[]{:S(2)}, u32[]{:S(2)}) collective-permute-start(bf16[144,1152]{1,0:T(8,128)(2,1)S(1)} %pad_maximum_fusion.6.refs_0_), channel_id=1, source_target_pairs={{0,16},{4,20},{8,24},{12,28},{16,0},{20,4},{24,8},{28,12},{1,17},{... | collective-permute-start | bytes 995336 | tf_op jit(solution)/shard_map/ppermute | solution.py:156
  61.5 25.6 %collective-permute-start.27 = (bf16[144,1152]{1,0:T(8,128)(2,1)S(1)}, bf16[144,1152]{1,0:T(8,128)(2,1)S(1)}, u32[]{:S(2)}, u32[]{:S(2)}) collective-permute-start(bf16[144,1152]{1,0:T(8,128)(2,1)S(1)} %pad_maximum_fusion.6.refs_0_), channel_id=1, source_target_pairs={{0,4},{4,0},{8,12},{12,8},{16,20},{20,16},{24,28},{28,24},{1,5},{5... | collective-permute-start | bytes 995336 | tf_op jit(solution)/shard_map/ppermute | solution.py:173
  88.9 21.7 %collective-permute-start.18 = (bf16[144,1536]{1,0:T(8,128)(2,1)S(1)}, bf16[144,1536]{1,0:T(8,128)(2,1)}, u32[]{:S(2)}, u32[]{:S(2)}) collective-permute-start(bf16[144,1536]{1,0:T(8,128)(2,1)S(1)} %pad_maximum_fusion.5.refs_0_), channel_id=1, source_target_pairs={{0,24},{4,28},{8,0},{12,4},{16,8},{20,12},{24,16},{28,20},{1,25},{... | collective-permute-start | bytes 1327112 | tf_op jit(solution)/shard_map/ppermute | solution.py:156
  106.2 45.1 %collective-permute-start.29 = (bf16[144,1152]{1,0:T(8,128)(2,1)}, bf16[144,1152]{1,0:T(8,128)(2,1)}, u32[]{:S(2)}, u32[]{:S(2)}) collective-permute-start(bf16[144,1152]{1,0:T(8,128)(2,1)} %collective-permute-done.26.refs_2_), channel_id=1, source_target_pairs={{0,4},{4,0},{8,12},{12,8},{16,20},{20,16},{24,28},{28,24},{1,5},{5... | collective-permute-start | bytes 995336 | tf_op jit(solution)/shard_map/ppermute | solution.py:173
  109.2 40.8 %collective-permute-start.41 = (bf16[144,1536]{1,0:T(8,128)(2,1)S(1)}, bf16[144,1536]{1,0:T(8,128)(2,1)S(1)}, u32[]{:S(2)}, u32[]{:S(2)}) collective-permute-start(bf16[144,1536]{1,0:T(8,128)(2,1)S(1)} %pad_maximum_fusion.5.refs_0_), channel_id=1, source_target_pairs={{0,16},{4,20},{8,24},{12,28},{16,0},{20,4},{24,8},{28,12},{1,17},{... | collective-permute-start | bytes 1327112 | tf_op jit(solution)/shard_map/ppermute | solution.py:156
  110.5 40.8 %collective-permute-start.42 = (bf16[144,1536]{1,0:T(8,128)(2,1)S(1)}, bf16[144,1536]{1,0:T(8,128)(2,1)S(1)}, u32[]{:S(2)}, u32[]{:S(2)}) collective-permute-start(bf16[144,1536]{1,0:T(8,128)(2,1)S(1)} %pad_maximum_fusion.5.refs_0_), channel_id=1, source_target_pairs={{0,4},{4,0},{8,12},{12,8},{16,20},{20,16},{24,28},{28,24},{1,5},{5... | collective-permute-start | bytes 1327112 | tf_op jit(solution)/shard_map/ppermute | solution.py:173
  117.3 35.6 %collective-permute-start.46 = (bf16[96,1152]{1,0:T(8,128)(2,1)}, bf16[96,1152]{1,0:T(8,128)(2,1)}, u32[]{:S(2)}, u32[]{:S(2)}) collective-permute-start(bf16[96,1152]{1,0:T(8,128)(2,1)} %copy-done.80), channel_id=1, source_target_pairs={{0,8},{4,12},{8,16},{12,20},{16,24},{20,28},{24,0},{28,4},{1,9},{5... | collective-permute-start | bytes 663560 | tf_op jit(solution)/shard_map/ppermute | solution.py:156
  122.7 42.6 %collective-permute-start.43 = (bf16[144,1536]{1,0:T(8,128)(2,1)S(1)}, bf16[144,1536]{1,0:T(8,128)(2,1)S(1)}, u32[]{:S(2)}, u32[]{:S(2)}) collective-permute-start(bf16[144,1536]{1,0:T(8,128)(2,1)S(1)} %collective-permute-done.40.refs_1_), channel_id=1, source_target_pairs={{0,4},{4,0},{8,12},{12,8},{16,20},{20,16},{24,28},{28,24},{1,5},{5... | collective-permute-start | bytes 1327112 | tf_op jit(solution)/shard_map/ppermute | solution.py:173
  151.3 30.6 %collective-permute-start.45 = (bf16[144,1536]{1,0:T(8,128)(2,1)}, bf16[144,1536]{1,0:T(8,128)(2,1)}, u32[]{:S(2)}, u32[]{:S(2)}) collective-permute-start(bf16[144,1536]{1,0:T(8,128)(2,1)} %collective-permute-done.18.refs_3_), channel_id=1, source_target_pairs={{0,4},{4,0},{8,12},{12,8},{16,20},{20,16},{24,28},{28,24},{1,5},{5... | collective-permute-start | bytes 1327112 | tf_op jit(solution)/shard_map/ppermute | solution.py:173
  160.9 23.8 %collective-permute-start.49 = (bf16[96,1152]{1,0:T(8,128)(2,1)}, bf16[96,1152]{1,0:T(8,128)(2,1)}, u32[]{:S(2)}, u32[]{:S(2)}) collective-permute-start(bf16[96,1152]{1,0:T(8,128)(2,1)} %copy-done.80), channel_id=1, source_target_pairs={{0,4},{4,0},{8,12},{12,8},{16,20},{20,16},{24,28},{28,24},{1,5},{5... | collective-permute-start | bytes 663560 | tf_op jit(solution)/shard_map/ppermute | solution.py:173
  167.9 22.7 %collective-permute-start.52 = (bf16[96,1152]{1,0:T(8,128)(2,1)}, bf16[96,1152]{1,0:T(8,128)(2,1)}, u32[]{:S(2)}, u32[]{:S(2)}) collective-permute-start(bf16[96,1152]{1,0:T(8,128)(2,1)} %collective-permute-done.48.refs_3_), channel_id=1, source_target_pairs={{0,4},{4,0},{8,12},{12,8},{16,20},{20,16},{24,28},{28,24},{1,5},{5... | collective-permute-start | bytes 663560 | tf_op jit(solution)/shard_map/ppermute | solution.py:173
  193.7 224.1 %all-gather.7.cloned.1.call-start = ((), (), s32[]{:S(2)}) async-start(), calls=%async_computation.5 | async-start | bytes 6635520 | tf_op jit(solution)/shard_map/all_gather | solution.py:162
  272.5 631.3 %reduce-scatter.5.cloned.1.call-start = ((), (), s32[]{:S(2)}) async-start(), calls=%async_computation.3 | async-start | bytes 6635520 | tf_op jit(solution)/shard_map/reduce_scatter | solution.py:165
  458.6 25.6 %collective-permute-start.85 = (bf16[288,1024]{1,0:T(8,128)(2,1)S(1)}, bf16[288,1024]{1,0:T(8,128)(2,1)S(1)}, u32[]{:S(2)}, u32[]{:S(2)}) collective-permute-start(bf16[288,1024]{1,0:T(8,128)(2,1)S(1)} %fusion.37), channel_id=1, source_target_pairs={{0,2},{1,3},{2,0},{3,1},{4,6},{5,7},{6,4},{7,5},{8,10},{9,11},{10,... | collective-permute-start | bytes 1769480 | tf_op jit(solution)/shard_map/ppermute | solution.py:68
  509.5 397.3 %reduce-scatter.3.cloned.1.call-start = ((), (), s32[]{:S(2)}) async-start(), calls=%async_computation.2 | async-start | bytes 8294400 | tf_op jit(solution)/shard_map/reduce_scatter | solution.py:165
  619.2 26.3 %collective-permute-start.140 = (f32[2,16,288]{2,0,1:T(2,128)}, f32[2,16,288]{2,0,1:T(2,128)}, u32[]{:S(2)}, u32[]{:S(2)}) collective-permute-start(f32[2,16,288]{2,0,1:T(2,128)} %bitcast.522), channel_id=1, source_target_pairs={{0,1},{1,0},{2,3},{3,2},{4,5},{5,4},{6,7},{7,6},{8,9},{9,8},{10,11... | collective-permute-start | bytes 110600 | tf_op jit(solution)/shard_map/ppermute | solution.py:68
  680.5 31.7 %collective-permute-start.131 = (bf16[4,96,1152]{2,1,0:T(8,128)(2,1)}, bf16[4,96,1152]{2,1,0:T(8,128)(2,1)}, u32[]{:S(2)}, u32[]{:S(2)}) collective-permute-start(bf16[4,96,1152]{2,1,0:T(8,128)(2,1)} %dynamic-slice_bitcast_fusion.1), channel_id=1, source_target_pairs={{0,4},{4,0},{8,12},{12,8},{16,20},{20,16},{24,28},{28,24},{1,5},{5... | collective-permute-start | bytes 2654216 | tf_op jit(solution)/shard_map/ppermute | solution.py:182
  695.2 117.2 %collective-permute-start.127 = (bf16[4,144,1536]{2,1,0:T(8,128)(2,1)}, bf16[4,144,1536]{2,1,0:T(8,128)(2,1)}, u32[]{:S(2)}, u32[]{:S(2)}) collective-permute-start(bf16[4,144,1536]{2,1,0:T(8,128)(2,1)} %dynamic-slice_bitcast_fusion), channel_id=1, source_target_pairs={{0,4},{4,0},{8,12},{12,8},{16,20},{20,16},{24,28},{28,24},{1,5},{5... | collective-permute-start | bytes 5308424 | tf_op jit(solution)/shard_map/ppermute | solution.py:182
  718.0 21.8 %collective-permute-start.133 = (bf16[96,1152]{1,0:T(8,128)(2,1)S(1)}, bf16[96,1152]{1,0:T(8,128)(2,1)S(1)}, u32[]{:S(2)}, u32[]{:S(2)}) collective-permute-start(bf16[96,1152]{1,0:T(8,128)(2,1)S(1)} %get-tuple-element.306), channel_id=1, source_target_pairs={{0,24},{4,28},{8,0},{12,4},{16,8},{20,12},{24,16},{28,20},{1,25},{... | collective-permute-start | bytes 663560 | tf_op jit(solution)/shard_map/ppermute | solution.py:156
  720.8 42.3 %collective-permute-start.134 = (bf16[96,1152]{1,0:T(8,128)(2,1)S(1)}, bf16[96,1152]{1,0:T(8,128)(2,1)S(1)}, u32[]{:S(2)}, u32[]{:S(2)}) collective-permute-start(bf16[96,1152]{1,0:T(8,128)(2,1)S(1)} %get-tuple-element.305), channel_id=1, source_target_pairs={{0,16},{4,20},{8,24},{12,28},{16,0},{20,4},{24,8},{28,12},{1,17},{... | collective-permute-start | bytes 663560 | tf_op jit(solution)/shard_map/ppermute | solution.py:156
  728.9 34.6 %collective-permute-start.104 = (bf16[2,64,1152]{2,1,0:T(8,128)(2,1)}, bf16[2,64,1152]{2,1,0:T(8,128)(2,1)}, u32[]{:S(2)}, u32[]{:S(2)}) collective-permute-start(bf16[2,64,1152]{2,1,0:T(8,128)(2,1)} %fusion.54), channel_id=1, source_target_pairs={{0,1},{1,0},{2,3},{3,2},{4,5},{5,4},{6,7},{7,6},{8,9},{9,8},{10,11... | collective-permute-start | bytes 884744 | tf_op jit(solution)/shard_map/ppermute | solution.py:68
  798.3 39.4 %collective-permute-start.123 = (bf16[4,144,1152]{2,1,0:T(8,128)(2,1)}, bf16[4,144,1152]{2,1,0:T(8,128)(2,1)}, u32[]{:S(2)}, u32[]{:S(2)}) collective-permute-start(bf16[4,144,1152]{2,1,0:T(8,128)(2,1)} %fusion.11), channel_id=1, source_target_pairs={{0,4},{4,0},{8,12},{12,8},{16,20},{20,16},{24,28},{28,24},{1,5},{5... | collective-permute-start | bytes 3981320 | tf_op jit(solution)/shard_map/ppermute | solution.py:182
  810.9 100.0 %collective-permute-start.139 = (f32[32,144]{1,0:T(8,128)S(1)}, f32[32,144]{1,0:T(8,128)S(1)}, u32[]{:S(2)}, u32[]{:S(2)}) collective-permute-start(f32[32,144]{1,0:T(8,128)S(1)} %add.751), channel_id=1, source_target_pairs={{0,2},{1,3},{2,0},{3,1},{4,6},{5,7},{6,4},{7,5},{8,10},{9,11},{10,... | collective-permute-start | bytes 55304 | tf_op jit(solution)/shard_map/ppermute | solution.py:68
  815.0 25.8 %collective-permute-start.128 = (bf16[144,1536]{1,0:T(8,128)(2,1)S(1)}, bf16[144,1536]{1,0:T(8,128)(2,1)S(1)}, u32[]{:S(2)}, u32[]{:S(2)}) collective-permute-start(bf16[144,1536]{1,0:T(8,128)(2,1)S(1)} %get-tuple-element.290), channel_id=1, source_target_pairs={{0,8},{4,12},{8,16},{12,20},{16,24},{20,28},{24,0},{28,4},{1,9},{5... | collective-permute-start | bytes 1327112 | tf_op jit(solution)/shard_map/ppermute | solution.py:156
  817.4 35.5 %collective-permute-start.129 = (bf16[144,1536]{1,0:T(8,128)(2,1)S(1)}, bf16[144,1536]{1,0:T(8,128)(2,1)S(1)}, u32[]{:S(2)}, u32[]{:S(2)}) collective-permute-start(bf16[144,1536]{1,0:T(8,128)(2,1)S(1)} %get-tuple-element.292), channel_id=1, source_target_pairs={{0,24},{4,28},{8,0},{12,4},{16,8},{20,12},{24,16},{28,20},{1,25},{... | collective-permute-start | bytes 1327112 | tf_op jit(solution)/shard_map/ppermute | solution.py:156
  819.1 67.5 %collective-permute-start.130 = (bf16[144,1536]{1,0:T(8,128)(2,1)S(1)}, bf16[144,1536]{1,0:T(8,128)(2,1)S(1)}, u32[]{:S(2)}, u32[]{:S(2)}) collective-permute-start(bf16[144,1536]{1,0:T(8,128)(2,1)S(1)} %get-tuple-element.291), channel_id=1, source_target_pairs={{0,16},{4,20},{8,24},{12,28},{16,0},{20,4},{24,8},{28,12},{1,17},{... | collective-permute-start | bytes 1327112 | tf_op jit(solution)/shard_map/ppermute | solution.py:156
  839.6 47.3 %collective-permute-start.124 = (bf16[144,1152]{1,0:T(8,128)(2,1)S(1)}, bf16[144,1152]{1,0:T(8,128)(2,1)S(1)}, u32[]{:S(2)}, u32[]{:S(2)}) collective-permute-start(bf16[144,1152]{1,0:T(8,128)(2,1)S(1)} %get-tuple-element.296), channel_id=1, source_target_pairs={{0,8},{4,12},{8,16},{12,20},{16,24},{20,28},{24,0},{28,4},{1,9},{5... | collective-permute-start | bytes 995336 | tf_op jit(solution)/shard_map/ppermute | solution.py:156
  840.8 46.1 %collective-permute-start.125 = (bf16[144,1152]{1,0:T(8,128)(2,1)S(1)}, bf16[144,1152]{1,0:T(8,128)(2,1)S(1)}, u32[]{:S(2)}, u32[]{:S(2)}) collective-permute-start(bf16[144,1152]{1,0:T(8,128)(2,1)S(1)} %get-tuple-element.298), channel_id=1, source_target_pairs={{0,24},{4,28},{8,0},{12,4},{16,8},{20,12},{24,16},{28,20},{1,25},{... | collective-permute-start | bytes 995336 | tf_op jit(solution)/shard_map/ppermute | solution.py:156
  852.9 47.8 %collective-permute-start.126 = (bf16[144,1152]{1,0:T(8,128)(2,1)S(1)}, bf16[144,1152]{1,0:T(8,128)(2,1)S(1)}, u32[]{:S(2)}, u32[]{:S(2)}) collective-permute-start(bf16[144,1152]{1,0:T(8,128)(2,1)S(1)} %get-tuple-element.297), channel_id=1, source_target_pairs={{0,16},{4,20},{8,24},{12,28},{16,0},{20,4},{24,8},{28,12},{1,17},{... | collective-permute-start | bytes 995336 | tf_op jit(solution)/shard_map/ppermute | solution.py:156
  (338 other events, 2901.5 us)
Sparse Core Ops, SparseCore 0:
  193.9 108.7 all-gather.4
  304.8 92.4 all-gather.6
  509.6 110.4 reduce-scatter.4
  675.8 176.9 reduce-scatter.2

commit v3 on v2

--- a/solution.py
+++ b/solution.py
@@ -446,10 +446,23 @@
     )(me, *near, weight)
 
 
+def rows_spec(weight, depth):
+    if weight.ndim == 2:
+        return full_spec(weight.shape)
+    count = weight.shape[0]
+    return pl.BlockSpec((count, depth // count, weight.shape[2]), lambda n, *_: (0, 0, 0))
+
+
+def rows_part(ref, n, parts):
+    size = ref.shape[0] // parts
+    part = ref[n * size : (n + 1) * size]
+    return part.reshape(-1, part.shape[-1])
+
+
 def units_kernel(me_ref, x0, x1, x2, x3, w_ref, full_ref, out_ref, hid_ref, parts):
     whole = joined(me_ref, (x0, x1, x2, x3), parts)
     full_ref[...] = whole
-    acts = dot_tn(whole, w_ref[...])
+    acts = dot_tn(whole, rows_part(w_ref, 0, 1))
     out_ref[...] = acts
     unit = hid_ref.shape[1]
     hid_ref[...] = (jax.nn.silu(acts[:, :unit]) * acts[:, unit:]).astype(BF)
@@ -457,11 +470,11 @@
 
 def units_dot(me, near, weight):
     quarter, rows = near[0].shape
-    width = weight.shape[1]
+    width = weight.shape[-1]
     return kernel_call(
         units_kernel,
         (rows // STEP,),
-        [up_spec(quarter)] * 4 + [full_spec(weight.shape)],
+        [up_spec(quarter)] * 4 + [rows_spec(weight, 4 * quarter)],
         [
             (shaped((4 * quarter, rows), BF), up_spec(4 * quarter)),
             (shaped((rows, width), F32), row_spec(width)),
@@ -577,18 +590,17 @@
     acts_ref[:, unit:] = (grad * (gate_act * gate)).astype(BF)
     value = acts_ref[...]
     for n in range(4):
-        term = dot_nt(w_ref[n * quarter : (n + 1) * quarter], value)
+        term = dot_nt(rows_part(w_ref, n, 4), value)
         parts[me_ref[0] ^ n] = term.astype(BF)
     give(parts, keep_ref, send_ref)
 
 
-def acts_back(me, grad, acts, weight):
+def acts_back(me, grad, acts, weight, quarter):
     rows, unit = grad.shape
-    quarter = weight.shape[0] // 4
     return kernel_call(
         acts_back_kernel,
         (rows // STEP,),
-        [row_spec(unit), row_spec(2 * unit), full_spec(weight.shape)],
+        [row_spec(unit), row_spec(2 * unit), rows_spec(weight, 4 * quarter)],
         [(shaped((rows, 2 * unit), BF), row_spec(2 * unit))] + give_outs(rows, quarter),
         [pltpu.VMEM((4, quarter, STEP), BF)],
     )(me, grad, acts, weight)
@@ -626,16 +638,19 @@
 
 
 def mod_kernel(x_ref, w_ref, out_ref):
-    out_ref[...] = dot(x_ref[...], w_ref[...]).T
-
-
-def mod_dot(value, weight):
+    out_ref[...] = dot(x_ref[...], w_ref[...]).T[: out_ref.shape[0]]
+
+
+def mod_spec(depth, wide):
+    return pl.BlockSpec((depth, -(-wide // 128) * 128), lambda n, *_: (0, 0))
+
+
+def mod_dot(value, weight, wide):
     rows, width = value.shape
-    wide = weight.shape[1]
     return kernel_call(
         mod_kernel,
         (rows // STEP,),
-        [row_spec(width), full_spec(weight.shape)],
+        [row_spec(width), mod_spec(width, wide)],
         [(shaped((wide, rows), F32), up_spec(wide))],
         scalars=0,
     )(value, weight)[0]
@@ -645,18 +660,19 @@
     parts, (w_ref, cat_ref, out_ref) = refs[:6], refs[6:]
     grad = jnp.concatenate([ref[...] for ref in parts]).T
     cat_ref[...] = grad
-    out_ref[...] = dot_nt(grad, w_ref[...])
+    out_ref[...] = dot_nt(grad, w_ref[:, : grad.shape[1]])
 
 
 def mod_back(parts, weight):
     quarter, rows = parts[0].shape
+    width = weight.shape[0]
     return kernel_call(
         mod_back_kernel,
         (rows // STEP,),
-        [up_spec(quarter)] * 6 + [full_spec(weight.shape)],
+        [up_spec(quarter)] * 6 + [mod_spec(width, 6 * quarter)],
         [
             (shaped((rows, 6 * quarter), BF), row_spec(6 * quarter)),
-            (shaped((rows, weight.shape[0]), F32), row_spec(weight.shape[0])),
+            (shaped((rows, width), F32), row_spec(width)),
         ],
         scalars=0,
     )(*parts, weight)
@@ -1129,6 +1145,7 @@
     d_first_s = jnp.concatenate(
         [
             d_mod_s.reshape(chunk_rows, -1),
+            jnp.zeros((chunk_rows, -6 * quarter % 128), BF),
             d_att_s.reshape(chunk_rows, -1),
             decoder_merge,
             time_weight,
@@ -1145,9 +1162,10 @@
     )
     d_first_s, _, _, _ = lax.optimization_barrier((d_first_s, e_first, e_units, e_lower))
     d_whole = flat(groups.gather_whole(d_first_s))
-    d_mod, d_att, d_merge, d_time = [
-        d_whole[:, first * quarter : last * quarter]
-        for first, last in ((0, 6), (6, 9), (9, 10), (10, 11))
+    after = -(-6 * quarter // 128) * 128
+    d_att, d_merge, d_time = [
+        d_whole[:, after + first * quarter : after + last * quarter]
+        for first, last in ((0, 3), (3, 4), (4, 5))
     ]
     clean_group = jnp.concatenate(noise.gather(clean_tokens.reshape(own_rows, width)))
     clean_all = clean_group.astype(F32)
@@ -1183,7 +1201,7 @@
     e_mixed = attend_forward(e_heads, encoder_gains, length)
     e_mixed, d_second_s = lax.optimization_barrier((e_mixed, d_second_s))
     d_pair = groups.gather_whole(d_second_s)
-    d_units = flat(d_pair[:, :chunk_rows])
+    d_units = d_pair if groups.quick else flat(d_pair[:, :chunk_rows])
     d_lower = flat(d_pair[:, chunk_rows:, :width])
     e_mixed_all = jnp.concatenate(noise.gather(e_mixed), -1)
     e_merged = jnp.concatenate(
@@ -1212,7 +1230,7 @@
         + temb.reshape(levels, images, 1, width)
     ).reshape(levels * rows, width)
     cond_low = jax.nn.silu(cond).astype(BF)
-    mod = mod_dot(cond_low, d_mod)
+    mod = mod_dot(cond_low, d_whole, 6 * quarter)
     shift_one, scale_one, gate_one, shift_two, scale_two, gate_two = [
         mod[n * quarter : (n + 1) * quarter] for n in range(6)
     ]
@@ -1250,7 +1268,7 @@
     low_cols = (cot_cols * gate_two).astype(BF)
     low_all, g_hidden = lower_back_dot(me, noise.near(low_cols), d_lower)
     g_gate_two = cot_cols * lowered
-    g_acts, *given = acts_back(me, g_hidden, acts, d_units)
+    g_acts, *given = acts_back(me, g_hidden, acts, d_units, quarter)
     g_two = noise.near_sum(*given)
     gw_lower = grad_dot(hidden, low_all, grad_low_kernel)
     gw_units = grad_dot(two_all, g_acts)
@@ -1272,7 +1290,7 @@
         g_two * norm_two,
         g_gate_two,
     )
-    g_mod, g_cond_low = mod_back([part.astype(BF) for part in g_parts], d_mod)
+    g_mod, g_cond_low = mod_back([part.astype(BF) for part in g_parts], d_whole)
     gw_mod = grad_dot(cond_low, g_mod, grad_low_kernel)
     g_cond = g_cond_low * silu_slope(cond)
     g_temb = noise.scatter_sum(

time: 962 us -> 957 us (level)
  waiting for transfers between devices: 382 us -> 395 us
  local copies, waits for them, and re-layouts: 148 us -> 138 us
  transfers between devices with their start and end apart: 152 -> 152, of which waited for: 64 -> 66; matrix products, arithmetic and copies ran while one was open for 23% -> 22% of each run, Pallas kernels for 15% -> 15%
where the time goes in v3:
time: 957 us; the launch traced here: 941 us
  waiting for transfers between devices  395 us (41%)
  Pallas kernels  145 us (15%)
  local copies, waits for them, and re-layouts  138 us (14%)
  starting transfers between devices  122 us (13%)
  other arithmetic  99.3 us (10%)
  matrix products  23.7 us (2%)
  between operations  18 us (2%)
    ppermute x102, waiting for transfers between devices, swap(): lax.ppermute(array, 'noise', [(n, n ^ mask) for n in range(self.count)])  192 us
    ppermute x18, waiting for transfers between devices, turn(): return lax.ppermute(array, 'dp', pairs)  122 us
    ppermute x102, starting transfers between devices, swap(): lax.ppermute(array, 'noise', [(n, n ^ mask) for n in range(self.count)])  56 us
    unnamed x448, local copies, waits for them, and re-layouts  50.6 us
    ppermute x18, starting transfers between devices, turn(): return lax.ppermute(array, 'dp', pairs)  36 us
    ppermute x6, waiting for transfers between devices, swap(): return lax.ppermute(array, 'dp', [(n, n ^ mask) for n in range(self.count)])  31.1 us
    pallas_call x2, Pallas kernels, attend_backward(): pl.pallas_call(functools.partial(attend_back_kernel, length, upward), out...  28.7 us
    ppermute x3, waiting for transfers between devices, scatter_sum(): half = keep + lax.ppermute(send, 'dp', self.across).astype(F32)  25.9 us
  transfers between devices with their start and end apart: 152, of which 66 were waited for; matrix products, arithmetic and copies ran while one was open for 22% of the time, Pallas kernels for 15%

profile of v3, /device:TPU:0, one launch (start us, length us, event | category | flops | bytes accessed | tf_op | source)
XLA Modules:
  0.0 941.3 jit_solution(14442978775669494088)
XLA Ops:
  36.5 7.9 collective-permute-done.13
  63.8 14.5 %collective-permute-done.19 = f32[4,4,1728]{2,1,0:T(4,128)} collective-permute-done((f32[4,4,1728]{2,1,0:T(4,128)S(1)}, f32[4,4,1728]{2,1,0:T(4,128)}, u32[]{:S(2)}, u32[]{:S(2)}) %collective-permute-start.19) | collective-permute-done | bytes 110624 | tf_op jit(solution)/shard_map/ppermute | solution.py:159
  91.5 8.1 collective-permute-done.32.refs_2_
  124.0 26.0 %collective-permute-done.41.refs_2_ = bf16[144,1536]{1,0:T(8,128)(2,1)S(1)} collective-permute-done((bf16[144,1536]{1,0:T(8,128)(2,1)S(1)}, bf16[144,1536]{1,0:T(8,128)(2,1)S(1)}, u32[]{:S(2)}, u32[]{:S(2)}) %collective-permute-start.41) | collective-permute-done | bytes 442400 | tf_op jit(solution)/shard_map/ppermute | solution.py:156
  152.9 8.0 collective-permute-done.47.refs_2_
  204.4 14.0 %collective-permute-done.6 = bf16[64,1152]{1,0:T(8,128)(2,1)S(1)} collective-permute-done((bf16[64,1152]{1,0:T(8,128)(2,1)S(1)}, bf16[64,1152]{1,0:T(8,128)(2,1)S(1)}, u32[]{:S(2)}, u32[]{:S(2)}) %collective-permute-start.6) | collective-permute-done | bytes 147488 | tf_op jit(solution)/shard_map/ppermute | solution.py:68
  247.4 6.6 collective-permute-done.37
  292.0 14.2 %all-gather.5.cloned.1.call-done.w_ref.refs_6_ = bf16[1152,3232]{1,0:T(8,128)(2,1)} async-done(((bf16[144,3232]{1,0:T(8,128)(2,1)}), bf16[1152,3232]{1,0:T(8,128)(2,1)}) %all-gather.5.cloned.1.call-update) | async-done | bytes 7446544 | tf_op jit(solution)/shard_map/all_gather | solution.py:162
  316.9 9.5 %shard_map.518 = f32[1728,1024]{1,0:T(8,128)} custom-call(bf16[1024,1152]{1,0:T(8,128)(2,1)S(1)} %fusion.5.x_ref, bf16[1152,3232]{1,0:T(8,128)(2,1)} %all-gather.5.cloned.1.call-done.w_ref.refs_6_), custom_call_target="tpu_custom_call" | custom-call | tf_op jit(solution)/shard_map/pallas_call | solution.py:650
  331.3 14.3 %collective-permute-done.65.x2 = bf16[288,1024]{1,0:T(8,128)(2,1)} collective-permute-done((bf16[288,1024]{1,0:T(8,128)(2,1)}, bf16[288,1024]{1,0:T(8,128)(2,1)}, u32[]{:S(2)}, u32[]{:S(2)}) %collective-permute-start.65) | collective-permute-done | bytes 589856 | tf_op jit(solution)/shard_map/ppermute | solution.py:68
  347.9 7.2 shard_map.519
  357.2 12.2 %shard_map.520.x0 = bf16[288,1024]{1,0:T(8,128)(2,1)S(1)} custom-call(f32[1024,864]{1,0:T(8,128)S(1)} %copy-done.2, f32[256,288]{1,0:T(8,128)S(1)} %copy-done.15, f32[256,288]{1,0:T(8,128)S(1)} %copy-done.17, f32[2,288]{1,0:T(2,128)S(1)} %tile.17.gain_ref, bf16[288,288]{1,0:T(8,128)(2,1)S(1)} %copy-done.27, bf16[288,288]{1,0:T(8,128)(2,1)S(1)} %copy-done.29), custom_call_target="tpu_custom_call" | custom-call | tf_op jit(solution)/shard_map/pallas_call | solution.py:971
  371.0 14.0 %collective-permute-done.68.x2 = bf16[288,1024]{1,0:T(8,128)(2,1)S(1)} collective-permute-done((bf16[288,1024]{1,0:T(8,128)(2,1)S(1)}, bf16[288,1024]{1,0:T(8,128)(2,1)S(1)}, u32[]{:S(2)}, u32[]{:S(2)}) %collective-permute-start.68) | collective-permute-done | bytes 589856 | tf_op jit(solution)/shard_map/ppermute | solution.py:68
  400.8 14.2 %collective-permute-done.74.x2 = bf16[288,1024]{1,0:T(8,128)(2,1)} collective-permute-done((bf16[288,1024]{1,0:T(8,128)(2,1)}, bf16[288,1024]{1,0:T(8,128)(2,1)}, u32[]{:S(2)}, u32[]{:S(2)}) %collective-permute-start.74) | collective-permute-done | bytes 589856 | tf_op jit(solution)/shard_map/ppermute | solution.py:68
  418.2 9.2 shard_map.522
  441.3 8.6 shard_map.525
  454.2 12.9 %collective-permute-done.77 = bf16[288,1024]{1,0:T(8,128)(2,1)S(1)} collective-permute-done((bf16[288,1024]{1,0:T(8,128)(2,1)S(1)}, bf16[288,1024]{1,0:T(8,128)(2,1)S(1)}, u32[]{:S(2)}, u32[]{:S(2)}) %collective-permute-start.77) | collective-permute-done | bytes 589856 | tf_op jit(solution)/shard_map/ppermute | solution.py:68
  467.1 12.0 %collective-permute-done.85 = bf16[288,1024]{1,0:T(8,128)(2,1)S(1)} collective-permute-done((bf16[288,1024]{1,0:T(8,128)(2,1)S(1)}, bf16[288,1024]{1,0:T(8,128)(2,1)S(1)}, u32[]{:S(2)}, u32[]{:S(2)}) %collective-permute-start.85) | collective-permute-done | bytes 589856 | tf_op jit(solution)/shard_map/ppermute | solution.py:68
  508.0 14.4 %collective-permute-done.89 = bf16[288,1024]{1,0:T(8,128)(2,1)S(1)} collective-permute-done((bf16[288,1024]{1,0:T(8,128)(2,1)S(1)}, bf16[288,1024]{1,0:T(8,128)(2,1)S(1)}, u32[]{:S(2)}, u32[]{:S(2)}) %collective-permute-start.89) | collective-permute-done | bytes 589856 | tf_op jit(solution)/shard_map/ppermute | solution.py:68
  522.6 23.3 %shard_map.527 = (bf16[1024,864]{1,0:T(8,128)(2,1)S(1)}, f32[2,288]{1,0:T(2,128)S(1)}) custom-call(f32[1024,864]{1,0:T(8,128)} %get-tuple-element.101.p_ref, f32[256,288]{1,0:T(8,128)S(1)} %copy-done.15, f32[256,288]{1,0:T(8,128)S(1)} %copy-done.18, f32[2,288]{1,0:T(2,128)S(1)} %tile.17.gain_ref, bf16[288,288]{1,0:T(8,128)(2,1)S(1)} %copy-done.27, ...), custom_call_target="tpu_custom_call" | custom-call | tf_op jit(solution)/shard_map/pallas_call | solution.py:988
  545.9 6.7 shard_map.528
  592.4 9.3 shard_map.529
  601.7 6.1 bitcast_reduce_fusion
  623.5 6.4 shard_map.533
  657.8 12.5 %concatenate.165 = bf16[8,144,3168]{2,1,0:T(8,128)(2,1)} concatenate(bf16[8,144,1728]{2,1,0:T(8,128)(2,1)} %bitcast.551, bf16[8,144,864]{2,1,0:T(8,128)(2,1)S(1)} %bitcast.525, bf16[8,144,288]{2,1,0:T(8,128)(2,1)} %bitcast.531, bf16[8,144,288]{2,1,0:T(8,128)(2,1)} %bitcast.568), dimensions={2} | concatenate | bytes 14598144 | tf_op jit(solution)/shard_map/concatenate | solution.py:1425
  697.7 9.4 %collective-permute-done.131 = bf16[4,96,1152]{2,1,0:T(8,128)(2,1)} collective-permute-done((bf16[4,96,1152]{2,1,0:T(8,128)(2,1)}, bf16[4,96,1152]{2,1,0:T(8,128)(2,1)}, u32[]{:S(2)}, u32[]{:S(2)}) %collective-permute-start.131) | collective-permute-done | bytes 884768 | tf_op jit(solution)/shard_map/ppermute | solution.py:182
  726.4 8.2 collective-permute-done.133
  734.7 22.7 %collective-permute-done.134 = bf16[96,1152]{1,0:T(8,128)(2,1)S(1)} collective-permute-done((bf16[96,1152]{1,0:T(8,128)(2,1)S(1)}, bf16[96,1152]{1,0:T(8,128)(2,1)S(1)}, u32[]{:S(2)}, u32[]{:S(2)}) %collective-permute-start.134) | collective-permute-done | bytes 221216 | tf_op jit(solution)/shard_map/ppermute | solution.py:156
  815.8 16.5 %collective-permute-done.123 = bf16[4,144,1152]{2,1,0:T(8,128)(2,1)} collective-permute-done((bf16[4,144,1152]{2,1,0:T(8,128)(2,1)}, bf16[4,144,1152]{2,1,0:T(8,128)(2,1)}, u32[]{:S(2)}, u32[]{:S(2)}) %collective-permute-start.123) | collective-permute-done | bytes 1327136 | tf_op jit(solution)/shard_map/ppermute | solution.py:182
  835.9 9.4 %collective-permute-start.125 = (bf16[144,1152]{1,0:T(8,128)(2,1)S(1)}, bf16[144,1152]{1,0:T(8,128)(2,1)S(1)}, u32[]{:S(2)}, u32[]{:S(2)}) collective-permute-start(bf16[144,1152]{1,0:T(8,128)(2,1)S(1)} %get-tuple-element.298), channel_id=1, source_target_pairs={{0,24},{4,28},{8,0},{12,4},{16,8},{20,12},{24,16},{28,20},{1,25},{... | collective-permute-start | bytes 995336 | tf_op jit(solution)/shard_map/ppermute | solution.py:156
  850.6 31.4 %collective-permute-done.130 = bf16[144,1536]{1,0:T(8,128)(2,1)S(1)} collective-permute-done((bf16[144,1536]{1,0:T(8,128)(2,1)S(1)}, bf16[144,1536]{1,0:T(8,128)(2,1)S(1)}, u32[]{:S(2)}, u32[]{:S(2)}) %collective-permute-start.130) | collective-permute-done | bytes 442400 | tf_op jit(solution)/shard_map/ppermute | solution.py:156
  882.3 13.9 %collective-permute-done.126 = bf16[144,1152]{1,0:T(8,128)(2,1)S(1)} collective-permute-done((bf16[144,1152]{1,0:T(8,128)(2,1)S(1)}, bf16[144,1152]{1,0:T(8,128)(2,1)S(1)}, u32[]{:S(2)}, u32[]{:S(2)}) %collective-permute-start.126) | collective-permute-done | bytes 331808 | tf_op jit(solution)/shard_map/ppermute | solution.py:156
  (1027 shorter events, 519.6 us)
Async XLA Ops:
  7.2 299.0 %all-gather.5.cloned.1.call-start = ((), (), s32[]{:S(2)}) async-start(), calls=%async_computation.4 | async-start | bytes 8626176 | tf_op jit(solution)/shard_map/all_gather | solution.py:162
  54.7 23.5 %collective-permute-start.19 = (f32[4,4,1728]{2,1,0:T(4,128)S(1)}, f32[4,4,1728]{2,1,0:T(4,128)}, u32[]{:S(2)}, u32[]{:S(2)}) collective-permute-start(f32[4,4,1728]{2,1,0:T(4,128)S(1)} %dynamic-slice_bitcast_fusion.2), channel_id=1, source_target_pairs={{0,16},{4,20},{8,24},{12,28},{16,0},{20,4},{24,8},{28,12},{1,17},{... | collective-permute-start | bytes 331784 | tf_op jit(solution)/shard_map/ppermute | solution.py:159
  57.6 29.0 %collective-permute-start.25 = (bf16[144,1152]{1,0:T(8,128)(2,1)S(1)}, bf16[144,1152]{1,0:T(8,128)(2,1)}, u32[]{:S(2)}, u32[]{:S(2)}) collective-permute-start(bf16[144,1152]{1,0:T(8,128)(2,1)S(1)} %pad_maximum_fusion.6.refs_0_), channel_id=1, source_target_pairs={{0,8},{4,12},{8,16},{12,20},{16,24},{20,28},{24,0},{28,4},{1,9},{5... | collective-permute-start | bytes 995336 | tf_op jit(solution)/shard_map/ppermute | solution.py:156
  58.8 28.3 %collective-permute-start.26 = (bf16[144,1152]{1,0:T(8,128)(2,1)S(1)}, bf16[144,1152]{1,0:T(8,128)(2,1)}, u32[]{:S(2)}, u32[]{:S(2)}) collective-permute-start(bf16[144,1152]{1,0:T(8,128)(2,1)S(1)} %pad_maximum_fusion.6.refs_0_), channel_id=1, source_target_pairs={{0,16},{4,20},{8,24},{12,28},{16,0},{20,4},{24,8},{28,12},{1,17},{... | collective-permute-start | bytes 995336 | tf_op jit(solution)/shard_map/ppermute | solution.py:156
  61.5 25.6 %collective-permute-start.27 = (bf16[144,1152]{1,0:T(8,128)(2,1)S(1)}, bf16[144,1152]{1,0:T(8,128)(2,1)S(1)}, u32[]{:S(2)}, u32[]{:S(2)}) collective-permute-start(bf16[144,1152]{1,0:T(8,128)(2,1)S(1)} %pad_maximum_fusion.6.refs_0_), channel_id=1, source_target_pairs={{0,4},{4,0},{8,12},{12,8},{16,20},{20,16},{24,28},{28,24},{1,5},{5... | collective-permute-start | bytes 995336 | tf_op jit(solution)/shard_map/ppermute | solution.py:173
  88.9 21.7 %collective-permute-start.18 = (bf16[144,1536]{1,0:T(8,128)(2,1)S(1)}, bf16[144,1536]{1,0:T(8,128)(2,1)}, u32[]{:S(2)}, u32[]{:S(2)}) collective-permute-start(bf16[144,1536]{1,0:T(8,128)(2,1)S(1)} %pad_maximum_fusion.5.refs_0_), channel_id=1, source_target_pairs={{0,24},{4,28},{8,0},{12,4},{16,8},{20,12},{24,16},{28,20},{1,25},{... | collective-permute-start | bytes 1327112 | tf_op jit(solution)/shard_map/ppermute | solution.py:156
  106.2 45.1 %collective-permute-start.29 = (bf16[144,1152]{1,0:T(8,128)(2,1)}, bf16[144,1152]{1,0:T(8,128)(2,1)}, u32[]{:S(2)}, u32[]{:S(2)}) collective-permute-start(bf16[144,1152]{1,0:T(8,128)(2,1)} %collective-permute-done.26.refs_2_), channel_id=1, source_target_pairs={{0,4},{4,0},{8,12},{12,8},{16,20},{20,16},{24,28},{28,24},{1,5},{5... | collective-permute-start | bytes 995336 | tf_op jit(solution)/shard_map/ppermute | solution.py:173
  109.2 40.8 %collective-permute-start.41 = (bf16[144,1536]{1,0:T(8,128)(2,1)S(1)}, bf16[144,1536]{1,0:T(8,128)(2,1)S(1)}, u32[]{:S(2)}, u32[]{:S(2)}) collective-permute-start(bf16[144,1536]{1,0:T(8,128)(2,1)S(1)} %pad_maximum_fusion.5.refs_0_), channel_id=1, source_target_pairs={{0,16},{4,20},{8,24},{12,28},{16,0},{20,4},{24,8},{28,12},{1,17},{... | collective-permute-start | bytes 1327112 | tf_op jit(solution)/shard_map/ppermute | solution.py:156
  110.5 40.8 %collective-permute-start.42 = (bf16[144,1536]{1,0:T(8,128)(2,1)S(1)}, bf16[144,1536]{1,0:T(8,128)(2,1)S(1)}, u32[]{:S(2)}, u32[]{:S(2)}) collective-permute-start(bf16[144,1536]{1,0:T(8,128)(2,1)S(1)} %pad_maximum_fusion.5.refs_0_), channel_id=1, source_target_pairs={{0,4},{4,0},{8,12},{12,8},{16,20},{20,16},{24,28},{28,24},{1,5},{5... | collective-permute-start | bytes 1327112 | tf_op jit(solution)/shard_map/ppermute | solution.py:173
  117.3 35.6 %collective-permute-start.46 = (bf16[96,1152]{1,0:T(8,128)(2,1)}, bf16[96,1152]{1,0:T(8,128)(2,1)}, u32[]{:S(2)}, u32[]{:S(2)}) collective-permute-start(bf16[96,1152]{1,0:T(8,128)(2,1)} %copy-done.80), channel_id=1, source_target_pairs={{0,8},{4,12},{8,16},{12,20},{16,24},{20,28},{24,0},{28,4},{1,9},{5... | collective-permute-start | bytes 663560 | tf_op jit(solution)/shard_map/ppermute | solution.py:156
  122.7 42.6 %collective-permute-start.43 = (bf16[144,1536]{1,0:T(8,128)(2,1)S(1)}, bf16[144,1536]{1,0:T(8,128)(2,1)S(1)}, u32[]{:S(2)}, u32[]{:S(2)}) collective-permute-start(bf16[144,1536]{1,0:T(8,128)(2,1)S(1)} %collective-permute-done.40.refs_1_), channel_id=1, source_target_pairs={{0,4},{4,0},{8,12},{12,8},{16,20},{20,16},{24,28},{28,24},{1,5},{5... | collective-permute-start | bytes 1327112 | tf_op jit(solution)/shard_map/ppermute | solution.py:173
  151.3 30.5 %collective-permute-start.45 = (bf16[144,1536]{1,0:T(8,128)(2,1)}, bf16[144,1536]{1,0:T(8,128)(2,1)}, u32[]{:S(2)}, u32[]{:S(2)}) collective-permute-start(bf16[144,1536]{1,0:T(8,128)(2,1)} %collective-permute-done.18.refs_3_), channel_id=1, source_target_pairs={{0,4},{4,0},{8,12},{12,8},{16,20},{20,16},{24,28},{28,24},{1,5},{5... | collective-permute-start | bytes 1327112 | tf_op jit(solution)/shard_map/ppermute | solution.py:173
  160.9 23.7 %collective-permute-start.49 = (bf16[96,1152]{1,0:T(8,128)(2,1)}, bf16[96,1152]{1,0:T(8,128)(2,1)}, u32[]{:S(2)}, u32[]{:S(2)}) collective-permute-start(bf16[96,1152]{1,0:T(8,128)(2,1)} %copy-done.80), channel_id=1, source_target_pairs={{0,4},{4,0},{8,12},{12,8},{16,20},{20,16},{24,28},{28,24},{1,5},{5... | collective-permute-start | bytes 663560 | tf_op jit(solution)/shard_map/ppermute | solution.py:173
  167.9 22.7 %collective-permute-start.52 = (bf16[96,1152]{1,0:T(8,128)(2,1)}, bf16[96,1152]{1,0:T(8,128)(2,1)}, u32[]{:S(2)}, u32[]{:S(2)}) collective-permute-start(bf16[96,1152]{1,0:T(8,128)(2,1)} %collective-permute-done.48.refs_3_), channel_id=1, source_target_pairs={{0,4},{4,0},{8,12},{12,8},{16,20},{20,16},{24,28},{28,24},{1,5},{5... | collective-permute-start | bytes 663560 | tf_op jit(solution)/shard_map/ppermute | solution.py:173
  193.7 222.9 %all-gather.7.cloned.1.call-start = ((), (), s32[]{:S(2)}) async-start(), calls=%async_computation.5 | async-start | bytes 6635520 | tf_op jit(solution)/shard_map/all_gather | solution.py:162
  272.4 626.8 %reduce-scatter.5.cloned.1.call-start = ((), (), s32[]{:S(2)}) async-start(), calls=%async_computation.3 | async-start | bytes 6635520 | tf_op jit(solution)/shard_map/reduce_scatter | solution.py:165
  453.4 25.6 %collective-permute-start.85 = (bf16[288,1024]{1,0:T(8,128)(2,1)S(1)}, bf16[288,1024]{1,0:T(8,128)(2,1)S(1)}, u32[]{:S(2)}, u32[]{:S(2)}) collective-permute-start(bf16[288,1024]{1,0:T(8,128)(2,1)S(1)} %fusion.37), channel_id=1, source_target_pairs={{0,2},{1,3},{2,0},{3,1},{4,6},{5,7},{6,4},{7,5},{8,10},{9,11},{10,... | collective-permute-start | bytes 1769480 | tf_op jit(solution)/shard_map/ppermute | solution.py:68
  504.3 398.0 %reduce-scatter.3.cloned.1.call-start = ((), (), s32[]{:S(2)}) async-start(), calls=%async_computation.2 | async-start | bytes 8294400 | tf_op jit(solution)/shard_map/reduce_scatter | solution.py:165
  614.0 26.3 %collective-permute-start.140 = (f32[2,16,288]{2,0,1:T(2,128)}, f32[2,16,288]{2,0,1:T(2,128)}, u32[]{:S(2)}, u32[]{:S(2)}) collective-permute-start(f32[2,16,288]{2,0,1:T(2,128)} %bitcast.521), channel_id=1, source_target_pairs={{0,1},{1,0},{2,3},{3,2},{4,5},{5,4},{6,7},{7,6},{8,9},{9,8},{10,11... | collective-permute-start | bytes 110600 | tf_op jit(solution)/shard_map/ppermute | solution.py:68
  675.3 31.9 %collective-permute-start.131 = (bf16[4,96,1152]{2,1,0:T(8,128)(2,1)}, bf16[4,96,1152]{2,1,0:T(8,128)(2,1)}, u32[]{:S(2)}, u32[]{:S(2)}) collective-permute-start(bf16[4,96,1152]{2,1,0:T(8,128)(2,1)} %dynamic-slice_bitcast_fusion.1), channel_id=1, source_target_pairs={{0,4},{4,0},{8,12},{12,8},{16,20},{20,16},{24,28},{28,24},{1,5},{5... | collective-permute-start | bytes 2654216 | tf_op jit(solution)/shard_map/ppermute | solution.py:182
  689.8 117.4 %collective-permute-start.127 = (bf16[4,144,1536]{2,1,0:T(8,128)(2,1)}, bf16[4,144,1536]{2,1,0:T(8,128)(2,1)}, u32[]{:S(2)}, u32[]{:S(2)}) collective-permute-start(bf16[4,144,1536]{2,1,0:T(8,128)(2,1)} %dynamic-slice_bitcast_fusion), channel_id=1, source_target_pairs={{0,4},{4,0},{8,12},{12,8},{16,20},{20,16},{24,28},{28,24},{1,5},{5... | collective-permute-start | bytes 5308424 | tf_op jit(solution)/shard_map/ppermute | solution.py:182
  712.9 21.8 %collective-permute-start.133 = (bf16[96,1152]{1,0:T(8,128)(2,1)S(1)}, bf16[96,1152]{1,0:T(8,128)(2,1)S(1)}, u32[]{:S(2)}, u32[]{:S(2)}) collective-permute-start(bf16[96,1152]{1,0:T(8,128)(2,1)S(1)} %get-tuple-element.306), channel_id=1, source_target_pairs={{0,24},{4,28},{8,0},{12,4},{16,8},{20,12},{24,16},{28,20},{1,25},{... | collective-permute-start | bytes 663560 | tf_op jit(solution)/shard_map/ppermute | solution.py:156
  715.6 41.8 %collective-permute-start.134 = (bf16[96,1152]{1,0:T(8,128)(2,1)S(1)}, bf16[96,1152]{1,0:T(8,128)(2,1)S(1)}, u32[]{:S(2)}, u32[]{:S(2)}) collective-permute-start(bf16[96,1152]{1,0:T(8,128)(2,1)S(1)} %get-tuple-element.305), channel_id=1, source_target_pairs={{0,16},{4,20},{8,24},{12,28},{16,0},{20,4},{24,8},{28,12},{1,17},{... | collective-permute-start | bytes 663560 | tf_op jit(solution)/shard_map/ppermute | solution.py:156
  723.7 34.0 %collective-permute-start.104 = (bf16[2,64,1152]{2,1,0:T(8,128)(2,1)}, bf16[2,64,1152]{2,1,0:T(8,128)(2,1)}, u32[]{:S(2)}, u32[]{:S(2)}) collective-permute-start(bf16[2,64,1152]{2,1,0:T(8,128)(2,1)} %fusion.54), channel_id=1, source_target_pairs={{0,1},{1,0},{2,3},{3,2},{4,5},{5,4},{6,7},{7,6},{8,9},{9,8},{10,11... | collective-permute-start | bytes 884744 | tf_op jit(solution)/shard_map/ppermute | solution.py:68
  792.7 39.6 %collective-permute-start.123 = (bf16[4,144,1152]{2,1,0:T(8,128)(2,1)}, bf16[4,144,1152]{2,1,0:T(8,128)(2,1)}, u32[]{:S(2)}, u32[]{:S(2)}) collective-permute-start(bf16[4,144,1152]{2,1,0:T(8,128)(2,1)} %fusion.11), channel_id=1, source_target_pairs={{0,4},{4,0},{8,12},{12,8},{16,20},{20,16},{24,28},{28,24},{1,5},{5... | collective-permute-start | bytes 3981320 | tf_op jit(solution)/shard_map/ppermute | solution.py:182
  805.8 100.6 %collective-permute-start.139 = (f32[32,144]{1,0:T(8,128)S(1)}, f32[32,144]{1,0:T(8,128)S(1)}, u32[]{:S(2)}, u32[]{:S(2)}) collective-permute-start(f32[32,144]{1,0:T(8,128)S(1)} %add.751), channel_id=1, source_target_pairs={{0,2},{1,3},{2,0},{3,1},{4,6},{5,7},{6,4},{7,5},{8,10},{9,11},{10,... | collective-permute-start | bytes 55304 | tf_op jit(solution)/shard_map/ppermute | solution.py:68
  809.8 26.1 %collective-permute-start.128 = (bf16[144,1536]{1,0:T(8,128)(2,1)S(1)}, bf16[144,1536]{1,0:T(8,128)(2,1)S(1)}, u32[]{:S(2)}, u32[]{:S(2)}) collective-permute-start(bf16[144,1536]{1,0:T(8,128)(2,1)S(1)} %get-tuple-element.290), channel_id=1, source_target_pairs={{0,8},{4,12},{8,16},{12,20},{16,24},{20,28},{24,0},{28,4},{1,9},{5... | collective-permute-start | bytes 1327112 | tf_op jit(solution)/shard_map/ppermute | solution.py:156
  812.3 35.8 %collective-permute-start.129 = (bf16[144,1536]{1,0:T(8,128)(2,1)S(1)}, bf16[144,1536]{1,0:T(8,128)(2,1)S(1)}, u32[]{:S(2)}, u32[]{:S(2)}) collective-permute-start(bf16[144,1536]{1,0:T(8,128)(2,1)S(1)} %get-tuple-element.292), channel_id=1, source_target_pairs={{0,24},{4,28},{8,0},{12,4},{16,8},{20,12},{24,16},{28,20},{1,25},{... | collective-permute-start | bytes 1327112 | tf_op jit(solution)/shard_map/ppermute | solution.py:156
  813.9 68.1 %collective-permute-start.130 = (bf16[144,1536]{1,0:T(8,128)(2,1)S(1)}, bf16[144,1536]{1,0:T(8,128)(2,1)S(1)}, u32[]{:S(2)}, u32[]{:S(2)}) collective-permute-start(bf16[144,1536]{1,0:T(8,128)(2,1)S(1)} %get-tuple-element.291), channel_id=1, source_target_pairs={{0,16},{4,20},{8,24},{12,28},{16,0},{20,4},{24,8},{28,12},{1,17},{... | collective-permute-start | bytes 1327112 | tf_op jit(solution)/shard_map/ppermute | solution.py:156
  834.2 48.1 %collective-permute-start.124 = (bf16[144,1152]{1,0:T(8,128)(2,1)S(1)}, bf16[144,1152]{1,0:T(8,128)(2,1)S(1)}, u32[]{:S(2)}, u32[]{:S(2)}) collective-permute-start(bf16[144,1152]{1,0:T(8,128)(2,1)S(1)} %get-tuple-element.296), channel_id=1, source_target_pairs={{0,8},{4,12},{8,16},{12,20},{16,24},{20,28},{24,0},{28,4},{1,9},{5... | collective-permute-start | bytes 995336 | tf_op jit(solution)/shard_map/ppermute | solution.py:156
  835.9 46.4 %collective-permute-start.125 = (bf16[144,1152]{1,0:T(8,128)(2,1)S(1)}, bf16[144,1152]{1,0:T(8,128)(2,1)S(1)}, u32[]{:S(2)}, u32[]{:S(2)}) collective-permute-start(bf16[144,1152]{1,0:T(8,128)(2,1)S(1)} %get-tuple-element.298), channel_id=1, source_target_pairs={{0,24},{4,28},{8,0},{12,4},{16,8},{20,12},{24,16},{28,20},{1,25},{... | collective-permute-start | bytes 995336 | tf_op jit(solution)/shard_map/ppermute | solution.py:156
  848.1 48.1 %collective-permute-start.126 = (bf16[144,1152]{1,0:T(8,128)(2,1)S(1)}, bf16[144,1152]{1,0:T(8,128)(2,1)S(1)}, u32[]{:S(2)}, u32[]{:S(2)}) collective-permute-start(bf16[144,1152]{1,0:T(8,128)(2,1)S(1)} %get-tuple-element.297), channel_id=1, source_target_pairs={{0,16},{4,20},{8,24},{12,28},{16,0},{20,4},{24,8},{28,12},{1,17},{... | collective-permute-start | bytes 995336 | tf_op jit(solution)/shard_map/ppermute | solution.py:156
  (338 other events, 2889.7 us)
Sparse Core Ops, SparseCore 0:
  193.8 112.3 all-gather.4
  308.4 92.4 all-gather.6
  504.4 110.4 reduce-scatter.4
  670.5 177.8 reduce-scatter.2
